TPU v7x, 32 devices: a whole 2x2x4 slice. The times are simulated.
32 devices in a mesh: dp: 8 (over z, y), seq: 4 (over x, core).
Axes of the slice: x: 2, y: 2, z: 4, core: 2. Of those that a mesh axis runs over, the one named last changes fastest.
Arguments:
- hidden_in: bfloat16 [6144, 2048], P(('dp', 'seq')), may hold values from -6 to 6
- valid_len: int32 [8], replicated, may hold values from 481 to 640, as said below
- doc_lengths: int32 [4, 8, 8], replicated, may hold values from 1 to 4, as said below
- doc_perm: int32 [4, 64], replicated, may hold values from 0 to 63, as said below
- attn_norm: bfloat16 [2048], P('dp'), may hold values from 0.5 to 1.5
- w_query: bfloat16 [2048, 2048], P('dp', 'seq'), may hold values from -0.125 to 0.125
- key_weight: bfloat16 [2048, 1024], P('dp', 'seq'), may hold values from -0.125 to 0.125
- value_weight: bfloat16 [2048, 1024], P('dp', 'seq'), may hold values from -0.125 to 0.125
- w_out: bfloat16 [2048, 2048], P('seq', 'dp'), may hold values from -0.5 to 0.5
- query_norm: bfloat16 [128], P('dp'), may hold values from 0.5 to 1.5
- key_norm_gain: bfloat16 [128], P('dp'), may hold values from 0.5 to 1.5
- mlp_norm: bfloat16 [2048], P('dp'), may hold values from 0.5 to 1.5
- w_gate: bfloat16 [2048, 6144], P('dp', 'seq'), may hold values from -0.125 to 0.125
- w_up: bfloat16 [2048, 6144], P('dp', 'seq'), may hold values from -0.125 to 0.125
- w_down: bfloat16 [6144, 2048], P('seq', 'dp'), may hold values from -0.078125 to 0.078125
- out_grad: bfloat16 [6144, 2048], P(('dp', 'seq')), may hold values from -6 to 6
Outputs:
- mixed: bfloat16 [6144, 2048], P(('dp', 'seq'))
- grad_hidden: bfloat16 [6144, 2048], P(('dp', 'seq'))
- grad_attn_norm: float32 [2048], P(('dp', 'seq'))
- grad_query: float32 [2048, 2048], P('dp', 'seq')
- grad_key: float32 [2048, 1024], P('dp', 'seq')
- grad_value: float32 [2048, 1024], P('dp', 'seq')
- grad_out: float32 [2048, 2048], P('seq', 'dp')
- grad_query_norm: float32 [128], P(('dp', 'seq'))
- grad_key_norm: float32 [128], P(('dp', 'seq'))
- grad_mlp_norm: float32 [2048], P(('dp', 'seq'))
- grad_gate: float32 [2048, 6144], P('dp', 'seq')
- grad_up: float32 [2048, 6144], P('dp', 'seq')
- grad_down: float32 [6144, 2048], P('seq', 'dp')
Inputs may be any that keep to these rules, and one draw needn't show every extreme that they name: `valid_len`: one row's long document fills all its reserved slots and one row has the least length, in every draw. `doc_lengths`: both ends are reached in every part. `doc_perm`: for each index of seq a permutation of the 64 short documents; the short documents of one row go to distinct rows, and every row receives exactly 8 of them, from distinct rows.
All inputs are finite; a program needn't handle non-finite values.
Results may differ from a plain program's by a relative error of at most 0.035.
Values may be sent and summed in bfloat16 or wider, within the bound.
A program may use at most 448 MiB of HBM per device.

v0:
```python
import math

import jax
import jax.numpy as jnp
from jax import lax
from jax.sharding import PartitionSpec as P

MAXSHORT = 4


NORM_EPS = 1e-06
ROPE_BASE = 1000000.0
MASKED = -1e30
CONTRACT_ROWS = (((0,), (0,)), ((), ()))
CONTRACT_COLS = (((1,), (1,)), ((), ()))


def root_mean_norm(values, gain):
    return values * lax.rsqrt(jnp.mean(values * values, axis=-1, keepdims=True) + NORM_EPS) * gain


def apply_rotary(values, position):
    half_width = values.shape[-1] // 2
    freq_index = jnp.arange(half_width, dtype=jnp.float32)
    inverse = jnp.exp(freq_index * (-2.0 * math.log(ROPE_BASE) / values.shape[-1]))
    angles = position.astype(jnp.float32)[:, None] * inverse[None, :]
    cosine = jnp.cos(angles)[:, None, :]
    sine_part = jnp.sin(angles)[:, None, :]
    first = values[..., :half_width]
    second = values[..., half_width:]
    return jnp.concatenate(
        [first * cosine - second * sine_part, second * cosine + first * sine_part], axis=-1
    )


def head_prep(flat, gain, position):
    return apply_rotary(
        root_mean_norm(flat.reshape(flat.shape[0], -1, gain.shape[0]), gain), position
    )


def product(left, right, dims):
    return lax.dot_general(left, right, dims, preferred_element_type=jnp.float32)


def layout(lengths_part, perm_part, body_len):
    row_count, shorts = lengths_part.shape
    doc_total = row_count * shorts
    starts = body_len + jnp.cumsum(lengths_part, axis=1) - lengths_part
    kept_flat = lengths_part.reshape(doc_total)
    matched = perm_part[:, None] == jnp.arange(doc_total, dtype=jnp.int32)[None, :]
    placed = jnp.sum(jnp.where(matched, kept_flat[:, None], 0), axis=0).reshape(row_count, shorts)
    new_at = body_len + jnp.cumsum(placed, axis=1) - placed
    new_start = jnp.sum(jnp.where(matched, new_at.reshape(doc_total)[None, :], 0), axis=1)
    return (starts.reshape(doc_total), kept_flat, new_start, perm_part // shorts)


def slot_labels(
    kept_flat,
    new_start,
    dest_row,
    part,
    my_row,
    valid_here,
    body_len,
    shard_len,
    row_len,
    row_count,
):
    doc_total = kept_flat.shape[0]
    local = jnp.arange(shard_len, dtype=jnp.int32)
    doc_ids = jnp.arange(doc_total, dtype=jnp.int32)
    inside = (
        (dest_row == my_row)[None, :]
        & (local[:, None] >= new_start[None, :])
        & (local[:, None] < (new_start + kept_flat)[None, :])
    )
    offset = local[:, None] - new_start[None, :]
    in_short = jnp.any(inside, axis=1)
    short_seg = jnp.sum(
        jnp.where(inside, row_count + part * doc_total + doc_ids[None, :], 0), axis=1
    )
    short_pos = jnp.sum(jnp.where(inside, offset, 0), axis=1)
    long_pos = part * body_len + local
    in_long = (local < body_len) & (long_pos < valid_here)
    flat_slot = my_row * row_len + part * shard_len + local
    segment = jnp.where(in_long, my_row, jnp.where(in_short, short_seg, -1 - flat_slot))
    position = jnp.where(in_long, long_pos, short_pos)
    return (segment, position, in_long, in_short)


def attend_scores(query_rows, keys_all, seg_query, pos_query, seg_key, pos_key):
    grouped_heads = query_rows.reshape(
        query_rows.shape[0], keys_all.shape[1], -1, query_rows.shape[-1]
    )
    raw = jnp.einsum(
        "tngd,und->ngtu", grouped_heads, keys_all, preferred_element_type=jnp.float32
    ) * query_rows.shape[-1] ** (-0.5)
    allowed = (seg_query[:, None] == seg_key[None, :]) & (pos_key[None, :] <= pos_query[:, None])
    return (jnp.where(allowed, raw, MASKED), grouped_heads)


def attend_forward(query_rows, keys_all, values_all, seg_query, pos_query, seg_key, pos_key):
    masked, grouped_heads = attend_scores(
        query_rows, keys_all, seg_query, pos_query, seg_key, pos_key
    )
    peak = jnp.max(masked, axis=-1, keepdims=True)
    expd = jnp.exp(masked - peak)
    total_weight = jnp.sum(expd, axis=-1, keepdims=True)
    probs = (expd / total_weight).astype(jnp.bfloat16)
    log_total = peak + jnp.log(total_weight)
    context = jnp.einsum(
        "ngtu,und->tngd", probs, values_all, preferred_element_type=jnp.float32
    ).reshape(query_rows.shape[0], -1)
    return (context.astype(jnp.bfloat16), log_total)


def attend_backward(
    query_rows, keys_all, values_all, grad_att, log_total, seg_query, pos_query, seg_key, pos_key
):
    masked, grouped_heads = attend_scores(
        query_rows, keys_all, seg_query, pos_query, seg_key, pos_key
    )
    probs_full = jnp.exp(masked - log_total)
    probs_low = probs_full.astype(jnp.bfloat16)
    grad_group = grad_att.reshape(grouped_heads.shape)
    grad_probs = jnp.einsum(
        "tngd,und->ngtu", grad_group, values_all, preferred_element_type=jnp.float32
    )
    grad_values = jnp.einsum(
        "ngtu,tngd->und", probs_low, grad_group, preferred_element_type=jnp.float32
    )
    spread_sum = jnp.sum(probs_full * grad_probs, axis=-1, keepdims=True)
    grad_scores = (probs_full * (grad_probs - spread_sum)).astype(jnp.bfloat16)
    scale_factor = query_rows.shape[-1] ** (-0.5)
    grad_queries = (
        jnp.einsum(
            "ngtu,und->tngd", grad_scores, keys_all, preferred_element_type=jnp.float32
        ).reshape(query_rows.shape)
        * scale_factor
    )
    grad_keys = (
        jnp.einsum("ngtu,tngd->und", grad_scores, grouped_heads, preferred_element_type=jnp.float32)
        * scale_factor
    )
    return (grad_queries, grad_keys, grad_values)


def feed_forward(resid, gain_mlp, gate_mat, up_mat):
    normed_mlp = root_mean_norm(resid, gain_mlp).astype(jnp.bfloat16)
    gate = jnp.dot(normed_mlp, gate_mat, preferred_element_type=jnp.float32)
    upper = jnp.dot(normed_mlp, up_mat, preferred_element_type=jnp.float32)
    hidden = (jax.nn.silu(gate) * upper).astype(jnp.bfloat16)
    return (normed_mlp, gate, upper, hidden)


def feed_back(grad_y_low, gate, upper, gate_mat, up_mat, down_mat):
    grad_mid = product(grad_y_low, down_mat, CONTRACT_COLS)
    silu_pull = jax.vjp(lambda gate_in, up_in: jax.nn.silu(gate_in) * up_in, gate, upper)[1]
    grad_gate_lin, grad_up_lin = silu_pull(grad_mid)
    grad_gate_low = grad_gate_lin.astype(jnp.bfloat16)
    grad_up_low = grad_up_lin.astype(jnp.bfloat16)
    grad_nmlp = product(grad_gate_low, gate_mat, CONTRACT_COLS) + product(
        grad_up_low, up_mat, CONTRACT_COLS
    )
    return (grad_gate_low, grad_up_low, grad_nmlp)


def per_device(
    hidden_in,
    valid_len,
    doc_lengths,
    doc_perm,
    attn_norm,
    w_query,
    key_weight,
    value_weight,
    w_out,
    query_norm,
    key_norm_gain,
    mlp_norm,
    w_gate,
    w_up,
    w_down,
    out_grad,
):
    shard_len = hidden_in.shape[0]
    model_width = hidden_in.shape[1]
    seq_count = doc_lengths.shape[0]
    row_count = doc_lengths.shape[1]
    shorts = doc_lengths.shape[2]
    row_len = shard_len * seq_count
    cap_len = MAXSHORT
    body_len = shard_len - shorts * cap_len
    my_row = lax.axis_index("dp")
    my_part = lax.axis_index("seq")
    valid_here = valid_len[my_row]
    all_starts, all_kept, all_new, all_dest = jax.vmap(
        lambda lengths_part, perm_part: layout(lengths_part, perm_part, body_len)
    )(doc_lengths, doc_perm)
    part_ids = jnp.arange(seq_count, dtype=jnp.int32)
    seg_parts, pos_parts, long_parts, short_parts = jax.vmap(
        lambda kept_p, new_p, dest_p, part: slot_labels(
            kept_p, new_p, dest_p, part, my_row, valid_here, body_len, shard_len, row_len, row_count
        )
    )(all_kept, all_new, all_dest, part_ids)
    segment = seg_parts.reshape(row_len)
    position = pos_parts.reshape(row_len)
    seg_local = lax.dynamic_index_in_dim(seg_parts, my_part, 0, keepdims=False)
    pos_local = lax.dynamic_index_in_dim(pos_parts, my_part, 0, keepdims=False)
    keep_long = lax.dynamic_index_in_dim(long_parts, my_part, 0, keepdims=False)
    live_local = keep_long | lax.dynamic_index_in_dim(short_parts, my_part, 0, keepdims=False)
    starts = lax.dynamic_index_in_dim(all_starts, my_part, 0, keepdims=False)
    kept_flat = lax.dynamic_index_in_dim(all_kept, my_part, 0, keepdims=False)
    new_start = lax.dynamic_index_in_dim(all_new, my_part, 0, keepdims=False)
    dest_row = lax.dynamic_index_in_dim(all_dest, my_part, 0, keepdims=False)
    row_ids = jnp.arange(row_count, dtype=jnp.int32)
    local_slots = jnp.arange(shard_len, dtype=jnp.int32)
    cap_ids = jnp.arange(cap_len, dtype=jnp.int32)
    my_dest = lax.dynamic_slice_in_dim(dest_row, my_row * shorts, shorts)
    my_starts = lax.dynamic_slice_in_dim(starts, my_row * shorts, shorts)
    my_kept = lax.dynamic_slice_in_dim(kept_flat, my_row * shorts, shorts)
    going = my_dest[None, :] == row_ids[:, None]
    send_start = jnp.sum(jnp.where(going, my_starts[None, :], 0), axis=1)
    send_len = jnp.sum(jnp.where(going, my_kept[None, :], 0), axis=1)
    send_map = (
        (
            (cap_ids[None, :, None] < send_len[:, None, None])
            & (local_slots[None, None, :] == send_start[:, None, None] + cap_ids[None, :, None])
        )
        .reshape(row_count * cap_len, shard_len)
        .astype(jnp.bfloat16)
    )
    coming = (dest_row == my_row).reshape(row_count, shorts)
    recv_start = jnp.sum(jnp.where(coming, new_start.reshape(row_count, shorts), 0), axis=1)
    recv_len = jnp.sum(jnp.where(coming, kept_flat.reshape(row_count, shorts), 0), axis=1)
    recv_map = (
        (
            (cap_ids[None, None, :] < recv_len[None, :, None])
            & (local_slots[:, None, None] == recv_start[None, :, None] + cap_ids[None, None, :])
        )
        .reshape(shard_len, row_count * cap_len)
        .astype(jnp.bfloat16)
    )
    outgoing = (
        jnp.dot(send_map, hidden_in, preferred_element_type=jnp.float32)
        .astype(jnp.bfloat16)
        .reshape(row_count, cap_len, model_width)
    )
    incoming = lax.all_to_all(outgoing, "dp", split_axis=0, concat_axis=0, tiled=True)
    moved = jnp.where(keep_long[:, None], hidden_in.astype(jnp.float32), 0.0) + jnp.dot(
        recv_map,
        incoming.reshape(row_count * cap_len, model_width),
        preferred_element_type=jnp.float32,
    )
    gathered = (
        lax.all_gather(w_query, "dp", axis=0, tiled=True),
        lax.all_gather(key_weight, "dp", axis=0, tiled=True),
        lax.all_gather(value_weight, "dp", axis=0, tiled=True),
        lax.all_gather(w_out, "dp", axis=1, tiled=True),
        lax.all_gather(w_gate, "dp", axis=0, tiled=True),
        lax.all_gather(w_up, "dp", axis=0, tiled=True),
        lax.all_gather(w_down, "dp", axis=1, tiled=True),
        lax.all_gather(attn_norm, "dp", axis=0, tiled=True),
        lax.all_gather(query_norm, "dp", axis=0, tiled=True),
        lax.all_gather(key_norm_gain, "dp", axis=0, tiled=True),
        lax.all_gather(mlp_norm, "dp", axis=0, tiled=True),
    )
    gain_attn = gathered[7].astype(jnp.float32)
    gain_query = gathered[8].astype(jnp.float32)
    gain_key = gathered[9].astype(jnp.float32)
    gain_mlp = gathered[10].astype(jnp.float32)
    live_scale = live_local.astype(jnp.float32)[:, None]
    grad_y = out_grad.astype(jnp.float32) * live_scale
    grad_y_low = grad_y.astype(jnp.bfloat16)
    matrices = (
        lax.all_gather(gathered[0], "seq", axis=1, tiled=True),
        lax.all_gather(gathered[1], "seq", axis=1, tiled=True),
        lax.all_gather(gathered[2], "seq", axis=1, tiled=True),
        lax.all_gather(gathered[3], "seq", axis=0, tiled=True),
        lax.all_gather(gathered[4], "seq", axis=1, tiled=True),
        lax.all_gather(gathered[5], "seq", axis=1, tiled=True),
        lax.all_gather(gathered[6], "seq", axis=0, tiled=True),
    )
    query_mat, key_mat, value_mat, out_mat, gate_mat, up_mat, down_mat = matrices
    row_total_count = moved.shape[0]
    normed = root_mean_norm(moved, gain_attn).astype(jnp.bfloat16)
    query_lin = jnp.dot(normed, query_mat, preferred_element_type=jnp.float32)
    key_linear = jnp.dot(normed, key_mat, preferred_element_type=jnp.float32)
    value_linear = jnp.dot(normed, value_mat, preferred_element_type=jnp.float32)
    query_rows = head_prep(query_lin, gain_query, pos_local).astype(jnp.bfloat16)
    rotated_keys = head_prep(key_linear, gain_key, pos_local).astype(jnp.bfloat16)
    value_heads = value_linear.astype(jnp.bfloat16).reshape(row_total_count, -1, gain_key.shape[0])
    keys_all, values_all = (
        lax.all_gather(rotated_keys, "seq", axis=0, tiled=True),
        lax.all_gather(value_heads, "seq", axis=0, tiled=True),
    )
    attended, log_total = attend_forward(
        query_rows, keys_all, values_all, seg_local, pos_local, segment, position
    )
    projected = jnp.dot(attended, out_mat, preferred_element_type=jnp.float32)
    resid_rows = moved + projected
    normed_mlp, gate, upper, hidden = feed_forward(resid_rows, gain_mlp, gate_mat, up_mat)
    down_part = jnp.dot(hidden, down_mat, preferred_element_type=jnp.float32)
    output = resid_rows + down_part
    mixed = (output * live_scale).astype(jnp.bfloat16)
    grad_down = product(hidden, grad_y_low, CONTRACT_ROWS)
    grad_gate_low, grad_up_low, grad_nmlp = feed_back(
        grad_y_low, gate, upper, gate_mat, up_mat, down_mat
    )
    mlp_pull = jax.vjp(root_mean_norm, resid_rows, gain_mlp)[1]
    grad_resid_part, grad_gain_mlp = mlp_pull(grad_nmlp)
    grad_resid = grad_y_low.astype(jnp.float32) + grad_resid_part
    mlp_totals = (
        lax.psum_scatter(
            product(normed_mlp, grad_gate_low, CONTRACT_ROWS).astype(jnp.bfloat16),
            "dp",
            scatter_dimension=0,
            tiled=True,
        ).astype(jnp.float32),
        lax.psum_scatter(
            product(normed_mlp, grad_up_low, CONTRACT_ROWS).astype(jnp.bfloat16),
            "dp",
            scatter_dimension=0,
            tiled=True,
        ).astype(jnp.float32),
        lax.psum_scatter(
            grad_down.astype(jnp.bfloat16), "dp", scatter_dimension=1, tiled=True
        ).astype(jnp.float32),
        lax.psum_scatter(
            grad_gain_mlp.astype(jnp.bfloat16), "dp", scatter_dimension=0, tiled=True
        ).astype(jnp.float32),
    )
    mlp_totals = (
        lax.psum_scatter(
            mlp_totals[0].astype(jnp.bfloat16), "seq", scatter_dimension=1, tiled=True
        ).astype(jnp.float32),
        lax.psum_scatter(
            mlp_totals[1].astype(jnp.bfloat16), "seq", scatter_dimension=1, tiled=True
        ).astype(jnp.float32),
        lax.psum_scatter(
            mlp_totals[2].astype(jnp.bfloat16), "seq", scatter_dimension=0, tiled=True
        ).astype(jnp.float32),
        lax.psum_scatter(
            mlp_totals[3].astype(jnp.bfloat16), "seq", scatter_dimension=0, tiled=True
        ).astype(jnp.float32),
    )
    grad_proj = grad_resid.astype(jnp.bfloat16)
    grad_w_out = product(attended, grad_proj, CONTRACT_ROWS)
    grad_att = product(grad_proj, out_mat, CONTRACT_COLS).astype(jnp.bfloat16)
    grad_queries, grad_keys_all, grad_values_all = attend_backward(
        query_rows,
        keys_all,
        values_all,
        grad_att,
        log_total,
        seg_local,
        pos_local,
        segment,
        position,
    )
    grad_keys_own, grad_values_own = (
        lax.psum_scatter(
            grad_keys_all.astype(jnp.bfloat16), "seq", scatter_dimension=0, tiled=True
        ).astype(jnp.float32),
        lax.psum_scatter(
            grad_values_all.astype(jnp.bfloat16), "seq", scatter_dimension=0, tiled=True
        ).astype(jnp.float32),
    )
    query_pull = jax.vjp(
        lambda flat, gain_in: head_prep(flat, gain_in, pos_local), query_lin, gain_query
    )[1]
    grad_query_lin, grad_gain_query = query_pull(grad_queries)
    key_pull = jax.vjp(
        lambda flat, gain_in: head_prep(flat, gain_in, pos_local), key_linear, gain_key
    )[1]
    grad_key_lin, grad_gain_key = key_pull(grad_keys_own)
    grad_query_low = grad_query_lin.astype(jnp.bfloat16)
    grad_key_low = grad_key_lin.astype(jnp.bfloat16)
    grad_value_low = grad_values_own.reshape(row_total_count, -1).astype(jnp.bfloat16)
    grad_normed = (
        product(grad_query_low, query_mat, CONTRACT_COLS)
        + product(grad_key_low, key_mat, CONTRACT_COLS)
        + product(grad_value_low, value_mat, CONTRACT_COLS)
    )
    attn_pull = jax.vjp(root_mean_norm, moved, gain_attn)[1]
    grad_moved_part, grad_gain_attn = attn_pull(grad_normed)
    grad_moved_rows = grad_resid + grad_moved_part
    attn_totals = (
        lax.psum_scatter(
            product(normed, grad_query_low, CONTRACT_ROWS).astype(jnp.bfloat16),
            "dp",
            scatter_dimension=0,
            tiled=True,
        ).astype(jnp.float32),
        lax.psum_scatter(
            product(normed, grad_key_low, CONTRACT_ROWS).astype(jnp.bfloat16),
            "dp",
            scatter_dimension=0,
            tiled=True,
        ).astype(jnp.float32),
        lax.psum_scatter(
            product(normed, grad_value_low, CONTRACT_ROWS).astype(jnp.bfloat16),
            "dp",
            scatter_dimension=0,
            tiled=True,
        ).astype(jnp.float32),
        lax.psum_scatter(
            grad_w_out.astype(jnp.bfloat16), "dp", scatter_dimension=1, tiled=True
        ).astype(jnp.float32),
        lax.psum_scatter(
            grad_gain_attn.astype(jnp.bfloat16), "dp", scatter_dimension=0, tiled=True
        ).astype(jnp.float32),
        lax.psum_scatter(
            grad_gain_query.astype(jnp.bfloat16), "dp", scatter_dimension=0, tiled=True
        ).astype(jnp.float32),
        lax.psum_scatter(
            grad_gain_key.astype(jnp.bfloat16), "dp", scatter_dimension=0, tiled=True
        ).astype(jnp.float32),
    )
    attn_totals = (
        lax.psum_scatter(
            attn_totals[0].astype(jnp.bfloat16), "seq", scatter_dimension=1, tiled=True
        ).astype(jnp.float32),
        lax.psum_scatter(
            attn_totals[1].astype(jnp.bfloat16), "seq", scatter_dimension=1, tiled=True
        ).astype(jnp.float32),
        lax.psum_scatter(
            attn_totals[2].astype(jnp.bfloat16), "seq", scatter_dimension=1, tiled=True
        ).astype(jnp.float32),
        lax.psum_scatter(
            attn_totals[3].astype(jnp.bfloat16), "seq", scatter_dimension=0, tiled=True
        ).astype(jnp.float32),
        lax.psum_scatter(
            attn_totals[4].astype(jnp.bfloat16), "seq", scatter_dimension=0, tiled=True
        ).astype(jnp.float32),
        lax.psum_scatter(
            attn_totals[5].astype(jnp.bfloat16), "seq", scatter_dimension=0, tiled=True
        ).astype(jnp.float32),
        lax.psum_scatter(
            attn_totals[6].astype(jnp.bfloat16), "seq", scatter_dimension=0, tiled=True
        ).astype(jnp.float32),
    )
    grad_moved = grad_moved_rows.astype(jnp.bfloat16)
    back_out = (
        product(recv_map, grad_moved, CONTRACT_ROWS)
        .astype(jnp.bfloat16)
        .reshape(row_count, cap_len, model_width)
    )
    returned = lax.all_to_all(back_out, "dp", split_axis=0, concat_axis=0, tiled=True)
    grad_hidden = (
        jnp.where(keep_long[:, None], grad_moved.astype(jnp.float32), 0.0)
        + product(send_map, returned.reshape(row_count * cap_len, model_width), CONTRACT_ROWS)
    ).astype(jnp.bfloat16)
    return (
        mixed,
        grad_hidden,
        attn_totals[4],
        attn_totals[0],
        attn_totals[1],
        attn_totals[2],
        attn_totals[3],
        attn_totals[5],
        attn_totals[6],
        mlp_totals[3],
        mlp_totals[0],
        mlp_totals[1],
        mlp_totals[2],
    )


def solution(mesh):
    in_specs = (
        P(("dp", "seq"), None),
        P(),
        P(),
        P(),
        P("dp"),
        P("dp", "seq"),
        P("dp", "seq"),
        P("dp", "seq"),
        P("seq", "dp"),
        P("dp"),
        P("dp"),
        P("dp"),
        P("dp", "seq"),
        P("dp", "seq"),
        P("seq", "dp"),
        P(("dp", "seq"), None),
    )
    out_specs = (
        P(("dp", "seq"), None),
        P(("dp", "seq"), None),
        P(("dp", "seq")),
        P("dp", "seq"),
        P("dp", "seq"),
        P("dp", "seq"),
        P("seq", "dp"),
        P(("dp", "seq")),
        P(("dp", "seq")),
        P(("dp", "seq")),
        P("dp", "seq"),
        P("dp", "seq"),
        P("seq", "dp"),
    )
    return jax.shard_map(
        per_device, mesh=mesh, in_specs=in_specs, out_specs=out_specs, check_vma=False
    )
```

profile of v0, /device:TPU:0, one launch (start us, length us, event | category | flops | bytes accessed | tf_op | source)
XLA Modules:
  0.0 3273.3 jit_solution(7495099887518992108)
XLA Ops:
  9.4 43.6 %all-gather.25.cloned.1.call-done = bf16[2048,256]{1,0:T(8,128)(2,1)} async-done(((bf16[256,256]{1,0:T(8,128)(2,1)}), bf16[2048,256]{1,0:T(8,128)(2,1)}) %all-gather.25.cloned.1.call-update) | async-done | bytes 1048592 | tf_op jit(solution)/shard_map/all_gather | solution.py:258
  53.1 41.0 %all-gather.19.cloned.1.call-done = bf16[2048,256]{1,0:T(8,128)(2,1)} async-done(((bf16[256,256]{1,0:T(8,128)(2,1)}), bf16[2048,256]{1,0:T(8,128)(2,1)}) %all-gather.19.cloned.1.call-update) | async-done | bytes 1048592 | tf_op jit(solution)/shard_map/all_gather | solution.py:259
  97.0 47.2 %all-gather.31.cloned.1.call-done = bf16[2048,512]{1,0:T(8,128)(2,1)} async-done(((bf16[256,512]{1,0:T(8,128)(2,1)}), bf16[2048,512]{1,0:T(8,128)(2,1)}) %all-gather.31.cloned.1.call-update) | async-done | bytes 2097168 | tf_op jit(solution)/shard_map/all_gather | solution.py:257
  155.1 21.7 all-reduce.15
  219.8 48.9 %all-gather.35.cloned.1.call-done = bf16[512,2048]{1,0:T(8,128)(2,1)} async-done(((bf16[512,256]{1,0:T(8,128)(2,1)}), bf16[512,2048]{1,0:T(8,128)(2,1)}) %all-gather.35.cloned.1.call-update) | async-done | bytes 2097168 | tf_op jit(solution)/shard_map/all_gather | solution.py:260
  268.8 99.4 %all-gather.43.cloned.1.call-done = bf16[2048,1536]{1,0:T(8,128)(2,1)} async-done(((bf16[256,1536]{1,0:T(8,128)(2,1)}), bf16[2048,1536]{1,0:T(8,128)(2,1)}) %all-gather.43.cloned.1.call-update) | async-done | bytes 6291472 | tf_op jit(solution)/shard_map/all_gather | solution.py:262
  368.3 99.4 %all-gather.39.cloned.1.call-done = bf16[2048,1536]{1,0:T(8,128)(2,1)} async-done(((bf16[256,1536]{1,0:T(8,128)(2,1)}), bf16[2048,1536]{1,0:T(8,128)(2,1)}) %all-gather.39.cloned.1.call-update) | async-done | bytes 6291472 | tf_op jit(solution)/shard_map/all_gather | solution.py:261
  467.7 100.1 %all-gather.47.cloned.1.call-done = bf16[1536,2048]{1,0:T(8,128)(2,1)} async-done(((bf16[1536,256]{1,0:T(8,128)(2,1)}), bf16[1536,2048]{1,0:T(8,128)(2,1)}) %all-gather.47.cloned.1.call-update) | async-done | bytes 6291472 | tf_op jit(solution)/shard_map/all_gather | solution.py:263
  587.6 38.1 %all-gather.33.cloned.1.call-done = bf16[2048,2048]{1,0:T(8,128)(2,1)} async-done(((bf16[2048,512]{1,0:T(8,128)(2,1)}), bf16[2048,2048]{1,0:T(8,128)(2,1)}) %all-gather.33.cloned.1.call-update) | async-done | bytes 8388624 | tf_op jit(solution)/shard_map/all_gather | solution.py:277
  679.9 49.3 %all-gather.37.cloned.1.call-done = bf16[2048,2048]{1,0:T(8,128)(2,1)} async-done(((bf16[512,2048]{1,0:T(8,128)(2,1)}), bf16[2048,2048]{1,0:T(8,128)(2,1)}) %all-gather.37.cloned.1.call-update) | async-done | bytes 8388624 | tf_op jit(solution)/shard_map/all_gather | solution.py:280
  736.1 149.3 %all-gather.45.cloned.1.call-done = bf16[2048,6144]{1,0:T(8,128)(2,1)} async-done(((bf16[2048,1536]{1,0:T(8,128)(2,1)}), bf16[2048,6144]{1,0:T(8,128)(2,1)}) %all-gather.45.cloned.1.call-update) | async-done | bytes 25165840 | tf_op jit(solution)/shard_map/all_gather | solution.py:282
  899.7 141.9 %all-gather.41.cloned.1.call-done = bf16[2048,6144]{1,0:T(8,128)(2,1)} async-done(((bf16[2048,1536]{1,0:T(8,128)(2,1)}), bf16[2048,6144]{1,0:T(8,128)(2,1)}) %all-gather.41.cloned.1.call-update) | async-done | bytes 25165840 | tf_op jit(solution)/shard_map/all_gather | solution.py:281
  1055.9 142.0 %all-gather.49.cloned.1.call-done = bf16[6144,2048]{1,0:T(8,128)(2,1)} async-done(((bf16[1536,2048]{1,0:T(8,128)(2,1)}), bf16[6144,2048]{1,0:T(8,128)(2,1)}) %all-gather.49.cloned.1.call-update) | async-done | bytes 25165840 | tf_op jit(solution)/shard_map/all_gather | solution.py:283
  1304.7 26.4 reduce-scatter.17.cloned.1.call-done
  1422.8 91.5 %reduce-scatter.25.cloned.1.call-done = bf16[256,1024]{1,0:T(8,128)(2,1)} async-done(((bf16[2048,1024]{1,0:T(8,128)(2,1)}), bf16[256,1024]{1,0:T(8,128)(2,1)}) %reduce-scatter.25.cloned.1.call-update) | async-done | bytes 524304 | tf_op jit(solution)/shard_map/reduce_scatter | solution.py:396
  1514.4 152.8 %reduce-scatter.33.cloned.1.call-done = bf16[2048,256]{1,0:T(8,128)(2,1)} async-done(((bf16[2048,2048]{1,0:T(8,128)(2,1)}), bf16[2048,256]{1,0:T(8,128)(2,1)}) %reduce-scatter.33.cloned.1.call-update) | async-done | bytes 1048592 | tf_op jit(solution)/shard_map/reduce_scatter | solution.py:408
  1667.2 152.0 %reduce-scatter.21.cloned.1.call-done = bf16[256,2048]{1,0:T(8,128)(2,1)} async-done(((bf16[2048,2048]{1,0:T(8,128)(2,1)}), bf16[256,2048]{1,0:T(8,128)(2,1)}) %reduce-scatter.21.cloned.1.call-update) | async-done | bytes 1048592 | tf_op jit(solution)/shard_map/reduce_scatter | solution.py:390
  1819.3 407.4 %reduce-scatter.45.cloned.1.call-done = bf16[6144,256]{1,0:T(8,128)(2,1)} async-done(((bf16[6144,2048]{1,0:T(8,128)(2,1)}), bf16[6144,256]{1,0:T(8,128)(2,1)}) %reduce-scatter.45.cloned.1.call-update) | async-done | bytes 3145744 | tf_op jit(solution)/shard_map/reduce_scatter | solution.py:327
  2226.8 406.5 %reduce-scatter.41.cloned.1.call-done = bf16[256,6144]{1,0:T(8,128)(2,1)} async-done(((bf16[2048,6144]{1,0:T(8,128)(2,1)}), bf16[256,6144]{1,0:T(8,128)(2,1)}) %reduce-scatter.41.cloned.1.call-update) | async-done | bytes 3145744 | tf_op jit(solution)/shard_map/reduce_scatter | solution.py:321
  2633.7 406.2 %reduce-scatter.37.cloned.1.call-done = bf16[256,6144]{1,0:T(8,128)(2,1)} async-done(((bf16[2048,6144]{1,0:T(8,128)(2,1)}), bf16[256,6144]{1,0:T(8,128)(2,1)}) %reduce-scatter.37.cloned.1.call-update) | async-done | bytes 3145744 | tf_op jit(solution)/shard_map/reduce_scatter | solution.py:315
  3116.4 25.9 reduce-scatter.23.cloned.1.call-done
  3144.1 38.5 %reduce-scatter.47.cloned.1.call-done = bf16[1536,256]{1,0:T(8,128)(2,1)} async-done(((bf16[6144,256]{1,0:T(8,128)(2,1)}), bf16[1536,256]{1,0:T(8,128)(2,1)}) %reduce-scatter.47.cloned.1.call-update) | async-done | bytes 786448 | tf_op jit(solution)/shard_map/reduce_scatter | solution.py:341
  3185.0 38.3 %reduce-scatter.43.cloned.1.call-done = bf16[256,1536]{1,0:T(8,128)(2,1)} async-done(((bf16[256,6144]{1,0:T(8,128)(2,1)}), bf16[256,1536]{1,0:T(8,128)(2,1)}) %reduce-scatter.43.cloned.1.call-update) | async-done | bytes 786448 | tf_op jit(solution)/shard_map/reduce_scatter | solution.py:338
  3225.8 38.1 %reduce-scatter.39.cloned.1.call-done = bf16[256,1536]{1,0:T(8,128)(2,1)} async-done(((bf16[256,6144]{1,0:T(8,128)(2,1)}), bf16[256,1536]{1,0:T(8,128)(2,1)}) %reduce-scatter.39.cloned.1.call-update) | async-done | bytes 786448 | tf_op jit(solution)/shard_map/reduce_scatter | solution.py:335
  (402 shorter events, 448.7 us)
Async XLA Ops:
  94.7 273.5 %all-gather.43.cloned.1.call-start = ((), (), s32[]{:S(2)}) async-start(), calls=%async_computation.30 | async-start | bytes 7077888 | tf_op jit(solution)/shard_map/all_gather | solution.py:262
  95.5 372.2 %all-gather.39.cloned.1.call-start = ((), (), s32[]{:S(2)}) async-start(), calls=%async_computation.28 | async-start | bytes 7077888 | tf_op jit(solution)/shard_map/all_gather | solution.py:261
  96.2 471.6 %all-gather.47.cloned.1.call-start = ((), (), s32[]{:S(2)}) async-start(), calls=%async_computation.32 | async-start | bytes 7077888 | tf_op jit(solution)/shard_map/all_gather | solution.py:263
  97.0 528.7 %all-gather.33.cloned.1.call-start = ((), (), s32[]{:S(2)}) async-start(), calls=%async_computation.25 | async-start | bytes 10485760 | tf_op jit(solution)/shard_map/all_gather | solution.py:277
  153.3 494.3 %all-gather.29.cloned.1.call-start = ((), (), s32[]{:S(2)}) async-start(), calls=%async_computation.23 | async-start | bytes 1966080 | tf_op jit(solution)/shard_map/all_gather | solution.py:295
  203.3 465.9 %all-gather.23.cloned.1.call-start = ((), (), s32[]{:S(2)}) async-start(), calls=%async_computation.20 | async-start | bytes 1966080 | tf_op jit(solution)/shard_map/all_gather | solution.py:296
  219.8 509.4 %all-gather.37.cloned.1.call-start = ((), (), s32[]{:S(2)}) async-start(), calls=%async_computation.27 | async-start | bytes 10485760 | tf_op jit(solution)/shard_map/all_gather | solution.py:280
  268.8 616.6 %all-gather.45.cloned.1.call-start = ((), (), s32[]{:S(2)}) async-start(), calls=%async_computation.31 | async-start | bytes 31457280 | tf_op jit(solution)/shard_map/all_gather | solution.py:282
  368.2 673.4 %all-gather.41.cloned.1.call-start = ((), (), s32[]{:S(2)}) async-start(), calls=%async_computation.29 | async-start | bytes 31457280 | tf_op jit(solution)/shard_map/all_gather | solution.py:281
  467.6 730.3 %all-gather.49.cloned.1.call-start = ((), (), s32[]{:S(2)}) async-start(), calls=%async_computation.33 | async-start | bytes 31457280 | tf_op jit(solution)/shard_map/all_gather | solution.py:283
  567.8 732.5 %reduce-scatter.19.cloned.1.call-start = ((), (), s32[]{:S(2)}) async-start(), calls=%async_computation.35 | async-start | bytes 1966080 | tf_op jit(solution)/shard_map/reduce_scatter | solution.py:366
  1304.7 209.6 %reduce-scatter.25.cloned.1.call-start = ((), (), s32[]{:S(2)}) async-start(), calls=%async_computation.38 | async-start | bytes 4718592 | tf_op jit(solution)/shard_map/reduce_scatter | solution.py:396
  1337.6 329.5 %reduce-scatter.33.cloned.1.call-start = ((), (), s32[]{:S(2)}) async-start(), calls=%async_computation.42 | async-start | bytes 9437184 | tf_op jit(solution)/shard_map/reduce_scatter | solution.py:408
  1344.4 474.8 %reduce-scatter.21.cloned.1.call-start = ((), (), s32[]{:S(2)}) async-start(), calls=%async_computation.36 | async-start | bytes 9437184 | tf_op jit(solution)/shard_map/reduce_scatter | solution.py:390
  1363.9 862.8 %reduce-scatter.45.cloned.1.call-start = ((), (), s32[]{:S(2)}) async-start(), calls=%async_computation.48 | async-start | bytes 28311552 | tf_op jit(solution)/shard_map/reduce_scatter | solution.py:327
  1377.8 1255.4 %reduce-scatter.41.cloned.1.call-start = ((), (), s32[]{:S(2)}) async-start(), calls=%async_computation.46 | async-start | bytes 28311552 | tf_op jit(solution)/shard_map/reduce_scatter | solution.py:321
  1392.5 1647.3 %reduce-scatter.37.cloned.1.call-start = ((), (), s32[]{:S(2)}) async-start(), calls=%async_computation.44 | async-start | bytes 28311552 | tf_op jit(solution)/shard_map/reduce_scatter | solution.py:315
  1406.5 1699.7 %reduce-scatter.31.cloned.1.call-start = ((), (), s32[]{:S(2)}) async-start(), calls=%async_computation.41 | async-start | bytes 655360 | tf_op jit(solution)/shard_map/reduce_scatter | solution.py:428
  1422.7 1685.1 %reduce-scatter.27.cloned.1.call-start = ((), (), s32[]{:S(2)}) async-start(), calls=%async_computation.39 | async-start | bytes 655360 | tf_op jit(solution)/shard_map/reduce_scatter | solution.py:425
  1514.3 1600.3 %reduce-scatter.35.cloned.1.call-start = ((), (), s32[]{:S(2)}) async-start(), calls=%async_computation.43 | async-start | bytes 1310720 | tf_op jit(solution)/shard_map/reduce_scatter | solution.py:431
  1667.1 1475.1 %reduce-scatter.23.cloned.1.call-start = ((), (), s32[]{:S(2)}) async-start(), calls=%async_computation.37 | async-start | bytes 1310720 | tf_op jit(solution)/shard_map/reduce_scatter | solution.py:422
  1819.3 1363.4 %reduce-scatter.47.cloned.1.call-start = ((), (), s32[]{:S(2)}) async-start(), calls=%async_computation.49 | async-start | bytes 3932160 | tf_op jit(solution)/shard_map/reduce_scatter | solution.py:341
  2226.7 996.6 %reduce-scatter.43.cloned.1.call-start = ((), (), s32[]{:S(2)}) async-start(), calls=%async_computation.47 | async-start | bytes 3932160 | tf_op jit(solution)/shard_map/reduce_scatter | solution.py:338
  2633.3 630.5 %reduce-scatter.39.cloned.1.call-start = ((), (), s32[]{:S(2)}) async-start(), calls=%async_computation.45 | async-start | bytes 3932160 | tf_op jit(solution)/shard_map/reduce_scatter | solution.py:335
  (87 other events, 6981.1 us)
Sparse Core Ops, SparseCore 0:
  10.1 42.8 all-gather.24
  55.1 38.8 all-gather.18
  96.2 48.0 all-gather.30
  145.7 33.5 all-gather.26
  180.7 34.9 all-gather.20
  217.7 51.0 all-gather.34
  270.9 97.2 all-gather.42
  370.4 97.1 all-gather.38
  469.7 98.1 all-gather.46
  569.2 56.4 all-gather.32
  670.8 58.2 all-gather.36
  730.6 154.7 all-gather.44
  886.8 154.7 all-gather.40
  1043.1 154.8 all-gather.48
  1334.7 87.9 reduce-scatter.28
  1426.6 87.6 reduce-scatter.24
  1517.9 149.1 reduce-scatter.32
  1671.2 148.0 reduce-scatter.20
  1823.1 403.5 reduce-scatter.44
  2230.4 402.7 reduce-scatter.40
  2637.1 402.6 reduce-scatter.36
  3144.7 37.9 reduce-scatter.46
  3185.3 37.9 reduce-scatter.42
  3225.8 37.9 reduce-scatter.38
  (8 shorter events, 187.4 us)
where the time goes:
time: 3280 us; the launch traced here: 3270 us
  waiting for transfers between devices  2860 us (87%)
  matrix products  220 us (7%)
  blocking collectives  81.8 us (2%)
  other arithmetic  49.3 us (2%)
  local copies, waits for them, and re-layouts  37.3 us (1%)
    reduce_scatter x1, waiting for transfers between devices, per_device(): lax.psum_scatter(grad_down.astype(jnp.bfloat16), 'dp', scatter_dimension=...  407 us
    reduce_scatter x1, waiting for transfers between devices, per_device(): lax.psum_scatter(product(normed_mlp, grad_up_low, CONTRACT_ROWS).astype(j...  406 us
    reduce_scatter x1, waiting for transfers between devices, per_device(): lax.psum_scatter(product(normed_mlp, grad_gate_low, CONTRACT_ROWS).astype...  406 us
    reduce_scatter x1, waiting for transfers between devices, per_device(): lax.psum_scatter(grad_w_out.astype(jnp.bfloat16), 'dp', scatter_dimension...  153 us
    reduce_scatter x1, waiting for transfers between devices, per_device(): lax.psum_scatter(product(normed, grad_query_low, CONTRACT_ROWS).astype(jn...  152 us
    all_gather x1, waiting for transfers between devices, per_device(): lax.all_gather(gathered[5], 'seq', axis=1, tiled=True)  149 us
    all_gather x1, waiting for transfers between devices, per_device(): lax.all_gather(gathered[6], 'seq', axis=0, tiled=True)  142 us
    all_gather x1, waiting for transfers between devices, per_device(): lax.all_gather(gathered[4], 'seq', axis=1, tiled=True)  142 us
  transfers between devices with their start and end apart: 34, of which 29 were waited for; matrix products, arithmetic and copies ran while one was open for 7% of the time, Pallas kernels for 0%

commit v1 on v0

v1 whole, which is shorter than its diff:
```python
import functools
import math

import jax
import jax.numpy as jnp
from jax import lax
from jax.experimental import pallas as pl
from jax.experimental.pallas import tpu as pltpu
from jax.sharding import PartitionSpec as P

MAXSHORT = 4
GROUP = 4
MESH = pl.DeviceIdType.MESH
HBM = pl.BlockSpec(memory_space=pltpu.HBM)
VMEM = pl.BlockSpec(memory_space=pltpu.VMEM)
BF16 = jnp.bfloat16
F32 = jnp.float32


NORM_EPS = 1e-06
ROPE_BASE = 1000000.0
MASKED = -1e30
CONTRACT_ROWS = (((0,), (0,)), ((), ()))
CONTRACT_COLS = (((1,), (1,)), ((), ()))


def root_mean_norm(values, gain):
    return values * lax.rsqrt(jnp.mean(values * values, axis=-1, keepdims=True) + NORM_EPS) * gain


def apply_rotary(values, position):
    half_width = values.shape[-1] // 2
    freq_index = jnp.arange(half_width, dtype=jnp.float32)
    inverse = jnp.exp(freq_index * (-2.0 * math.log(ROPE_BASE) / values.shape[-1]))
    angles = position.astype(jnp.float32)[:, None] * inverse[None, :]
    cosine = jnp.cos(angles)[:, None, :]
    sine_part = jnp.sin(angles)[:, None, :]
    first = values[..., :half_width]
    second = values[..., half_width:]
    return jnp.concatenate(
        [first * cosine - second * sine_part, second * cosine + first * sine_part], axis=-1
    )


def head_prep(flat, gain, position):
    return apply_rotary(
        root_mean_norm(flat.reshape(flat.shape[0], -1, gain.shape[0]), gain), position
    )


def product(left, right, dims):
    return lax.dot_general(left, right, dims, preferred_element_type=jnp.float32)


def layout(lengths_part, perm_part, body_len):
    row_count, shorts = lengths_part.shape
    doc_total = row_count * shorts
    starts = body_len + jnp.cumsum(lengths_part, axis=1) - lengths_part
    kept_flat = lengths_part.reshape(doc_total)
    matched = perm_part[:, None] == jnp.arange(doc_total, dtype=jnp.int32)[None, :]
    placed = jnp.sum(jnp.where(matched, kept_flat[:, None], 0), axis=0).reshape(row_count, shorts)
    new_at = body_len + jnp.cumsum(placed, axis=1) - placed
    new_start = jnp.sum(jnp.where(matched, new_at.reshape(doc_total)[None, :], 0), axis=1)
    return (starts.reshape(doc_total), kept_flat, new_start, perm_part // shorts)


def slot_labels(
    kept_flat,
    new_start,
    dest_row,
    part,
    my_row,
    valid_here,
    body_len,
    shard_len,
    row_len,
    row_count,
):
    doc_total = kept_flat.shape[0]
    local = jnp.arange(shard_len, dtype=jnp.int32)
    doc_ids = jnp.arange(doc_total, dtype=jnp.int32)
    inside = (
        (dest_row == my_row)[None, :]
        & (local[:, None] >= new_start[None, :])
        & (local[:, None] < (new_start + kept_flat)[None, :])
    )
    offset = local[:, None] - new_start[None, :]
    in_short = jnp.any(inside, axis=1)
    short_seg = jnp.sum(
        jnp.where(inside, row_count + part * doc_total + doc_ids[None, :], 0), axis=1
    )
    short_pos = jnp.sum(jnp.where(inside, offset, 0), axis=1)
    long_pos = part * body_len + local
    in_long = (local < body_len) & (long_pos < valid_here)
    flat_slot = my_row * row_len + part * shard_len + local
    segment = jnp.where(in_long, my_row, jnp.where(in_short, short_seg, -1 - flat_slot))
    position = jnp.where(in_long, long_pos, short_pos)
    return (segment, position, in_long, in_short)


def attend_scores(query_rows, keys_all, seg_query, pos_query, seg_key, pos_key):
    grouped_heads = query_rows.reshape(
        query_rows.shape[0], keys_all.shape[1], -1, query_rows.shape[-1]
    )
    raw = jnp.einsum(
        "tngd,und->ngtu", grouped_heads, keys_all, preferred_element_type=jnp.float32
    ) * query_rows.shape[-1] ** (-0.5)
    allowed = (seg_query[:, None] == seg_key[None, :]) & (pos_key[None, :] <= pos_query[:, None])
    return (jnp.where(allowed, raw, MASKED), grouped_heads)


def attend_forward(query_rows, keys_all, values_all, seg_query, pos_query, seg_key, pos_key):
    masked, grouped_heads = attend_scores(
        query_rows, keys_all, seg_query, pos_query, seg_key, pos_key
    )
    peak = jnp.max(masked, axis=-1, keepdims=True)
    expd = jnp.exp(masked - peak)
    total_weight = jnp.sum(expd, axis=-1, keepdims=True)
    probs = (expd / total_weight).astype(jnp.bfloat16)
    log_total = peak + jnp.log(total_weight)
    context = jnp.einsum(
        "ngtu,und->tngd", probs, values_all, preferred_element_type=jnp.float32
    ).reshape(query_rows.shape[0], -1)
    return (context.astype(jnp.bfloat16), log_total)


def attend_backward(
    query_rows, keys_all, values_all, grad_att, log_total, seg_query, pos_query, seg_key, pos_key
):
    masked, grouped_heads = attend_scores(
        query_rows, keys_all, seg_query, pos_query, seg_key, pos_key
    )
    probs_full = jnp.exp(masked - log_total)
    probs_low = probs_full.astype(jnp.bfloat16)
    grad_group = grad_att.reshape(grouped_heads.shape)
    grad_probs = jnp.einsum(
        "tngd,und->ngtu", grad_group, values_all, preferred_element_type=jnp.float32
    )
    grad_values = jnp.einsum(
        "ngtu,tngd->und", probs_low, grad_group, preferred_element_type=jnp.float32
    )
    spread_sum = jnp.sum(probs_full * grad_probs, axis=-1, keepdims=True)
    grad_scores = (probs_full * (grad_probs - spread_sum)).astype(jnp.bfloat16)
    scale_factor = query_rows.shape[-1] ** (-0.5)
    grad_queries = (
        jnp.einsum(
            "ngtu,und->tngd", grad_scores, keys_all, preferred_element_type=jnp.float32
        ).reshape(query_rows.shape)
        * scale_factor
    )
    grad_keys = (
        jnp.einsum("ngtu,tngd->und", grad_scores, grouped_heads, preferred_element_type=jnp.float32)
        * scale_factor
    )
    return (grad_queries, grad_keys, grad_values)


class Place:
    def __init__(self, dp_size, seq_size):
        self.dp_size = dp_size
        self.seq_size = seq_size
        self.high = dp_size // GROUP
        self.cores = seq_size // 2
        self.d = lax.axis_index("dp")
        self.s = lax.axis_index("seq")
        self.g = lax.rem(self.d, GROUP)
        self.h = lax.div(self.d, GROUP)
        self.x = lax.div(self.s, self.cores)
        self.c = lax.rem(self.s, self.cores)
        self.y = lax.rem(self.g, 2)
        self.l = lax.div(self.g, 2)
        self.gy = self.g + 1 - 2 * self.y
        self.gl = lax.rem(self.g + 2, GROUP)
        self.gd = 3 - self.g
        self.y_peer = (self.h * GROUP + self.gy, self.s)
        self.l_peer = (self.h * GROUP + self.gl, self.s)
        self.d_peer = (self.h * GROUP + self.gd, self.s)
        self.x_peer = (self.d, (1 - self.x) * self.cores + self.c)
        self.c_peer = (self.d, self.x * self.cores + 1 - self.c)

    def h_peer(self, step):
        return (lax.rem(self.h + step, self.high) * GROUP + self.g, self.s)

    def h_from(self, step):
        return lax.rem(self.h + self.high - step, self.high)

    def g_peer(self, step):
        return (self.h * GROUP + lax.rem(self.g + step, GROUP), self.s)


class Mover:
    def __init__(self, send_sems, recv_sems, local_sems):
        self.send_sems = send_sems
        self.recv_sems = recv_sems
        self.local_sems = local_sems
        self.count = 0
        self.local_count = 0
        self.sent = []

    def send(self, source, target, device):
        index = self.count
        self.count += 1
        copy = pltpu.make_async_remote_copy(
            src_ref=source,
            dst_ref=target,
            send_sem=self.send_sems.at[index],
            recv_sem=self.recv_sems.at[index],
            device_id=device,
            device_id_type=MESH,
        )
        copy.start()
        self.sent.append(copy)
        return copy

    def local(self, source, target):
        index = self.local_count
        self.local_count += 1
        copy = pltpu.make_async_copy(source, target, self.local_sems.at[index])
        copy.start()
        return copy

    def finish(self):
        for copy in self.sent:
            copy.wait_send()


def greet(peers):
    barrier = pltpu.get_barrier_semaphore()
    for peer in peers:
        pl.semaphore_signal(barrier, inc=1, device_id=peer, device_id_type=MESH)
    pl.semaphore_wait(barrier, len(peers))


def dp_peers(place):
    return [
        (lax.rem(place.d + step, place.dp_size), place.s) for step in range(1, place.dp_size)
    ]


def sems(count, local):
    return [
        pltpu.SemaphoreType.DMA((count,)),
        pltpu.SemaphoreType.DMA((count,)),
        pltpu.SemaphoreType.DMA((max(local, 1),)),
    ]


def comm_params(collective_id, vmem=None):
    return pltpu.CompilerParams(
        collective_id=collective_id,
        has_side_effects=True,
        vmem_limit_bytes=vmem if vmem is not None else 60 * 1024 * 1024,
    )


def add_rows(target, terms, rows, chunk):
    def step(index, carry):
        part = pl.ds(pl.multiple_of(index * chunk, chunk), chunk)
        total = terms[0][part, :].astype(F32)
        for term in terms[1:]:
            total = total + term[part, :].astype(F32)
        target[part, :] = total.astype(target.dtype)
        return carry

    lax.fori_loop(0, rows // chunk, step, 0)


def exchange_kernel(sizes, with_row, *refs):
    place = Place(*sizes)
    if with_row:
        out_ref, row_ref, in_ref, rows_ref, send_sems, recv_sems, local_sems = refs
    else:
        out_ref, in_ref, send_sems, recv_sems, local_sems = refs
    mover = Mover(send_sems, recv_sems, local_sems)
    greet(dp_peers(place))
    copies = []
    for step in range(1, place.dp_size):
        other = lax.rem(place.d + step, place.dp_size)
        copies.append(mover.send(out_ref.at[other], in_ref.at[place.d], (other, place.s)))
        if with_row:
            copies.append(mover.send(row_ref, rows_ref.at[place.d], (other, place.s)))
    in_ref[place.d] = out_ref[place.d]
    if with_row:
        rows_ref[place.d] = row_ref[...]
    for copy in copies:
        copy.wait_recv()
    mover.finish()


def exchange(sizes, collective_id, blocks, row=None):
    dp_size = sizes[0]
    args = (blocks,) if row is None else (blocks, row)
    shapes = [jax.ShapeDtypeStruct(blocks.shape, blocks.dtype)]
    if row is not None:
        shapes.append(jax.ShapeDtypeStruct((dp_size,) + row.shape, row.dtype))
    return pl.pallas_call(
        functools.partial(exchange_kernel, sizes, row is not None),
        out_shape=shapes,
        in_specs=[VMEM] * len(args),
        out_specs=[VMEM] * len(shapes),
        scratch_shapes=sems((dp_size - 1) * len(args), 0),
        compiler_params=comm_params(collective_id),
        name="exchange_rows",
    )(*args)


class GatherSeq:
    sends = 3

    def __init__(self, place, mover, own, full):
        self.place, self.mover, self.full = place, mover, full
        self.local = mover.local(own, full.at[place.s])
        self.over_x = mover.send(own, full.at[place.s], place.x_peer)
        self.over_c = mover.send(own, full.at[place.s], place.c_peer)

    def forward(self):
        self.over_x.wait_recv()
        block = self.full.at[self.place.x_peer[1]]
        self.passed = self.mover.send(block, block, self.place.c_peer)

    def finish(self):
        self.local.wait()
        self.over_c.wait_recv()
        self.passed.wait_recv()


class GatherGroup:
    sends = 10

    def __init__(self, place, mover, own, full):
        self.place, self.mover, self.full = place, mover, full
        half = own.shape[0] // 2
        self.low, self.top = pl.ds(0, half), pl.ds(half, half)
        self.local = mover.local(own, full.at[place.g, place.c])
        spot = full.at[place.g, place.c]
        self.y_low = mover.send(own.at[self.low], spot.at[self.low], place.y_peer)
        self.l_top = mover.send(own.at[self.top], spot.at[self.top], place.l_peer)
        self.y_top = mover.send(own.at[self.top], spot.at[self.top], place.y_peer)
        self.l_low = mover.send(own.at[self.low], spot.at[self.low], place.l_peer)
        self.core = [mover.send(own, spot, place.c_peer)]

    def forward(self):
        place, mover, full = self.place, self.mover, self.full
        self.y_low.wait_recv()
        part = full.at[place.gy, place.c, self.low]
        self.d_low = mover.send(part, part, place.l_peer)
        self.l_top.wait_recv()
        part = full.at[place.gl, place.c, self.top]
        self.d_top = mover.send(part, part, place.y_peer)
        self.y_top.wait_recv()
        part = full.at[place.gy, place.c]
        self.core.append(mover.send(part, part, place.c_peer))
        self.l_low.wait_recv()
        part = full.at[place.gl, place.c]
        self.core.append(mover.send(part, part, place.c_peer))

    def finish(self):
        place = self.place
        self.d_low.wait_recv()
        self.d_top.wait_recv()
        part = self.full.at[place.gd, place.c]
        self.core.append(self.mover.send(part, part, place.c_peer))
        self.local.wait()
        for copy in self.core:
            copy.wait_recv()


def gather_seq_kernel(sizes, own, full, send_sems, recv_sems, local_sems):
    place = Place(*sizes)
    mover = Mover(send_sems, recv_sems, local_sems)
    greet([place.x_peer, place.c_peer])
    gather = GatherSeq(place, mover, own, full)
    gather.forward()
    gather.finish()
    mover.finish()


def gather_seq(sizes, collective_id, own):
    return pl.pallas_call(
        functools.partial(gather_seq_kernel, sizes),
        out_shape=jax.ShapeDtypeStruct((sizes[1],) + own.shape, own.dtype),
        in_specs=[HBM],
        out_specs=HBM,
        scratch_shapes=sems(GatherSeq.sends, 1),
        compiler_params=comm_params(collective_id),
        name="gather_row",
    )(own)


def gather_group_kernel(sizes, own, full, send_sems, recv_sems, local_sems):
    place = Place(*sizes)
    mover = Mover(send_sems, recv_sems, local_sems)
    greet([place.y_peer, place.l_peer, place.c_peer])
    gather = GatherGroup(place, mover, own, full)
    gather.forward()
    gather.finish()
    mover.finish()


def gather_group(sizes, collective_id, own):
    return pl.pallas_call(
        functools.partial(gather_group_kernel, sizes),
        out_shape=jax.ShapeDtypeStruct((GROUP, sizes[1] // 2) + own.shape, own.dtype),
        in_specs=[HBM],
        out_specs=HBM,
        scratch_shapes=sems(GatherGroup.sends, 1),
        compiler_params=comm_params(collective_id),
        name="gather_group",
    )(own)


class ScatterSeq:
    sends = 3
    locals = 2

    @staticmethod
    def scratch(rows, width):
        block = (rows, width)
        return [
            pltpu.VMEM((2,) + block, BF16),
            pltpu.VMEM((2,) + block, BF16),
            pltpu.VMEM(block, BF16),
        ]

    def __init__(self, place, mover, parts, out, own, from_c, from_x):
        self.place, self.mover, self.out = place, mover, out
        self.own, self.from_c, self.from_x = own, from_c, from_x
        cores = place.cores
        places = ((1 - place.x) * cores, place.x * cores)
        self.over_c, self.mine = [], []
        for index, base in enumerate(places):
            self.over_c.append(
                mover.send(parts.at[base + 1 - place.c], from_c.at[index], place.c_peer)
            )
            self.mine.append(mover.local(parts.at[base + place.c], own.at[index]))

    def forward(self):
        rows = self.own.shape[1]
        self.over_c[0].wait_recv()
        self.mine[0].wait()
        add_rows(self.own.at[0], [self.own.at[0], self.from_c.at[0]], rows, 32)
        self.over_x = self.mover.send(self.own.at[0], self.from_x, self.place.x_peer)

    def finish(self):
        rows = self.own.shape[1]
        self.over_c[1].wait_recv()
        self.mine[1].wait()
        self.over_x.wait_recv()
        add_rows(self.out, [self.own.at[1], self.from_c.at[1], self.from_x], rows, 32)


class ScatterGroup:
    sends = 10
    locals = 4

    @staticmethod
    def scratch(rows, width):
        block = (GROUP, rows, width)
        half = (rows // 2, width)
        return [
            pltpu.VMEM(block, BF16),
            pltpu.VMEM(block, BF16),
            pltpu.VMEM((6,) + half, BF16),
        ]

    def __init__(self, place, mover, parts, out, own, from_c, landed):
        self.place, self.mover, self.out = place, mover, out
        self.own, self.from_c, self.landed = own, from_c, landed
        self.over_c, self.mine = [], []
        for index, owner in enumerate((place.gd, place.gy, place.gl, place.g)):
            self.over_c.append(
                mover.send(parts.at[owner, 1 - place.c], from_c.at[index], place.c_peer)
            )
            self.mine.append(mover.local(parts.at[owner, place.c], own.at[index]))

    def ready(self, index):
        self.over_c[index].wait_recv()
        self.mine[index].wait()
        rows = self.own.shape[1]
        add_rows(self.own.at[index], [self.own.at[index], self.from_c.at[index]], rows, 32)

    def forward(self):
        place, mover, own, landed = self.place, self.mover, self.own, self.landed
        half = own.shape[1] // 2
        low, top = pl.ds(0, half), pl.ds(half, half)
        self.ready(0)
        self.y_diag = mover.send(own.at[0, low], landed.at[0], place.y_peer)
        self.l_diag = mover.send(own.at[0, top], landed.at[1], place.l_peer)
        self.ready(1)
        self.y_own = mover.send(own.at[1, low], landed.at[2], place.y_peer)
        self.ready(2)
        self.l_own = mover.send(own.at[2, top], landed.at[3], place.l_peer)
        self.y_diag.wait_recv()
        add_rows(own.at[2, low], [own.at[2, low], landed.at[0]], half, 32)
        self.l_last = mover.send(own.at[2, low], landed.at[4], place.l_peer)
        self.l_diag.wait_recv()
        add_rows(own.at[1, top], [own.at[1, top], landed.at[1]], half, 32)
        self.y_last = mover.send(own.at[1, top], landed.at[5], place.y_peer)
        self.ready(3)

    def finish(self):
        own, landed = self.own, self.landed
        half = own.shape[1] // 2
        low, top = pl.ds(0, half), pl.ds(half, half)
        self.y_own.wait_recv()
        self.l_last.wait_recv()
        add_rows(self.out.at[low], [own.at[3, low], landed.at[2], landed.at[4]], half, 32)
        self.l_own.wait_recv()
        self.y_last.wait_recv()
        add_rows(self.out.at[top], [own.at[3, top], landed.at[3], landed.at[5]], half, 32)


def scatter_seq_kernel(sizes, parts, out, own, from_c, from_x, send_sems, recv_sems, local_sems):
    place = Place(*sizes)
    mover = Mover(send_sems, recv_sems, local_sems)
    greet([place.x_peer, place.c_peer])
    scatter = ScatterSeq(place, mover, parts, out, own, from_c, from_x)
    scatter.forward()
    scatter.finish()
    mover.finish()


def scatter_seq(sizes, collective_id, parts):
    rows, width = parts.shape[1:]
    return pl.pallas_call(
        functools.partial(scatter_seq_kernel, sizes),
        out_shape=jax.ShapeDtypeStruct((rows, width), F32),
        in_specs=[HBM],
        out_specs=VMEM,
        scratch_shapes=ScatterSeq.scratch(rows, width) + sems(ScatterSeq.sends, ScatterSeq.locals),
        compiler_params=comm_params(collective_id),
        name="scatter_row",
    )(parts)


def scatter_group_kernel(sizes, parts, out, own, from_c, landed, send_sems, recv_sems, local_sems):
    place = Place(*sizes)
    mover = Mover(send_sems, recv_sems, local_sems)
    greet([place.y_peer, place.l_peer, place.c_peer])
    scatter = ScatterGroup(place, mover, parts, out, own, from_c, landed)
    scatter.forward()
    scatter.finish()
    mover.finish()


def scatter_group(sizes, collective_id, parts):
    rows, width = parts.shape[2:]
    return pl.pallas_call(
        functools.partial(scatter_group_kernel, sizes),
        out_shape=jax.ShapeDtypeStruct((rows, width), F32),
        in_specs=[HBM],
        out_specs=VMEM,
        scratch_shapes=ScatterGroup.scratch(rows, width)
        + sems(ScatterGroup.sends, ScatterGroup.locals),
        compiler_params=comm_params(collective_id),
        name="scatter_group",
    )(parts)


class GatherDp:
    def __init__(self, place, mover, own, full):
        self.place, self.mover, self.own, self.full = place, mover, own, full
        self.local = mover.local(own, full.at[place.d])
        spot = full.at[place.d]
        self.over_h = [
            mover.send(own, spot, place.h_peer(step)) for step in range(1, place.high)
        ]
        self.over_l = [mover.send(own, spot, place.l_peer)]
        self.over_y = [mover.send(own, spot, place.y_peer)]

    def forward_high(self):
        place = self.place
        for step, copy in enumerate(self.over_h, 1):
            copy.wait_recv()
            block = self.full.at[place.h_from(step) * GROUP + place.g]
            self.over_l.append(self.mover.send(block, block, place.l_peer))
            self.over_y.append(self.mover.send(block, block, place.y_peer))

    def forward_l(self):
        place = self.place
        for step, copy in enumerate(self.over_l):
            copy.wait_recv()
            high = place.h if step == 0 else place.h_from(step)
            block = self.full.at[high * GROUP + place.gl]
            self.over_y.append(self.mover.send(block, block, place.y_peer))

    def finish(self):
        self.local.wait()
        for copy in self.over_y:
            copy.wait_recv()


class GatherColumns:
    def __init__(self, place, mover, own, full):
        self.place, self.mover, self.full = place, mover, full
        self.quarter = own.shape[1] // GROUP
        self.near = pl.ds(0, self.quarter)
        self.far = pl.ds(self.quarter, self.quarter)
        self.over_g = []
        spot = full.at[place.h, place.g, :, self.near]
        for step in (3, 1, 2):
            to = lax.rem(place.g + step, GROUP)
            columns = pl.ds(pl.multiple_of(to * self.quarter, self.quarter), self.quarter)
            self.over_g.append(mover.send(own.at[:, columns], spot, place.g_peer(step)))
        columns = pl.ds(pl.multiple_of(place.g * self.quarter, self.quarter), self.quarter)
        self.local = mover.local(own.at[:, columns], spot)

    def forward_g(self):
        place = self.place
        self.local.wait()
        for copy in self.over_g:
            copy.wait_recv()
        near = self.full.at[place.h, :, :, self.near]
        far = self.full.at[place.h, :, :, self.far]
        self.over_h = [
            self.mover.send(near, near, place.h_peer(step)) for step in range(1, place.high)
        ]
        self.over_x = [self.mover.send(near, far, place.x_peer)]

    def forward_high(self):
        place = self.place
        for step, copy in enumerate(self.over_h, 1):
            copy.wait_recv()
            high = place.h_from(step)
            self.over_x.append(
                self.mover.send(
                    self.full.at[high, :, :, self.near],
                    self.full.at[high, :, :, self.far],
                    place.x_peer,
                )
            )

    def finish(self):
        for copy in self.over_x:
            copy.wait_recv()


def gather_all_kernel(sizes, *refs):
    qkv, wo, wg, wu, wd, gy, nrm = refs[:7]
    full_qkv, full_wo, full_g, full_u, full_d, full_gy, full_nrm = refs[7:14]
    send_sems, recv_sems, local_sems = refs[14:]
    place = Place(*sizes)
    mover = Mover(send_sems, recv_sems, local_sems)
    greet(dp_peers(place) + [place.x_peer, place.c_peer])
    row = GatherSeq(place, mover, nrm, full_nrm)
    attn = [GatherDp(place, mover, qkv, full_qkv)]
    mlp = [GatherColumns(place, mover, wg, full_g)]
    mlp.append(GatherColumns(place, mover, wu, full_u))
    mlp[0].forward_g()
    attn[0].forward_high()
    attn.append(GatherDp(place, mover, wo, full_wo))
    mlp[1].forward_g()
    mlp.append(GatherColumns(place, mover, wd, full_d))
    row.forward()
    attn[0].forward_l()
    mlp[0].forward_high()
    attn[1].forward_high()
    mlp[2].forward_g()
    attn[1].forward_l()
    group = GatherGroup(place, mover, gy, full_gy)
    mlp[1].forward_high()
    group.forward()
    mlp[2].forward_high()
    for part in [row, group] + attn + mlp:
        part.finish()
    mover.finish()


def gather_all(sizes, collective_id, qkv, wo, wg, wu, wd, gy, nrm):
    dp_size, seq_size = sizes
    high = dp_size // GROUP
    rows = qkv.shape[0]
    wide = (high, GROUP, rows, wg.shape[1] // 2)
    shapes = [
        (dp_size,) + qkv.shape,
        (dp_size,) + wo.shape,
        wide,
        wide,
        wide,
        (GROUP, seq_size // 2) + gy.shape,
        (seq_size,) + nrm.shape,
    ]
    sends = 2 * (high + 1 + high * 3) + 3 * (3 + 2 * high) + GatherGroup.sends + GatherSeq.sends
    return pl.pallas_call(
        functools.partial(gather_all_kernel, sizes),
        out_shape=[jax.ShapeDtypeStruct(shape, BF16) for shape in shapes],
        in_specs=[HBM] * 7,
        out_specs=[HBM] * 7,
        scratch_shapes=sems(sends, 7),
        compiler_params=comm_params(collective_id),
        name="gather_weights",
    )(qkv, wo, wg, wu, wd, gy, nrm)


class ScatterColumns:
    @staticmethod
    def scratch(place_high, rows, quarter):
        group_rows = GROUP * rows
        return [
            pltpu.VMEM((place_high * group_rows, quarter), BF16),
            pltpu.VMEM((place_high * group_rows, quarter), BF16),
            pltpu.VMEM((max(place_high - 1, 1), group_rows, quarter), BF16),
            pltpu.VMEM((group_rows, quarter), BF16),
            pltpu.VMEM((GROUP - 1, rows, quarter), BF16),
        ]

    def __init__(self, place, mover, parts, out, own, from_x, from_h, mine, from_g):
        self.place, self.mover, self.out = place, mover, out
        self.own, self.from_x, self.from_h = own, from_x, from_h
        self.mine, self.from_g = mine, from_g
        quarter = own.shape[1]
        self.over_x = mover.send(parts.at[:, pl.ds(quarter, quarter)], from_x, place.x_peer)
        self.local = mover.local(parts.at[:, pl.ds(0, quarter)], own)

    def forward_x(self):
        place, own = self.place, self.own
        group_rows = self.mine.shape[0]
        self.over_x.wait_recv()
        self.local.wait()
        add_rows(own, [own, self.from_x], own.shape[0], 64)
        self.over_h = []
        for step in range(1, place.high):
            high = lax.rem(place.h + step, place.high)
            rows = pl.ds(pl.multiple_of(high * group_rows, group_rows), group_rows)
            self.over_h.append(
                self.mover.send(own.at[rows], self.from_h.at[step - 1], place.h_peer(step))
            )

    def forward_high(self):
        place = self.place
        group_rows = self.mine.shape[0]
        own_rows = pl.ds(pl.multiple_of(place.h * group_rows, group_rows), group_rows)
        for copy in self.over_h:
            copy.wait_recv()
        terms = [self.own.at[own_rows]]
        terms += [self.from_h.at[step] for step in range(place.high - 1)]
        add_rows(self.mine, terms, group_rows, 64)
        rows = group_rows // GROUP
        self.over_g = []
        for step in range(1, GROUP):
            to = lax.rem(place.g + step, GROUP)
            block = pl.ds(pl.multiple_of(to * rows, rows), rows)
            self.over_g.append(
                self.mover.send(self.mine.at[block], self.from_g.at[step - 1], place.g_peer(step))
            )

    def finish(self):
        place, quarter = self.place, self.own.shape[1]
        rows = self.mine.shape[0] // GROUP
        block = pl.ds(pl.multiple_of(place.g * rows, rows), rows)
        columns = pl.ds(pl.multiple_of(place.g * quarter, quarter), quarter)
        self.out[:, columns] = self.mine[block, :].astype(F32)
        for step, copy in enumerate(self.over_g, 1):
            copy.wait_recv()
            source = lax.rem(place.g + GROUP - step, GROUP)
            columns = pl.ds(pl.multiple_of(source * quarter, quarter), quarter)
            self.out[:, columns] = self.from_g[step - 1].astype(F32)


class ScatterDp:
    @staticmethod
    def scratch(high, rows, width):
        return [
            pltpu.VMEM((2, high, rows, width), BF16),
            pltpu.VMEM((2, high, rows, width), BF16),
            pltpu.VMEM((high, rows, width), BF16),
            pltpu.VMEM((max(high - 1, 1), rows, width), BF16),
        ]

    def __init__(self, place, mover, parts, out, own, from_y, from_l, from_h):
        self.place, self.mover, self.out = place, mover, out
        self.own, self.from_y, self.from_l, self.from_h = own, from_y, from_l, from_h
        self.over_y, self.local = [], []
        for index, l_owner in enumerate((1 - place.l, place.l)):
            self.over_y.append(
                mover.send(parts.at[:, l_owner, 1 - place.y], from_y.at[index], place.y_peer)
            )
            self.local.append(mover.local(parts.at[:, l_owner, place.y], own.at[index]))

    def ready(self, index):
        self.over_y[index].wait_recv()
        self.local[index].wait()
        for high in range(self.place.high):
            own = self.own.at[index, high]
            add_rows(own, [own, self.from_y.at[index, high]], own.shape[0], 32)

    def forward_y(self):
        self.ready(0)
        self.over_l = self.mover.send(self.own.at[0], self.from_l, self.place.l_peer)

    def forward_l(self):
        place = self.place
        self.ready(1)
        self.over_l.wait_recv()
        for high in range(place.high):
            own = self.own.at[1, high]
            add_rows(own, [own, self.from_l.at[high]], own.shape[0], 32)
        self.over_h = []
        for step in range(1, place.high):
            high = lax.rem(place.h + step, place.high)
            self.over_h.append(
                self.mover.send(self.own.at[1, high], self.from_h.at[step - 1], place.h_peer(step))
            )

    def finish(self):
        for copy in self.over_h:
            copy.wait_recv()
        terms = [self.own.at[1, self.place.h]]
        terms += [self.from_h.at[step] for step in range(self.place.high - 1)]
        add_rows(self.out, terms, self.out.shape[0], 32)


def scatter_all_kernel(sizes, *refs):
    grad_qkv, grad_wo, grad_g, grad_u, grad_d, down = refs[:6]
    out_qkv, out_wo, out_g, out_u, out_d, out_down = refs[6:12]
    send_sems, recv_sems, local_sems = refs[-3:]
    scratch = list(refs[12:-3])

    def take(count):
        taken = scratch[:count]
        del scratch[:count]
        return taken

    place = Place(*sizes)
    mover = Mover(send_sems, recv_sems, local_sems)
    greet(dp_peers(place) + [place.x_peer, place.c_peer])
    wo = ScatterDp(place, mover, grad_wo, out_wo, *take(4))
    qkv = ScatterDp(place, mover, grad_qkv, out_qkv, *take(4))
    mlp = [
        ScatterColumns(place, mover, grad, out, *take(5))
        for grad, out in ((grad_d, out_d), (grad_g, out_g), (grad_u, out_u))
    ]
    row = ScatterGroup(place, mover, down, out_down, *take(3))
    mlp[0].forward_x()
    wo.forward_y()
    qkv.forward_y()
    mlp[1].forward_x()
    mlp[0].forward_high()
    wo.forward_l()
    mlp[2].forward_x()
    qkv.forward_l()
    mlp[1].forward_high()
    row.forward()
    mlp[2].forward_high()
    for part in (mlp[0], wo, mlp[1], qkv, row, mlp[2]):
        part.finish()
    mover.finish()


def scatter_all(sizes, collective_id, grad_qkv, grad_wo, grad_g, grad_u, grad_d, down):
    dp_size, _ = sizes
    high = dp_size // GROUP
    rows = grad_g.shape[0] // dp_size
    quarter = grad_g.shape[1] // 2
    shapes = [
        (rows, grad_qkv.shape[1]),
        (rows, grad_wo.shape[1]),
        (rows, GROUP * quarter),
        (rows, GROUP * quarter),
        (rows, GROUP * quarter),
        down.shape[2:],
    ]
    split = (high, 2, 2, rows)
    args = (
        grad_qkv.reshape(split + (-1,)),
        grad_wo.reshape(split + (-1,)),
        grad_g,
        grad_u,
        grad_d,
        down,
    )
    scratch = ScatterDp.scratch(high, rows, grad_wo.shape[1])
    scratch += ScatterDp.scratch(high, rows, grad_qkv.shape[1])
    for _ in range(3):
        scratch += ScatterColumns.scratch(high, rows, quarter)
    scratch += ScatterGroup.scratch(*down.shape[2:])
    sends = 2 * (2 + high) + 3 * (high + 3) + ScatterGroup.sends
    return pl.pallas_call(
        functools.partial(scatter_all_kernel, sizes),
        out_shape=[jax.ShapeDtypeStruct(shape, F32) for shape in shapes],
        in_specs=[HBM] * 6,
        out_specs=[VMEM] * 6,
        scratch_shapes=scratch + sems(sends, 4 + 3 + ScatterGroup.locals),
        compiler_params=comm_params(collective_id),
        name="scatter_grads",
    )(*args)


def per_device(
    sizes,
    hidden_in,
    valid_len,
    doc_lengths,
    doc_perm,
    attn_norm,
    w_query,
    key_weight,
    value_weight,
    w_out,
    query_norm,
    key_norm_gain,
    mlp_norm,
    w_gate,
    w_up,
    w_down,
    out_grad,
):
    shard_len = hidden_in.shape[0]
    model_width = hidden_in.shape[1]
    seq_count = doc_lengths.shape[0]
    row_count = doc_lengths.shape[1]
    shorts = doc_lengths.shape[2]
    row_len = shard_len * seq_count
    cap_len = MAXSHORT
    body_len = shard_len - shorts * cap_len
    my_row = lax.axis_index("dp")
    my_part = lax.axis_index("seq")
    valid_here = valid_len[my_row]
    all_starts, all_kept, all_new, all_dest = jax.vmap(
        lambda lengths_part, perm_part: layout(lengths_part, perm_part, body_len)
    )(doc_lengths, doc_perm)
    part_ids = jnp.arange(seq_count, dtype=jnp.int32)
    seg_parts, pos_parts, long_parts, short_parts = jax.vmap(
        lambda kept_p, new_p, dest_p, part: slot_labels(
            kept_p, new_p, dest_p, part, my_row, valid_here, body_len, shard_len, row_len, row_count
        )
    )(all_kept, all_new, all_dest, part_ids)
    segment = seg_parts.reshape(row_len)
    position = pos_parts.reshape(row_len)
    seg_local = lax.dynamic_index_in_dim(seg_parts, my_part, 0, keepdims=False)
    pos_local = lax.dynamic_index_in_dim(pos_parts, my_part, 0, keepdims=False)
    keep_long = lax.dynamic_index_in_dim(long_parts, my_part, 0, keepdims=False)
    live_local = keep_long | lax.dynamic_index_in_dim(short_parts, my_part, 0, keepdims=False)
    starts = lax.dynamic_index_in_dim(all_starts, my_part, 0, keepdims=False)
    kept_flat = lax.dynamic_index_in_dim(all_kept, my_part, 0, keepdims=False)
    new_start = lax.dynamic_index_in_dim(all_new, my_part, 0, keepdims=False)
    dest_row = lax.dynamic_index_in_dim(all_dest, my_part, 0, keepdims=False)
    row_ids = jnp.arange(row_count, dtype=jnp.int32)
    local_slots = jnp.arange(shard_len, dtype=jnp.int32)
    cap_ids = jnp.arange(cap_len, dtype=jnp.int32)
    my_dest = lax.dynamic_slice_in_dim(dest_row, my_row * shorts, shorts)
    my_starts = lax.dynamic_slice_in_dim(starts, my_row * shorts, shorts)
    my_kept = lax.dynamic_slice_in_dim(kept_flat, my_row * shorts, shorts)
    going = my_dest[None, :] == row_ids[:, None]
    send_start = jnp.sum(jnp.where(going, my_starts[None, :], 0), axis=1)
    send_len = jnp.sum(jnp.where(going, my_kept[None, :], 0), axis=1)
    send_map = (
        (
            (cap_ids[None, :, None] < send_len[:, None, None])
            & (local_slots[None, None, :] == send_start[:, None, None] + cap_ids[None, :, None])
        )
        .reshape(row_count * cap_len, shard_len)
        .astype(jnp.bfloat16)
    )
    coming = (dest_row == my_row).reshape(row_count, shorts)
    recv_start = jnp.sum(jnp.where(coming, new_start.reshape(row_count, shorts), 0), axis=1)
    recv_len = jnp.sum(jnp.where(coming, kept_flat.reshape(row_count, shorts), 0), axis=1)
    recv_map = (
        (
            (cap_ids[None, None, :] < recv_len[None, :, None])
            & (local_slots[:, None, None] == recv_start[None, :, None] + cap_ids[None, None, :])
        )
        .reshape(shard_len, row_count * cap_len)
        .astype(jnp.bfloat16)
    )
    high_dims = (row_count * cap_len, model_width)
    outgoing = jnp.dot(send_map, hidden_in, preferred_element_type=F32).astype(BF16)
    flat_blocks = (row_count, 16, cap_len * model_width // 16)

    def spread(piece, total):
        return lax.dynamic_update_slice(
            jnp.zeros((total,), F32), piece.astype(F32), (my_row * piece.shape[0],)
        )

    head_size = query_norm.shape[0] * row_count
    gain_row = jnp.concatenate(
        [
            spread(attn_norm, model_width),
            spread(mlp_norm, model_width),
            spread(query_norm, head_size),
            spread(key_norm_gain, head_size),
        ]
    )[None, :]
    incoming, gain_rows = exchange(sizes, 0, outgoing.reshape(flat_blocks), gain_row)
    gains = jnp.sum(gain_rows, axis=0)[0]
    cuts = (model_width, 2 * model_width, 2 * model_width + head_size)
    gain_attn, gain_mlp, gain_query, gain_key = jnp.split(gains, cuts)
    moved = jnp.where(keep_long[:, None], hidden_in.astype(F32), 0.0) + jnp.dot(
        recv_map, incoming.reshape(high_dims), preferred_element_type=F32
    )
    live_scale = live_local.astype(F32)[:, None]
    grad_y_low = (out_grad.astype(F32) * live_scale).astype(BF16)
    normed_own = root_mean_norm(moved, gain_attn).astype(BF16)
    qkv_own = jnp.concatenate([w_query, key_weight, value_weight], axis=1)
    qkv_mat, out_mat, gate_mat, up_mat, down_mat, grad_y_all, normed = gather_all(
        sizes, 1, qkv_own, w_out.T, w_gate, w_up, w_down.T, grad_y_low, normed_own
    )
    qkv_mat = qkv_mat.reshape(model_width, -1)
    out_mat = out_mat.reshape(model_width, -1)
    gate_mat = gate_mat.reshape(model_width, -1)
    up_mat = up_mat.reshape(model_width, -1)
    down_mat = down_mat.reshape(model_width, -1)
    group_rows = GROUP * (seq_count // 2) * shard_len
    grad_y_all = grad_y_all.reshape(group_rows, model_width)
    normed = normed.reshape(row_len, model_width)
    query_width = w_query.shape[1]
    key_width = key_weight.shape[1]
    qkv_cuts = (query_width, query_width + key_width)
    qkv_lin = jnp.dot(normed, qkv_mat, preferred_element_type=F32)
    query_lin, key_linear, value_linear = jnp.split(qkv_lin, qkv_cuts, axis=1)
    query_rows = head_prep(query_lin, gain_query, position).astype(BF16)
    rotated_keys = head_prep(key_linear, gain_key, position).astype(BF16)
    value_heads = value_linear.astype(BF16).reshape(row_len, -1, head_size)
    attended, log_total = attend_forward(
        query_rows, rotated_keys, value_heads, segment, position, segment, position
    )
    projected = product(attended, out_mat, CONTRACT_COLS).astype(BF16)
    resid_rows = moved + scatter_seq(
        sizes, 2, projected.reshape(seq_count, shard_len, model_width)
    )
    normed_mlp_own = root_mean_norm(resid_rows, gain_mlp).astype(BF16)
    normed_mlp = gather_group(sizes, 3, normed_mlp_own).reshape(group_rows, model_width)
    gate = jnp.dot(normed_mlp, gate_mat, preferred_element_type=F32)
    upper = jnp.dot(normed_mlp, up_mat, preferred_element_type=F32)
    hidden = (jax.nn.silu(gate) * upper).astype(BF16)
    down_part = product(hidden, down_mat, CONTRACT_COLS).astype(BF16)
    grad_mid = jnp.dot(grad_y_all, down_mat, preferred_element_type=F32)
    silu_pull = jax.vjp(lambda gate_in, up_in: jax.nn.silu(gate_in) * up_in, gate, upper)[1]
    grad_gate_lin, grad_up_lin = silu_pull(grad_mid)
    grad_gate_low = grad_gate_lin.astype(BF16)
    grad_up_low = grad_up_lin.astype(BF16)
    grad_nmlp_part = (
        product(grad_gate_low, gate_mat, CONTRACT_COLS)
        + product(grad_up_low, up_mat, CONTRACT_COLS)
    ).astype(BF16)
    group_shape = (GROUP, seq_count // 2, shard_len, model_width)
    grad_nmlp = scatter_group(sizes, 4, grad_nmlp_part.reshape(group_shape))
    grad_down = product(grad_y_all, hidden, CONTRACT_ROWS).astype(BF16)
    grad_gate = product(normed_mlp, grad_gate_low, CONTRACT_ROWS).astype(BF16)
    grad_up = product(normed_mlp, grad_up_low, CONTRACT_ROWS).astype(BF16)
    mlp_pull = jax.vjp(root_mean_norm, resid_rows, gain_mlp)[1]
    grad_resid_part, grad_gain_mlp = mlp_pull(grad_nmlp)
    grad_resid = grad_y_low.astype(F32) + grad_resid_part
    grad_proj = gather_seq(sizes, 5, grad_resid.astype(BF16)).reshape(row_len, model_width)
    grad_w_out = product(grad_proj, attended, CONTRACT_ROWS).astype(BF16)
    grad_att = jnp.dot(grad_proj, out_mat, preferred_element_type=F32).astype(BF16)
    grad_queries, grad_keys, grad_values = attend_backward(
        query_rows,
        rotated_keys,
        value_heads,
        grad_att,
        log_total,
        segment,
        position,
        segment,
        position,
    )
    query_pull = jax.vjp(
        lambda flat, gain_in: head_prep(flat, gain_in, position), query_lin, gain_query
    )[1]
    grad_query_lin, grad_gain_query = query_pull(grad_queries)
    key_pull = jax.vjp(
        lambda flat, gain_in: head_prep(flat, gain_in, position), key_linear, gain_key
    )[1]
    grad_key_lin, grad_gain_key = key_pull(grad_keys)
    grad_qkv_low = jnp.concatenate(
        [
            grad_query_lin.astype(BF16),
            grad_key_lin.astype(BF16),
            grad_values.reshape(row_len, -1).astype(BF16),
        ],
        axis=1,
    )
    grad_normed_part = product(grad_qkv_low, qkv_mat, CONTRACT_COLS).astype(BF16)
    grad_normed = scatter_seq(
        sizes, 6, grad_normed_part.reshape(seq_count, shard_len, model_width)
    )
    grad_qkv = product(normed, grad_qkv_low, CONTRACT_ROWS).astype(BF16)
    attn_pull = jax.vjp(root_mean_norm, moved, gain_attn)[1]
    grad_moved_part, grad_gain_attn = attn_pull(grad_normed)
    grad_moved = (grad_resid + grad_moved_part).astype(BF16)
    gain_grads = lax.psum(
        jnp.concatenate([grad_gain_attn, grad_gain_mlp, grad_gain_query, grad_gain_key]),
        ("dp", "seq"),
    )
    back_out = product(recv_map, grad_moved, CONTRACT_ROWS).astype(BF16)
    (returned,) = exchange(sizes, 7, back_out.reshape(flat_blocks))
    grad_hidden = (
        jnp.where(keep_long[:, None], grad_moved.astype(F32), 0.0)
        + product(send_map, returned.reshape(high_dims), CONTRACT_ROWS)
    ).astype(BF16)
    out_qkv, out_wo, out_gate, out_up, out_down, down_sum = scatter_all(
        sizes, 8, grad_qkv, grad_w_out, grad_gate, grad_up, grad_down,
        down_part.reshape(group_shape),
    )
    mixed = ((resid_rows + down_sum) * live_scale).astype(BF16)
    out_query, out_key, out_value = jnp.split(out_qkv, qkv_cuts, axis=1)
    device = my_row * seq_count + my_part

    def own_piece(vector):
        size = vector.shape[0] // (row_count * seq_count)
        return lax.dynamic_slice_in_dim(vector, device * size, size)

    sum_attn, sum_mlp, sum_query, sum_key = [own_piece(v) for v in jnp.split(gain_grads, cuts)]
    return (
        mixed,
        grad_hidden,
        sum_attn,
        out_query,
        out_key,
        out_value,
        out_wo.T,
        sum_query,
        sum_key,
        sum_mlp,
        out_gate,
        out_up,
        out_down.T,
    )


def solution(mesh):
    in_specs = (
        P(("dp", "seq"), None),
        P(),
        P(),
        P(),
        P("dp"),
        P("dp", "seq"),
        P("dp", "seq"),
        P("dp", "seq"),
        P("seq", "dp"),
        P("dp"),
        P("dp"),
        P("dp"),
        P("dp", "seq"),
        P("dp", "seq"),
        P("seq", "dp"),
        P(("dp", "seq"), None),
    )
    out_specs = (
        P(("dp", "seq"), None),
        P(("dp", "seq"), None),
        P(("dp", "seq")),
        P("dp", "seq"),
        P("dp", "seq"),
        P("dp", "seq"),
        P("seq", "dp"),
        P(("dp", "seq")),
        P(("dp", "seq")),
        P(("dp", "seq")),
        P("dp", "seq"),
        P("dp", "seq"),
        P("seq", "dp"),
    )
    return jax.shard_map(
        functools.partial(per_device, (mesh.shape["dp"], mesh.shape["seq"])), mesh=mesh, in_specs=in_specs, out_specs=out_specs, check_vma=False
    )
```

time: 3280 us -> 850 us (0.26)
  waiting for transfers between devices: 2860 us -> 0 us
  Pallas kernels: 0 us -> 536 us
  matrix products: 220 us -> 129 us
  blocking collectives: 81.8 us -> 41.6 us
    reduce_scatter x16 -> x0, waiting for transfers between devices: 1810 us -> none  [the longest x1 407 us: per_device(): lax.psum_scatter(grad_down.astype(jnp.bfloat16), 'dp', scatter_dimension=...]
    all_gather x16 -> x0, waiting for transfers between devices: 1040 us -> none  [the longest x1 149 us: per_device(): lax.all_gather(gathered[5], 'seq', axis=1, tiled=True)]
    pallas_call x0 -> x9, Pallas kernels: none -> 536 us  [the longest x1 194 us: scatter_all(): pl.pallas_call(functools.partial(scatter_all_kernel, sizes), out_shape=[j...]
    dot_general x16 -> x12, matrix products: 129 us -> 67.4 us  [product(): lax.dot_general(left, right, dims, preferred_element_type=jnp.float32)]
    unnamed x3 -> x0, blocking collectives: 47.3 us -> none
    psum x0 -> x1, blocking collectives: none -> 41.6 us  [per_device(): lax.psum(jnp.concatenate([grad_gain_attn, grad_gain_mlp, grad_gain_query,...]
    all_gather x2 -> x0, blocking collectives: 34.5 us -> none  [the longest x1 18.2 us: per_device(): lax.all_gather(mlp_norm, 'dp', axis=0, tiled=True)]
  transfers between devices with their start and end apart: 34 -> 0, of which waited for: 29 -> 0; matrix products, arithmetic and copies ran while one was open for 7% -> 0% of each run, Pallas kernels for 0% -> 0%
where the time goes in v1:
time: 850 us; the launch traced here: 840 us
  Pallas kernels  536 us (63%)
  matrix products  129 us (15%)
  other arithmetic  71.4 us (8%)
  local copies, waits for them, and re-layouts  58.9 us (7%)
  blocking collectives  41.6 us (5%)
    pallas_call x1, Pallas kernels, scatter_all(): pl.pallas_call(functools.partial(scatter_all_kernel, sizes), out_shape=[j...  194 us
    pallas_call x1, Pallas kernels, gather_all(): pl.pallas_call(functools.partial(gather_all_kernel, sizes), out_shape=[ja...  185 us
    dot_general x12, matrix products, product(): lax.dot_general(left, right, dims, preferred_element_type=jnp.float32)  67.4 us
    pallas_call x2, Pallas kernels, scatter_seq(): pl.pallas_call(functools.partial(scatter_seq_kernel, sizes), out_shape=ja...  45.6 us
    psum x1, blocking collectives, per_device(): lax.psum(jnp.concatenate([grad_gain_attn, grad_gain_mlp, grad_gain_query,...  41.6 us
    pallas_call x1, Pallas kernels, scatter_group(): pl.pallas_call(functools.partial(scatter_group_kernel, sizes), out_shape=...  32.7 us
    pallas_call x1, Pallas kernels, gather_group(): pl.pallas_call(functools.partial(gather_group_kernel, sizes), out_shape=j...  31.1 us
    pallas_call x1, Pallas kernels, gather_seq(): pl.pallas_call(functools.partial(gather_seq_kernel, sizes), out_shape=jax...  26.3 us

profile of v1, /device:TPU:0, one launch (start us, length us, event | category | flops | bytes accessed | tf_op | source)
XLA Modules:
  0.0 840.0 jit_solution(6239839387567745597)
XLA Ops:
  18.5 12.6 %exchange_rows.2 = (bf16[8,16,512]{2,1,0:T(8,128)(2,1)}, f32[8,1,4352]{2,1,0:T(1,128)}) custom-call(bf16[8,16,512]{2,1,0:T(8,128)(2,1)} %reshape.616.refs_0_, f32[1,4352]{1,0:T(1,128)} %broadcast_in_dim.117.refs_1_), custom_call_target="tpu_custom_call" | custom-call | tf_op jit(solution)/shard_map/exchange_rows/pallas_call | solution.py:296
  43.1 184.8 %gather_weights.1 = (bf16[8,256,1024]{2,1,0:T(8,128)(2,1)}, bf16[8,256,512]{2,1,0:T(8,128)(2,1)}, bf16[2,4,256,768]{3,2,1,0:T(8,128)(2,1)}, bf16[2,4,256,768]{3,...) custom-call(bf16[256,1024]{1,0:T(8,128)(2,1)} %pad_maximum_fusion.4., ...), custom_call_target="tpu_custom_call" | custom-call | tf_op jit(solution)/shard_map/gather_weights/pallas_call | solution.py:684
  227.9 6.1 fusion.77
  266.1 6.9 fusion.78
  284.8 22.6 %scatter_row.2 = f32[192,2048]{1,0:T(8,128)} custom-call(bf16[4,192,2048]{2,1,0:T(8,128)(2,1)} %bitcast.157), custom_call_target="tpu_custom_call" | custom-call | tf_op jit(solution)/shard_map/scatter_row/pallas_call | solution.py:525
  310.2 31.1 %gather_group.1 = bf16[4,2,192,2048]{3,2,1,0:T(8,128)(2,1)} custom-call(bf16[192,2048]{1,0:T(8,128)(2,1)} %multiply_convert_fusion.3.own), custom_call_target="tpu_custom_call" | custom-call | tf_op jit(solution)/shard_map/gather_group/pallas_call | solution.py:401
  341.3 9.6 %fusion.79 = f32[1536,768]{1,0:T(8,128)} fusion(bf16[1536,2048]{1,0:T(8,128)(2,1)} %bitcast.146, bf16[2048,768]{1,0:T(8,128)(2,1)} %bitcast.191), kind=kOutput, calls=%fused_computation.196 | convolution fusion | flops 4831838208 | bytes 14155776 | tf_op jit(solution)/shard_map/dot_general | solution.py:1023
  350.9 11.0 %multiply_convert_fusion = (bf16[1536,768]{1,0:T(8,128)(2,1)}, bf16[1536,768]{1,0:T(8,128)(2,1)S(1)}, bf16[1536,768]{1,0:T(8,128)(2,1)}) fusion(f32[1536,768]{1,0:T(8,128)} %fusion.79, f32[1536,768]{1,0:T(8,128)} %fusion.78, bf16[1536,2048]{1,0:T(8,128)(2,1)S(1)} %bitcast.147, bf16[2048,768]{1,0:T(8,128)(2,1)S(1)} %bitcast.189), kind=kOutput, calls=%fused_computation.18 | convolution fusion | flops 4850712576 | bytes 25952256 | tf_op jit(solution)/shard_map/dot_general | solution.py:1024
  362.0 8.3 convolution_convert_fusion.4.refs_4_
  370.3 7.1 convolution_convert_fusion
  377.4 6.5 convolution_convert_fusion.6.refs_2_
  383.9 6.7 convolution_convert_fusion.5.refs_3_
  390.6 8.0 fusion.80
  398.6 9.8 %add_convert_fusion = bf16[1536,2048]{1,0:T(8,128)(2,1)} fusion(f32[1536,2048]{1,0:T(8,128)} %fusion.80, bf16[1536,768]{1,0:T(8,128)(2,1)S(1)} %copy-done.85, bf16[2048,768]{1,0:T(8,128)(2,1)S(1)} %bitcast.190), kind=kOutput, calls=%fused_computation | convolution fusion | flops 4838129664 | bytes 24379392 | tf_op jit(solution)/shard_map/dot_general | solution.py:52
  408.4 32.7 %scatter_group.1 = f32[192,2048]{1,0:T(8,128)} custom-call(bf16[4,2,192,2048]{3,2,1,0:T(8,128)(2,1)} %bitcast.152), custom_call_target="tpu_custom_call" | custom-call | tf_op jit(solution)/shard_map/scatter_group/pallas_call | solution.py:548
  444.7 26.3 %gather_row.1 = bf16[4,192,2048]{2,1,0:T(8,128)(2,1)} custom-call(bf16[192,2048]{1,0:T(8,128)(2,1)} %fusion.65.own), custom_call_target="tpu_custom_call" | custom-call | tf_op jit(solution)/shard_map/gather_row/pallas_call | solution.py:379
  481.5 9.4 %fusion = (f32[2,2,768]{2,1,0:T(2,128)S(1)}, f32[2,768,768,2]{2,1,3,0:T(8,128)}) fusion(f32[2,2,768,768]{2,3,1,0:T(8,128)} %copy-done, f32[2,2,768]{2,1,0:T(2,128)} %copy-done.41, bf16[768,2,2,128]{0,3,2,1:T(8,128)(2,1)} %bitcast.161, bf16[768,2,128,1]{2,1,0,3:T(2,128)(2,1)} %bitcast.166), kind=kOutput, calls=%fused_computation.3 | convolution fusion | flops 611054592 | bytes 20078592 | tf_op jit(solution)/shard_map/tngd,und->ngtu/dot_general | solution.py:136
  490.9 10.2 %fusion.2 = bf16[2,2,768,768]{2,3,1,0:T(8,128)(2,1)} fusion(f32[2,768,768,2]{2,1,3,0:T(8,128)} %get-tuple-element.193, f32[2,2,768,768]{2,3,1,0:T(8,128)} %copy-done, f32[2,2,768]{2,1,0:T(2,128)S(1)} %get-tuple-element.192, f32[2,2,768]{2,1,0:T(2,128)S(1)} %copy-done.42), kind=kLoop, calls=%fused_computation.5 | loop fusion | flops 9437184 | bytes 23617536 | tf_op jit(solution)/shard_map/convert_element_type | solution.py:143
  501.1 5.3 fusion.23
  543.6 5.3 convolution_convert_fusion.1
  548.9 194.0 %scatter_grads.1 = (f32[256,1024]{1,0:T(8,128)}, f32[256,512]{1,0:T(8,128)}, f32[256,1536]{1,0:T(8,128)}, f32[256,1536]{1,0:T(8,128)}, f32[256,1536]{1,0:T(8,128)}, /*index=5*/f32[192,2048]{1,0:T(8,128)}) custom-call(bf16[2,2,2,256,1024]{4,3,2,1,0:T(8,128)(2,1)} %bitcast.153, bf16[2,2,2,256,512]{4,3,2,1,0:T(8,128)(2,1)} %bitcast.162, ...), custom_call_target="tpu_custom_call" | custom-call | tf_op jit(solution)/shard_map/scatter_grads/pallas_call | solution.py:878
  745.0 23.0 %scatter_row.3 = f32[192,2048]{1,0:T(8,128)} custom-call(bf16[4,192,2048]{2,1,0:T(8,128)(2,1)} %bitcast.156), custom_call_target="tpu_custom_call" | custom-call | tf_op jit(solution)/shard_map/scatter_row/pallas_call | solution.py:525
  774.3 41.6 %psum.7 = f32[4352]{0:T(1024)S(1)} all-reduce(f32[4352]{0:T(1024)S(1)} %pad_maximum_fusion.8), channel_id=1, replica_groups=mesh['dp'=8,'seq'=4] {'dp','seq'}, use_global_device_ids=true, to_apply=%region_27.28 | all-reduce | flops 4352 | bytes 34816 | tf_op jit(solution)/shard_map/psum | solution.py:1082
  820.4 9.0 %exchange_rows.3 = bf16[8,16,512]{2,1,0:T(8,128)(2,1)} custom-call(bf16[8,16,512]{2,1,0:T(8,128)(2,1)} %reshape.637.refs_0_), custom_call_target="tpu_custom_call" | custom-call | tf_op jit(solution)/shard_map/exchange_rows/pallas_call | solution.py:296
  (341 shorter events, 149.4 us)
Async XLA Ops:
  0.6 33.1 %copy-start.39 = (bf16[512,256]{1,0:T(8,128)(2,1)S(1)}, bf16[512,256]{1,0:T(8,128)(2,1)}, u32[]{:S(2)}) copy-start(bf16[512,256]{1,0:T(8,128)(2,1)} %param.24) | copy-start | bytes 786436
  0.7 33.9 %copy-start.45 = (bf16[256,256]{1,0:T(8,128)(2,1)S(1)}, bf16[256,256]{1,0:T(8,128)(2,1)}, u32[]{:S(2)}) copy-start(bf16[256,256]{1,0:T(8,128)(2,1)} %param.23) | copy-start | bytes 393220
  0.7 33.9 %copy-start.46 = (bf16[256,256]{1,0:T(8,128)(2,1)S(1)}, bf16[256,256]{1,0:T(8,128)(2,1)}, u32[]{:S(2)}) copy-start(bf16[256,256]{1,0:T(8,128)(2,1)} %param.22) | copy-start | bytes 393220
  0.7 33.9 %copy-start.40 = (bf16[256,512]{1,0:T(8,128)(2,1)S(1)}, bf16[256,512]{1,0:T(8,128)(2,1)}, u32[]{:S(2)}) copy-start(bf16[256,512]{1,0:T(8,128)(2,1)} %param.21) | copy-start | bytes 786436
  11.1 30.3 %copy-start.68 = (pred[192]{0:T(512)(128)(4,1)}, pred[192]{0:T(512)(128)(4,1)S(1)}, u32[]{:S(2)}) copy-start(pred[192]{0:T(512)(128)(4,1)S(1)} %get-tuple-element.195) | copy-start | bytes 580
  11.1 28.1 %copy-start.54 = (f32[192]{0:T(256)}, f32[192]{0:T(256)S(1)}, u32[]{:S(2)}) copy-start(f32[192]{0:T(256)S(1)} %or_convert_fusion) | copy-start | bytes 2308
  16.0 25.4 %copy-start.64 = (pred[32]{0:T(512)(128)(4,1)}, pred[32]{0:T(512)(128)(4,1)S(1)}, u32[]{:S(2)}) copy-start(pred[32]{0:T(512)(128)(4,1)S(1)} %get-tuple-element.184) | copy-start | bytes 100
  16.2 25.2 %copy-start.66 = (s32[32]{0:T(128)}, s32[32]{0:T(128)S(1)}, u32[]{:S(2)}) copy-start(s32[32]{0:T(128)S(1)} %get-tuple-element.186) | copy-start | bytes 388
  16.2 23.0 %copy-start.13 = (bf16[192,2048]{1,0:T(8,128)(2,1)S(1)}, bf16[192,2048]{1,0:T(8,128)(2,1)}, u32[]{:S(2)}) copy-start(bf16[192,2048]{1,0:T(8,128)(2,1)} %param.31) | copy-start | bytes 2359300
  39.2 222.7 %copy-start.10 = (f32[768,64]{1,0:T(8,128)}, f32[768,64]{1,0:T(8,128)S(1)}, u32[]{:S(2)}) copy-start(f32[768,64]{1,0:T(8,128)S(1)} %get-tuple-element.182) | copy-start | bytes 589828
  41.9 185.9 %copy-start.59 = (f32[192]{0:T(256)}, f32[192]{0:T(256)S(1)}, u32[]{:S(2)}) copy-start(f32[192]{0:T(256)S(1)} %get-tuple-element.188) | copy-start | bytes 2308
  42.0 185.9 %copy-start.52 = (f32[192]{0:T(256)}, f32[192]{0:T(256)S(1)}, u32[]{:S(2)}) copy-start(f32[192]{0:T(256)S(1)} %fusion.56) | copy-start | bytes 2308
  243.5 17.4 %copy-start.2 = (f32[768,4,128]{2,1,0:T(4,128)}, f32[768,4,128]{2,1,0:T(4,128)S(1)}, u32[]{:S(2)}) copy-start(f32[768,4,128]{2,1,0:T(4,128)S(1)} %reshape.622) | copy-start | bytes 4718596
  279.2 199.7 %copy-start.41 = (f32[2,2,768]{2,1,0:T(2,128)}, f32[2,2,768]{2,1,0:T(2,128)S(1)}, u32[]{:S(2)}) copy-start(f32[2,2,768]{2,1,0:T(2,128)S(1)} %log_add_fusion) | copy-start | bytes 36868
  309.1 134.0 %copy-start.50 = (f32[192]{0:T(256)}, f32[192]{0:T(256)S(1)}, u32[]{:S(2)}) copy-start(f32[192]{0:T(256)S(1)} %fusion.57) | copy-start | bytes 2308
  341.3 20.6 %slice-start.5 = ((s8[6291456]{0:T(1024)(128)(4,1)}), s8[4194304]{0:T(1024)(128)(4,1)S(1)}, s32[]{:S(2)}) async-start(s8[6291456]{0:T(1024)(128)(4,1)} %bitcast.182), calls=%async_computation.5 | async-start | bytes 8388608
  745.0 23.0 %copy-start.44 = (f32[1,2048]{1,0:T(1,128)S(1)}, f32[1,2048]{1,0:T(1,128)}, u32[]{:S(2)}) copy-start(f32[1,2048]{1,0:T(1,128)} %copy-done.43) | copy-start | bytes 24580
  745.0 23.0 %copy-start.53 = (f32[192]{0:T(256)S(1)}, f32[192]{0:T(256)}, u32[]{:S(2)}) copy-start(f32[192]{0:T(256)} %copy-done.52) | copy-start | bytes 2308
  770.4 47.9 %copy-start.65 = (pred[32]{0:T(512)(128)(4,1)S(1)}, pred[32]{0:T(512)(128)(4,1)}, u32[]{:S(2)}) copy-start(pred[32]{0:T(512)(128)(4,1)} %copy-done.64) | copy-start | bytes 100
  770.4 47.9 %copy-start.67 = (s32[32]{0:T(128)S(1)}, s32[32]{0:T(128)}, u32[]{:S(2)}) copy-start(s32[32]{0:T(128)} %copy-done.66) | copy-start | bytes 388
  770.4 60.0 %copy-start.69 = (pred[192]{0:T(512)(128)(4,1)S(1)}, pred[192]{0:T(512)(128)(4,1)}, u32[]{:S(2)}) copy-start(pred[192]{0:T(512)(128)(4,1)} %copy-done.68) | copy-start | bytes 580
  770.4 60.0 %copy-start.73 = (pred[32]{0:T(512)(128)(4,1)S(1)}, pred[32]{0:T(512)(128)(4,1)}, u32[]{:S(2)}) copy-start(pred[32]{0:T(512)(128)(4,1)} %copy-done.72) | copy-start | bytes 100
  770.4 60.0 %copy-start.75 = (s32[32]{0:T(128)S(1)}, s32[32]{0:T(128)}, u32[]{:S(2)}) copy-start(s32[32]{0:T(128)} %copy-done.74) | copy-start | bytes 388
  774.2 58.8 %copy-start.34 = (f32[256,1024]{1,0:T(8,128)S(1)}, f32[256,1024]{1,0:T(8,128)}, u32[]{:S(2)}) copy-start(f32[256,1024]{1,0:T(8,128)} %get-tuple-element.38) | copy-start | bytes 3145732
  (70 other events, 367.1 us)

commit v2 on v1

v2 whole, which is shorter than its diff:
```python
import functools
import math

import jax
import jax.numpy as jnp
from jax import lax
from jax.experimental import pallas as pl
from jax.experimental.pallas import tpu as pltpu
from jax.sharding import PartitionSpec as P

MAXSHORT = 4
GROUP = 4
MESH = pl.DeviceIdType.MESH
HBM = pl.BlockSpec(memory_space=pltpu.HBM)
VMEM = pl.BlockSpec(memory_space=pltpu.VMEM)
BF16 = jnp.bfloat16
F32 = jnp.float32


NORM_EPS = 1e-06
ROPE_BASE = 1000000.0
MASKED = -1e30
CONTRACT_ROWS = (((0,), (0,)), ((), ()))
CONTRACT_COLS = (((1,), (1,)), ((), ()))


def product(left, right, dims):
    return lax.dot_general(left, right, dims, preferred_element_type=jnp.float32)


def layout(lengths_part, perm_part, body_len):
    row_count, shorts = lengths_part.shape
    doc_total = row_count * shorts
    starts = body_len + jnp.cumsum(lengths_part, axis=1) - lengths_part
    kept_flat = lengths_part.reshape(doc_total)
    matched = perm_part[:, None] == jnp.arange(doc_total, dtype=jnp.int32)[None, :]
    placed = jnp.sum(jnp.where(matched, kept_flat[:, None], 0), axis=0).reshape(row_count, shorts)
    new_at = body_len + jnp.cumsum(placed, axis=1) - placed
    new_start = jnp.sum(jnp.where(matched, new_at.reshape(doc_total)[None, :], 0), axis=1)
    return (starts.reshape(doc_total), kept_flat, new_start, perm_part // shorts)


def slot_labels(
    kept_flat,
    new_start,
    dest_row,
    part,
    my_row,
    valid_here,
    body_len,
    shard_len,
    row_len,
    row_count,
):
    doc_total = kept_flat.shape[0]
    local = jnp.arange(shard_len, dtype=jnp.int32)
    doc_ids = jnp.arange(doc_total, dtype=jnp.int32)
    inside = (
        (dest_row == my_row)[None, :]
        & (local[:, None] >= new_start[None, :])
        & (local[:, None] < (new_start + kept_flat)[None, :])
    )
    offset = local[:, None] - new_start[None, :]
    in_short = jnp.any(inside, axis=1)
    short_seg = jnp.sum(
        jnp.where(inside, row_count + part * doc_total + doc_ids[None, :], 0), axis=1
    )
    short_pos = jnp.sum(jnp.where(inside, offset, 0), axis=1)
    long_pos = part * body_len + local
    in_long = (local < body_len) & (long_pos < valid_here)
    flat_slot = my_row * row_len + part * shard_len + local
    segment = jnp.where(in_long, my_row, jnp.where(in_short, short_seg, -1 - flat_slot))
    position = jnp.where(in_long, long_pos, short_pos)
    return (segment, position, in_long, in_short)


class Place:
    def __init__(self, dp_size, seq_size):
        self.dp_size = dp_size
        self.seq_size = seq_size
        self.high = dp_size // GROUP
        self.cores = seq_size // 2
        self.d = lax.axis_index("dp")
        self.s = lax.axis_index("seq")
        self.g = lax.rem(self.d, GROUP)
        self.h = lax.div(self.d, GROUP)
        self.x = lax.div(self.s, self.cores)
        self.c = lax.rem(self.s, self.cores)
        self.y = lax.rem(self.g, 2)
        self.l = lax.div(self.g, 2)
        self.gy = self.g + 1 - 2 * self.y
        self.gl = lax.rem(self.g + 2, GROUP)
        self.gd = 3 - self.g
        self.y_peer = (self.h * GROUP + self.gy, self.s)
        self.l_peer = (self.h * GROUP + self.gl, self.s)
        self.d_peer = (self.h * GROUP + self.gd, self.s)
        self.x_peer = (self.d, (1 - self.x) * self.cores + self.c)
        self.c_peer = (self.d, self.x * self.cores + 1 - self.c)

    def h_peer(self, step):
        return (lax.rem(self.h + step, self.high) * GROUP + self.g, self.s)

    def h_from(self, step):
        return lax.rem(self.h + self.high - step, self.high)

    def g_peer(self, step):
        return (self.h * GROUP + lax.rem(self.g + step, GROUP), self.s)


class Mover:
    def __init__(self, send_sems, recv_sems, local_sems):
        self.send_sems = send_sems
        self.recv_sems = recv_sems
        self.local_sems = local_sems
        self.count = 0
        self.local_count = 0
        self.sent = []

    def send(self, source, target, device):
        index = self.count
        self.count += 1
        copy = pltpu.make_async_remote_copy(
            src_ref=source,
            dst_ref=target,
            send_sem=self.send_sems.at[index],
            recv_sem=self.recv_sems.at[index],
            device_id=device,
            device_id_type=MESH,
        )
        copy.start()
        self.sent.append(copy)
        return copy

    def local(self, source, target):
        index = self.local_count
        self.local_count += 1
        copy = pltpu.make_async_copy(source, target, self.local_sems.at[index])
        copy.start()
        return copy

    def drain(self, copy):
        copy.wait_send()
        self.sent = [other for other in self.sent if other is not copy]

    def finish(self):
        for copy in self.sent:
            copy.wait_send()


def greet(peers):
    barrier = pltpu.get_barrier_semaphore()
    for peer in peers:
        pl.semaphore_signal(barrier, inc=1, device_id=peer, device_id_type=MESH)
    pl.semaphore_wait(barrier, len(peers))


def dp_peers(place):
    return [
        (lax.rem(place.d + step, place.dp_size), place.s) for step in range(1, place.dp_size)
    ]


def sems(count, local):
    return [
        pltpu.SemaphoreType.DMA((count,)),
        pltpu.SemaphoreType.DMA((count,)),
        pltpu.SemaphoreType.DMA((max(local, 1),)),
    ]


def comm_params(collective_id, vmem=None):
    return pltpu.CompilerParams(
        collective_id=collective_id,
        has_side_effects=True,
        vmem_limit_bytes=vmem if vmem is not None else 60 * 1024 * 1024,
    )


def add_rows(target, terms, rows, chunk):
    def step(index, carry):
        part = pl.ds(pl.multiple_of(index * chunk, chunk), chunk)
        total = terms[0][part, :].astype(F32)
        for term in terms[1:]:
            total = total + term[part, :].astype(F32)
        target[part, :] = total.astype(target.dtype)
        return carry

    lax.fori_loop(0, rows // chunk, step, 0)


class GatherSeq:
    sends = 3

    def __init__(self, place, mover, own, full):
        self.place, self.mover, self.full = place, mover, full
        self.local = mover.local(own, full.at[place.s])
        self.over_x = mover.send(own, full.at[place.s], place.x_peer)
        self.over_c = mover.send(own, full.at[place.s], place.c_peer)

    def forward(self):
        self.over_x.wait_recv()
        block = self.full.at[self.place.x_peer[1]]
        self.passed = self.mover.send(block, block, self.place.c_peer)

    def finish(self):
        self.local.wait()
        self.over_c.wait_recv()
        self.passed.wait_recv()


class GatherGroup:
    sends = 10

    def __init__(self, place, mover, own, full):
        self.place, self.mover, self.full = place, mover, full
        half = own.shape[0] // 2
        self.low, self.top = pl.ds(0, half), pl.ds(half, half)
        self.local = mover.local(own, full.at[place.g, place.c])
        spot = full.at[place.g, place.c]
        self.y_low = mover.send(own.at[self.low], spot.at[self.low], place.y_peer)
        self.l_top = mover.send(own.at[self.top], spot.at[self.top], place.l_peer)
        self.y_top = mover.send(own.at[self.top], spot.at[self.top], place.y_peer)
        self.l_low = mover.send(own.at[self.low], spot.at[self.low], place.l_peer)
        self.core = [mover.send(own, spot, place.c_peer)]

    def forward(self):
        place, mover, full = self.place, self.mover, self.full
        self.y_low.wait_recv()
        part = full.at[place.gy, place.c, self.low]
        self.d_low = mover.send(part, part, place.l_peer)
        self.l_top.wait_recv()
        part = full.at[place.gl, place.c, self.top]
        self.d_top = mover.send(part, part, place.y_peer)
        self.y_top.wait_recv()
        part = full.at[place.gy, place.c]
        self.core.append(mover.send(part, part, place.c_peer))
        self.l_low.wait_recv()
        part = full.at[place.gl, place.c]
        self.core.append(mover.send(part, part, place.c_peer))

    def finish_ici(self):
        place = self.place
        self.d_low.wait_recv()
        self.d_top.wait_recv()
        part = self.full.at[place.gd, place.c]
        self.core.append(self.mover.send(part, part, place.c_peer))

    def finish(self):
        self.local.wait()
        for copy in self.core:
            copy.wait_recv()


class GatherDp:
    def __init__(self, place, mover, pieces, full):
        self.place, self.mover, self.full = place, mover, full
        first, last = pieces[0], pieces[-1]
        self.window = pl.ds(first[1], last[1] + last[2] - first[1])
        self.rows = full.shape[0] // place.dp_size
        self.local, self.over_h, self.over_l, self.over_y = [], [], [], []
        own_rows = self.block(place.d)
        high_sends = [[] for _ in range(1, place.high)]
        l_own, y_own = [], []
        for own, start, size in pieces:
            spot = full.at[own_rows, pl.ds(start, size)]
            for step in range(1, place.high):
                high_sends[step - 1].append(mover.send(own, spot, place.h_peer(step)))
            l_own.append(mover.send(own, spot, place.l_peer))
            y_own.append(mover.send(own, spot, place.y_peer))
            self.local.append(mover.local(own, spot))
        self.over_h = high_sends
        self.over_l = [l_own]
        self.over_y = y_own

    def block(self, index):
        return pl.ds(pl.multiple_of(index * self.rows, self.rows), self.rows)

    def forward_high(self):
        place = self.place
        for step, copies in enumerate(self.over_h, 1):
            for copy in copies:
                copy.wait_recv()
            part = self.full.at[self.block(place.h_from(step) * GROUP + place.g), self.window]
            self.over_l.append([self.mover.send(part, part, place.l_peer)])
            self.over_y.append(self.mover.send(part, part, place.y_peer))

    def forward_l(self):
        place = self.place
        for step, copies in enumerate(self.over_l):
            for copy in copies:
                copy.wait_recv()
            high = place.h if step == 0 else place.h_from(step)
            part = self.full.at[self.block(high * GROUP + place.gl), self.window]
            self.over_y.append(self.mover.send(part, part, place.y_peer))

    def finish(self):
        for copy in self.local:
            copy.wait()
        for copy in self.over_y:
            copy.wait_recv()


class GatherColumns:
    def __init__(self, place, mover, own, full):
        self.place, self.mover, self.full = place, mover, full
        self.quarter = own.shape[1] // GROUP
        self.near = pl.ds(0, self.quarter)
        self.far = pl.ds(self.quarter, self.quarter)
        self.over_g = []
        spot = full.at[place.h, place.g, :, self.near]
        for step in (3, 1, 2):
            to = lax.rem(place.g + step, GROUP)
            columns = pl.ds(pl.multiple_of(to * self.quarter, self.quarter), self.quarter)
            self.over_g.append(mover.send(own.at[:, columns], spot, place.g_peer(step)))
        columns = pl.ds(pl.multiple_of(place.g * self.quarter, self.quarter), self.quarter)
        self.local = mover.local(own.at[:, columns], spot)

    def forward_g(self):
        place = self.place
        self.local.wait()
        for copy in self.over_g:
            copy.wait_recv()
        near = self.full.at[place.h, :, :, self.near]
        far = self.full.at[place.h, :, :, self.far]
        self.over_h = [
            self.mover.send(near, near, place.h_peer(step)) for step in range(1, place.high)
        ]
        self.over_x = [self.mover.send(near, far, place.x_peer)]

    def forward_high(self):
        place = self.place
        for step, copy in enumerate(self.over_h, 1):
            copy.wait_recv()
            high = place.h_from(step)
            self.over_x.append(
                self.mover.send(
                    self.full.at[high, :, :, self.near],
                    self.full.at[high, :, :, self.far],
                    place.x_peer,
                )
            )

    def finish(self):
        for copy in self.over_x:
            copy.wait_recv()


def lane_swap(values):
    half = values.shape[-1] // 2
    return jnp.concatenate([values[:, half:], values[:, :half]], axis=-1)


def norm_rows(values, gain):
    scale = lax.rsqrt(jnp.mean(values * values, axis=-1, keepdims=True) + NORM_EPS)
    return values * scale * gain


def forward_kernel(sizes, *refs):
    (hidden, keep, send_maps, recv_maps, gain_row, cosine, sine, seg_col, pos_col, seg_row,
     pos_row, out_grad, live, wq, wk, wv, wo, wg, wu, wd) = refs[:20]
    (moved, gains, normed, full_qkv, full_wo, full_g, full_u, full_d, grad_y, lin, rot, attended,
     log_total, resid, full_nm) = refs[20:35]
    (blocks_out, blocks_in, rows_in, normed_own, bias, part_own, from_c, from_x, to_c,
     nm_own, send_sems, recv_sems, local_sems) = refs[35:]
    place = Place(*sizes)
    mover = Mover(send_sems, recv_sems, local_sems)
    tokens, width = hidden.shape
    head = cosine.shape[1]
    query_width, key_width = wq.shape[1], wk.shape[1]
    columns = width // GROUP
    parts = sizes[1]
    repeat = query_width // key_width

    for q in range(GROUP):
        lanes = pl.ds(q * columns, columns)
        piece = jnp.dot(send_maps[q], hidden[:, lanes], preferred_element_type=F32)
        if q == 0:
            total = piece
        else:
            total = total + piece
    blocks_out[...] = total.astype(BF16).reshape(blocks_out.shape)
    greet(dp_peers(place) + [place.x_peer, place.c_peer])
    copies = []
    for step in range(1, place.dp_size):
        other = lax.rem(place.d + step, place.dp_size)
        copies.append(mover.send(blocks_out.at[other], blocks_in.at[place.d], (other, place.s)))
        copies.append(mover.send(gain_row, rows_in.at[place.d], (other, place.s)))
    key_parts = [(wk, query_width, key_width), (wv, query_width + key_width, key_width)]
    attn = [
        GatherDp(place, mover, [(wq, 0, query_width)], full_qkv),
        GatherDp(place, mover, key_parts, full_qkv),
    ]
    mlp = [GatherColumns(place, mover, wg, full_g)]
    attn.append(GatherDp(place, mover, [(wo, 0, wo.shape[1])], full_wo))
    mlp.append(GatherColumns(place, mover, wu, full_u))
    mlp.append(GatherColumns(place, mover, wd, full_d))
    blocks_in[place.d] = blocks_out[place.d]
    rows_in[place.d] = gain_row[...]
    for copy in copies:
        copy.wait_recv()
    all_gains = rows_in[0]
    for index in range(1, place.dp_size):
        all_gains = all_gains + rows_in[index]
    gains[...] = all_gains
    incoming = blocks_in[...].reshape(place.dp_size * 16, columns)
    for q in range(GROUP):
        lanes = pl.ds(q * columns, columns)
        here = jnp.dot(recv_maps[q], incoming, preferred_element_type=F32)
        here = here + jnp.where(keep[...] > 0.0, hidden[:, lanes].astype(F32), 0.0)
        moved[:, lanes] = here.astype(BF16)

    def norm_moved(index, carry):
        rows = pl.ds(pl.multiple_of(index * 32, 32), 32)
        normed_own[rows, :] = norm_rows(moved[rows, :].astype(F32), gains[:, :width]).astype(BF16)
        grad_y[rows, :] = (out_grad[rows, :].astype(F32) * live[rows, :]).astype(BF16)
        return carry

    lax.fori_loop(0, tokens // 32, norm_moved, 0)
    row = GatherSeq(place, mover, normed_own, normed)
    attn[0].forward_high()
    mlp[0].forward_g()
    attn[1].forward_high()
    attn[0].forward_l()
    row.forward()
    attn[1].forward_l()
    mlp[1].forward_g()
    attn[2].forward_high()
    mlp[2].forward_g()
    attn[2].forward_l()
    row.finish()
    attn[0].finish()
    attn[1].finish()

    gain_query = gains[:, 2 * width : 2 * width + head]
    gain_key = gains[:, 2 * width + head : 2 * width + 2 * head]
    rotated = query_width + key_width
    tile = 2 * head

    def project(part, carry):
        spots = pl.ds(pl.multiple_of(part * tokens, tokens), tokens)
        source = normed[part]
        cos_part, sin_part = cosine[spots, :], sine[spots, :]
        for start in range(0, rotated + key_width, tile):
            result = jnp.dot(source, full_qkv[:, start : start + tile], preferred_element_type=F32)
            if start < rotated:
                lin[spots, start : start + tile] = result.astype(BF16)
                gain = gain_query if start < query_width else gain_key
                for inner in (0, head):
                    unit = norm_rows(result[:, inner : inner + head], gain)
                    turned = unit * cos_part + lane_swap(unit) * sin_part
                    rot[spots, start + inner : start + inner + head] = turned.astype(BF16)
            else:
                rot[spots, start : start + tile] = result.astype(BF16)
        return carry

    lax.fori_loop(0, parts, project, 0)
    mlp[0].forward_high()
    scale = head ** (-0.5)
    for part in range(parts):
        keys = (part + 1) * tokens
        spots = pl.ds(part * tokens, tokens)
        allowed = (seg_col[spots, :] == seg_row[:, :keys]) & (pos_row[:, :keys] <= pos_col[spots, :])
        some = jnp.where(allowed, 0.0, MASKED)
        for copy in range(repeat):
            bias[copy * tokens : (copy + 1) * tokens, :keys] = some

        def attend(pair, carry):
            key_lanes = pl.ds(pl.multiple_of(query_width + pair * head, head), head)
            value_lanes = pl.ds(pl.multiple_of(rotated + pair * head, head), head)
            query_lanes = [
                pl.ds(pl.multiple_of((pair * repeat + copy) * head, head), head)
                for copy in range(repeat)
            ]
            queries = jnp.concatenate([rot[spots, lanes] for lanes in query_lanes], axis=0)
            scores = product(queries, rot[:keys, key_lanes], CONTRACT_COLS) * scale
            scores = scores + bias[:, :keys]
            peak = jnp.max(scores, axis=-1, keepdims=True)
            expd = jnp.exp(scores - peak)
            weight = jnp.sum(expd, axis=-1, keepdims=True)
            probs = (expd / weight).astype(BF16)
            log_total[pair, part] = peak + jnp.log(weight)
            context = jnp.dot(probs, rot[:keys, value_lanes], preferred_element_type=F32)
            for copy in range(repeat):
                attended[spots, query_lanes[copy]] = context[
                    copy * tokens : (copy + 1) * tokens
                ].astype(BF16)
            return carry

        lax.fori_loop(0, key_width // head, attend, 0)
    mlp[1].forward_high()
    attn[2].finish()

    def project_out(part, target):
        source = attended[pl.ds(pl.multiple_of(part * tokens, tokens), tokens), :]

        def step(index, carry):
            block = pl.ds(pl.multiple_of(index * 256, 256), 256)
            target[:, block] = product(source, full_wo[block, :], CONTRACT_COLS).astype(BF16)
            return carry

        lax.fori_loop(0, width // 256, step, 0)

    cores = place.cores
    places = ((1 - place.x) * cores, place.x * cores)
    project_out(places[0] + 1 - place.c, to_c.at[0])
    over_c = [mover.send(to_c.at[0], from_c.at[0], place.c_peer)]
    project_out(places[0] + place.c, part_own.at[0])
    over_c[0].wait_recv()
    add_rows(part_own.at[0], [part_own.at[0], from_c.at[0]], tokens, 32)
    over_x = mover.send(part_own.at[0], from_x, place.x_peer)
    project_out(places[1] + 1 - place.c, to_c.at[1])
    over_c.append(mover.send(to_c.at[1], from_c.at[1], place.c_peer))
    project_out(places[1] + place.c, part_own.at[1])
    mlp[2].forward_high()
    over_c[1].wait_recv()
    over_x.wait_recv()

    def norm_resid(index, carry):
        rows = pl.ds(pl.multiple_of(index * 32, 32), 32)
        total = moved[rows, :].astype(F32) + part_own[1, rows, :].astype(F32)
        total = total + from_c[1, rows, :].astype(F32) + from_x[rows, :].astype(F32)
        resid[rows, :] = total
        nm_own[rows, :] = norm_rows(total, gains[:, width : 2 * width]).astype(BF16)
        return carry

    lax.fori_loop(0, tokens // 32, norm_resid, 0)
    group = GatherGroup(place, mover, nm_own, full_nm)
    group.forward()
    group.finish_ici()
    for part in [group] + mlp:
        part.finish()
    mover.finish()


def forward(sizes, collective_id, head_size, args):
    dp_size, seq_size = sizes
    hidden, wq, wk, wo, wg = args[0], args[13], args[14], args[16], args[17]
    tokens, width = hidden.shape
    high = dp_size // GROUP
    rows = wq.shape[0]
    row_len = seq_size * tokens
    rotated = wq.shape[1] + wk.shape[1]
    wide = (high, GROUP, rows, wg.shape[1] // 2)
    group = (GROUP, seq_size // 2, tokens, width)
    heads = wq.shape[1] // head_size
    gain_width = args[4].shape[1]
    outs = [
        ((tokens, width), BF16, VMEM),
        ((1, gain_width), F32, VMEM),
        ((seq_size, tokens, width), BF16, VMEM),
        ((width, rotated + wk.shape[1]), BF16, VMEM),
        ((width, wo.shape[1]), BF16, VMEM),
        (wide, BF16, HBM),
        (wide, BF16, HBM),
        (wide, BF16, HBM),
        ((tokens, width), BF16, VMEM),
        ((row_len, rotated), BF16, VMEM),
        ((row_len, rotated + wk.shape[1]), BF16, VMEM),
        ((row_len, wq.shape[1]), BF16, VMEM),
        ((wk.shape[1] // head_size, seq_size, heads * head_size // wk.shape[1] * tokens, 1), F32, VMEM),
        ((tokens, width), F32, VMEM),
        (group, BF16, HBM),
    ]
    scratch = [
        pltpu.VMEM((dp_size, 16, width // GROUP), BF16),
        pltpu.VMEM((dp_size, 16, width // GROUP), BF16),
        pltpu.VMEM((dp_size, 1, gain_width), F32),
        pltpu.VMEM((tokens, width), BF16),
        pltpu.VMEM((wq.shape[1] // wk.shape[1] * tokens, row_len), F32),
        pltpu.VMEM((2, tokens, width), BF16),
        pltpu.VMEM((2, tokens, width), BF16),
        pltpu.VMEM((tokens, width), BF16),
        pltpu.VMEM((2, tokens, width), BF16),
        pltpu.VMEM((tokens, width), BF16),
    ]
    sends = 2 * (dp_size - 1) + 4 * (high + 1) + 9 * high
    sends += 3 * (3 + 2 * high) + 2 * GatherGroup.sends + GatherSeq.sends + 3
    return pl.pallas_call(
        functools.partial(forward_kernel, sizes),
        out_shape=[jax.ShapeDtypeStruct(shape, dtype) for shape, dtype, _ in outs],
        in_specs=[VMEM] * 13 + [HBM] * 7,
        out_specs=[spec for _, _, spec in outs],
        scratch_shapes=scratch + sems(sends, 16),
        compiler_params=comm_params(collective_id),
        name="forward_attention",
    )(*args)


class ScatterColumns:
    sends = GROUP
    pieces = 4

    @staticmethod
    def scratch(high, rows, quarter):
        group_rows = GROUP * rows
        return [
            pltpu.VMEM((high * group_rows, quarter), BF16),
            pltpu.VMEM((max(high - 1, 1), group_rows, quarter), BF16),
            pltpu.VMEM((GROUP - 1, rows, quarter), BF16),
        ]

    def __init__(self, place, mover, parts, from_x, from_h, from_g):
        self.place, self.mover, self.parts = place, mover, parts
        self.from_x, self.from_h, self.from_g = from_x, from_h, from_g
        self.group_rows = from_h.shape[1]
        self.quarter = from_x.shape[1]

    def start(self):
        quarter = self.quarter
        far = self.parts.at[:, pl.ds(quarter, quarter)]
        self.over_x = self.mover.send(far, self.from_x, self.place.x_peer)

    def forward_x(self, stage):
        place, mover, total = self.place, self.mover, self.from_x
        rows = total.shape[0] // self.pieces
        near = pl.ds(0, self.quarter)

        def load(index):
            block = pl.ds(index * rows, rows)
            return mover.local(self.parts.at[block, near], stage.at[index % 2])

        copies = [load(0)]
        self.over_x.wait_recv()
        for index in range(self.pieces):
            if index + 1 < self.pieces:
                copies.append(load(index + 1))
            copies[index].wait()
            part = total.at[pl.ds(index * rows, rows)]
            add_rows(part, [part, stage.at[index % 2]], rows, 64)
        self.over_h = []
        for step in range(1, place.high):
            high = lax.rem(place.h + step, place.high)
            block = pl.ds(pl.multiple_of(high * self.group_rows, self.group_rows), self.group_rows)
            self.over_h.append(
                mover.send(total.at[block], self.from_h.at[step - 1], place.h_peer(step))
            )

    def block(self, index):
        rows = self.group_rows // GROUP
        return pl.ds(
            pl.multiple_of(self.place.h * self.group_rows + index * rows, rows), rows
        )

    def forward_high(self):
        place = self.place
        own_rows = pl.ds(
            pl.multiple_of(place.h * self.group_rows, self.group_rows), self.group_rows
        )
        for copy in self.over_h:
            copy.wait_recv()
        mine = self.from_x.at[own_rows]
        terms = [mine] + [self.from_h.at[step] for step in range(place.high - 1)]
        add_rows(mine, terms, self.group_rows, 64)
        self.over_g = []
        for step in (3, 1, 2):
            block = self.block(lax.rem(place.g + step, GROUP))
            self.over_g.append(
                (
                    step,
                    self.mover.send(
                        self.from_x.at[block], self.from_g.at[step - 1], place.g_peer(step)
                    ),
                )
            )

    def finish(self, stage, out):
        place, quarter = self.place, self.quarter
        columns = pl.ds(pl.multiple_of(place.g * quarter, quarter), quarter)
        stage[:, columns] = self.from_x[self.block(place.g), :].astype(F32)
        for step, copy in self.over_g:
            copy.wait_recv()
            source = lax.rem(place.g + GROUP - step, GROUP)
            columns = pl.ds(pl.multiple_of(source * quarter, quarter), quarter)
            stage[:, columns] = self.from_g[step - 1].astype(F32)
        self.mover.local(stage, out).wait()


class ScatterDp:
    @staticmethod
    def sends(high):
        return 2 * high + high + high - 1

    @staticmethod
    def scratch(high, rows, width):
        return [
            pltpu.VMEM((2, high, rows, width), BF16),
            pltpu.VMEM((high, rows, width), BF16),
            pltpu.VMEM((max(high - 1, 1), rows, width), BF16),
        ]

    def __init__(self, place, mover, parts, out, from_y, from_l, from_h):
        self.place, self.mover, self.parts, self.out = place, mover, parts, out
        self.from_y, self.from_l, self.from_h = from_y, from_l, from_h
        self.rows = out.shape[0]

    def block(self, high, l_index, y_index):
        index = high * GROUP + l_index * 2 + y_index
        return self.parts.at[pl.ds(pl.multiple_of(index * self.rows, self.rows), self.rows)]

    def start(self):
        place = self.place
        self.owners = (1 - place.l, place.l)
        self.over_y = []
        for index, l_owner in enumerate(self.owners):
            for high in range(place.high):
                source = self.block(high, l_owner, 1 - place.y)
                self.over_y.append(
                    self.mover.send(source, self.from_y.at[index, high], place.y_peer)
                )

    def ready(self, index, extra=None):
        place = self.place
        for high in range(place.high):
            self.over_y[index * place.high + high].wait_recv()
            mine = self.block(high, self.owners[index], place.y)
            terms = [mine, self.from_y.at[index, high]]
            if extra is not None:
                extra[high].wait_recv()
                terms.append(self.from_l.at[high])
            add_rows(mine, terms, self.rows, 32)

    def forward_y(self):
        place = self.place
        self.ready(0)
        self.over_l = []
        for high in range(place.high):
            source = self.block(high, 1 - place.l, place.y)
            self.over_l.append(self.mover.send(source, self.from_l.at[high], place.l_peer))

    def forward_l(self):
        place = self.place
        self.ready(1, self.over_l)
        self.over_h = []
        for step in range(1, place.high):
            source = self.block(lax.rem(place.h + step, place.high), place.l, place.y)
            self.over_h.append(
                self.mover.send(source, self.from_h.at[step - 1], place.h_peer(step))
            )

    def finish(self):
        place = self.place
        for copy in self.over_h:
            copy.wait_recv()
        terms = [self.block(place.h, place.l, place.y)]
        terms += [self.from_h.at[step] for step in range(place.high - 1)]
        add_rows(self.out, terms, self.rows, 32)


class ScatterGroup:
    sends = 10

    @staticmethod
    def scratch(rows, width):
        return [
            pltpu.VMEM((GROUP, rows, width), BF16),
            pltpu.VMEM((6, rows // 2, width), BF16),
        ]

    def __init__(self, place, mover, parts, from_c, landed):
        self.place, self.mover, self.parts = place, mover, parts
        self.from_c, self.landed = from_c, landed
        self.owners = (place.gd, place.gy, place.gl, place.g)
        self.over_c = []
        half = from_c.shape[1] // 2
        self.low, self.top = pl.ds(0, half), pl.ds(half, half)

    def start(self, index):
        place = self.place
        source = self.parts.at[self.owners[index], 1 - place.c]
        self.over_c.append(self.mover.send(source, self.from_c.at[index], place.c_peer))

    def forward(self, index):
        place, mover, sums, landed = self.place, self.mover, self.from_c, self.landed
        low, top = self.low, self.top
        self.over_c[index].wait_recv()
        total = sums.at[index]
        own = self.parts.at[self.owners[index], place.c]
        add_rows(total, [total, own], total.shape[0], 32)
        if index == 0:
            self.y_diag = mover.send(sums.at[0, low], landed.at[0], place.y_peer)
            self.l_diag = mover.send(sums.at[0, top], landed.at[1], place.l_peer)
        if index == 1:
            self.y_own = mover.send(sums.at[1, low], landed.at[2], place.y_peer)
        if index == 2:
            self.l_own = mover.send(sums.at[2, top], landed.at[3], place.l_peer)

    def forward_diag(self):
        place, mover, sums, landed = self.place, self.mover, self.from_c, self.landed
        half = sums.shape[1] // 2
        low, top = self.low, self.top
        self.y_diag.wait_recv()
        add_rows(sums.at[2, low], [sums.at[2, low], landed.at[0]], half, 32)
        self.l_last = mover.send(sums.at[2, low], landed.at[4], place.l_peer)
        self.l_diag.wait_recv()
        add_rows(sums.at[1, top], [sums.at[1, top], landed.at[1]], half, 32)
        self.y_last = mover.send(sums.at[1, top], landed.at[5], place.y_peer)

    def finish(self, take):
        half = self.from_c.shape[1] // 2
        chunk = 32
        self.y_own.wait_recv()
        self.l_last.wait_recv()
        self.l_own.wait_recv()
        self.y_last.wait_recv()
        for base, first, second in ((0, 2, 4), (half, 3, 5)):

            def step(index, carry):
                rows = pl.ds(pl.multiple_of(base + index * chunk, chunk), chunk)
                inner = pl.ds(pl.multiple_of(index * chunk, chunk), chunk)
                total = self.from_c[3, rows, :].astype(F32)
                total = total + self.landed[first, inner, :].astype(F32)
                take(rows, total + self.landed[second, inner, :].astype(F32))
                return carry

            lax.fori_loop(0, half // chunk, step, 0)


def norm_back(values, gain, cotangent):
    scale = lax.rsqrt(jnp.mean(values * values, axis=-1, keepdims=True) + NORM_EPS)
    weighted = cotangent * gain
    inner = jnp.mean(weighted * values, axis=-1, keepdims=True)
    unit = values * scale
    return scale * (weighted - unit * (scale * inner)), cotangent * unit


def feed_forward_kernel(sizes, *refs):
    nm_hbm, wg_hbm, wu_hbm, wd_hbm, grad_y, resid, live, gains = refs[:8]
    mixed, grad_resid, full_proj, gain_sum, out_gd, out_gg, out_gu = refs[8:15]
    (nm, gy, wg, wu, wd, hidden, gate_grad, up_grad, part_nmlp, part_down, nmlp_c, nmlp_landed,
     down_c, down_landed, grad_proj, stage) = refs[15:31]
    send_sems, recv_sems, local_sems = refs[31:]
    place = Place(*sizes)
    mover = Mover(send_sems, recv_sems, local_sems)
    tokens, width = resid.shape
    cores = place.cores
    block = cores * tokens
    inner = wg.shape[1]
    tile = 256
    loads = [mover.local(wg_hbm, wg), mover.local(wu_hbm, wu)]
    nm_loads = [mover.local(nm_hbm.at[index], nm.at[index]) for index in range(GROUP)]
    wd_load = mover.local(wd_hbm, wd)
    greet([place.y_peer, place.l_peer, place.c_peer, place.x_peer])
    gather = GatherGroup(place, mover, grad_y, gy)
    gain_sum[...] = jnp.zeros_like(gain_sum)
    for copy in loads:
        copy.wait()

    def gate_up(index, carry):
        source = nm[index].reshape(block, width)
        rows = pl.ds(pl.multiple_of(index * block, block), block)
        for start in range(0, inner, tile):
            lanes = slice(start, start + tile)
            gate = jnp.dot(source, wg[:, lanes], preferred_element_type=F32)
            upper = jnp.dot(source, wu[:, lanes], preferred_element_type=F32)
            gain = 1.0 / (1.0 + jnp.exp(-gate))
            silu = gate * gain
            hidden[rows, lanes] = (silu * upper).astype(BF16)
            up_grad[rows, lanes] = silu.astype(BF16)
            gate_grad[rows, lanes] = (upper * (gain + silu * (1.0 - gain))).astype(BF16)
        return carry

    nm_loads[0].wait()
    nm_loads[1].wait()
    lax.fori_loop(0, 2, gate_up, 0)
    gather.forward()
    nm_loads[2].wait()
    nm_loads[3].wait()
    lax.fori_loop(2, GROUP, gate_up, 0)
    gather.finish_ici()
    wd_load.wait()

    def down_block(owner):
        rows = pl.ds(pl.multiple_of(owner * block, block), block)

        def step(index, carry):
            lanes = pl.ds(pl.multiple_of(index * tile, tile), tile)
            result = product(hidden[rows, :], wd[lanes, :], CONTRACT_COLS).astype(BF16)
            part_down[owner, :, :, lanes] = result.reshape(cores, tokens, tile)
            return carry

        lax.fori_loop(0, width // tile, step, 0)

    down = ScatterGroup(place, mover, part_down, down_c, down_landed)
    down_block(down.owners[0])
    down_block(down.owners[1])
    gather.finish()

    def back_block(owner):
        rows = pl.ds(pl.multiple_of(owner * block, block), block)
        source = gy[owner].reshape(block, width)
        for start in range(0, inner, tile):
            lanes = slice(start, start + tile)
            grad_mid = jnp.dot(source, wd[:, lanes], preferred_element_type=F32)
            gate_grad[rows, lanes] = (grad_mid * gate_grad[rows, lanes].astype(F32)).astype(BF16)
            up_grad[rows, lanes] = (grad_mid * up_grad[rows, lanes].astype(F32)).astype(BF16)

        def step(index, carry):
            lanes = pl.ds(pl.multiple_of(index * tile, tile), tile)
            result = product(gate_grad[rows, :], wg[lanes, :], CONTRACT_COLS)
            result = result + product(up_grad[rows, :], wu[lanes, :], CONTRACT_COLS)
            part_nmlp[owner, :, :, lanes] = result.astype(BF16).reshape(cores, tokens, tile)
            return carry

        lax.fori_loop(0, width // tile, step, 0)

    nmlp = ScatterGroup(place, mover, part_nmlp, nmlp_c, nmlp_landed)
    back_block(nmlp.owners[0])
    nmlp.start(0)
    back_block(nmlp.owners[1])
    nmlp.start(1)
    nmlp.forward(0)
    back_block(nmlp.owners[2])
    nmlp.start(2)
    nmlp.forward(1)
    back_block(nmlp.owners[3])
    nmlp.start(3)
    nmlp.forward(2)
    down_block(down.owners[2])
    nmlp.forward(3)
    nmlp.forward_diag()
    down_block(down.owners[3])
    for index in range(GROUP):
        down.start(index)

    def weight_grad(grad, source, target):
        copies = []
        tiles = width // tile
        for index in range(tiles):
            lanes = pl.ds(index * tile, tile)
            left = source[:, :, :, lanes].reshape(GROUP * block, tile)
            if index >= 2:
                copies[index - 2].wait()
            stage[index % 2] = product(left, grad[...], CONTRACT_ROWS).astype(BF16)
            copies.append(mover.local(stage.at[index % 2], target.at[lanes]))
        copies[-2].wait()
        copies[-1].wait()

    def back_mlp(rows, total):
        grad, terms = norm_back(resid[rows, :], gains[:, width : 2 * width], total)
        grad = grad + grad_y[rows, :].astype(F32)
        grad_resid[rows, :] = grad
        grad_proj[rows, :] = grad.astype(BF16)
        gain_sum[...] += jnp.sum(terms, axis=0, keepdims=True)

    def mix(rows, total):
        mixed[rows, :] = ((resid[rows, :] + total) * live[rows, :]).astype(BF16)

    weight_grad(hidden, gy, out_gd)
    nmlp.finish(back_mlp)
    row = GatherSeq(place, mover, grad_proj, full_proj)
    for index in range(GROUP):
        down.forward(index)
    weight_grad(gate_grad, nm, out_gg)
    down.forward_diag()
    row.forward()
    weight_grad(up_grad, nm, out_gu)
    down.finish(mix)
    row.finish()
    mover.finish()


def feed_forward(sizes, collective_id, args):
    dp_size, seq_size = sizes
    nm, wg, resid, gains = args[0], args[1], args[5], args[7]
    tokens, width = resid.shape
    inner = wg.shape[1]
    rows = GROUP * (seq_size // 2) * tokens
    outs = [
        ((tokens, width), BF16, VMEM),
        ((tokens, width), F32, VMEM),
        ((seq_size, tokens, width), BF16, HBM),
        ((1, width), F32, VMEM),
        ((width, inner), BF16, HBM),
        ((width, inner), BF16, HBM),
        ((width, inner), BF16, HBM),
    ]
    scratch = [pltpu.VMEM(nm.shape, BF16)] * 2
    scratch += [pltpu.VMEM((width, inner), BF16)] * 3
    scratch += [pltpu.VMEM((rows, inner), BF16)] * 3
    scratch += [pltpu.VMEM(nm.shape, BF16)] * 2
    scratch += ScatterGroup.scratch(tokens, width) * 2
    scratch += [pltpu.VMEM((tokens, width), BF16), pltpu.VMEM((2, 256, inner), BF16)]
    sends = 3 * 10 + GatherSeq.sends
    local = 9 + 3 * (width // 256)
    return pl.pallas_call(
        functools.partial(feed_forward_kernel, sizes),
        out_shape=[jax.ShapeDtypeStruct(shape, dtype) for shape, dtype, _ in outs],
        in_specs=[HBM] * 4 + [VMEM] * 4,
        out_specs=[spec for _, _, spec in outs],
        scratch_shapes=scratch + sems(sends, local),
        compiler_params=comm_params(collective_id, 63 * 1024 * 1024),
        name="feed_forward",
    )(*args)


def backward_kernel(sizes, *refs):
    (part_gd, part_gg, part_gu, wo, grad_resid, full_proj, moved, keep, gain_mlp, gains, cosine,
     sine, seg_col, pos_col, seg_row, pos_row, log_row, normed, full_qkv, lin, rot, attended,
     recv_maps_t, send_maps_t) = refs[:24]
    grad_hidden, gain_sums, out_gd, out_gg, out_gu, out_qkv, out_wo = refs[24:31]
    send_sems, recv_sems, local_sems = refs[-3:]
    scratch = list(refs[31:-3])

    def take(count):
        taken = scratch[:count]
        del scratch[:count]
        return taken

    place = Place(*sizes)
    mover = Mover(send_sems, recv_sems, local_sems)
    tokens, width = moved.shape
    parts = sizes[1]
    head = cosine.shape[1]
    query_width = attended.shape[1]
    key_width = (rot.shape[1] - query_width) // 2
    rotated = query_width + key_width
    columns = width // GROUP
    repeat = query_width // key_width
    column_stage, out_stage = take(2)
    grad_wo, grad_key, grad_query = take(3)
    mlp = [
        ScatterColumns(place, mover, part, *take(3)) for part in (part_gd, part_gg, part_gu)
    ]
    wo_sum = ScatterDp(place, mover, grad_wo, out_wo, *take(3))
    key_sum = ScatterDp(place, mover, grad_key, out_qkv.at[:, pl.ds(query_width, 2 * key_width)], *take(3))
    query_sum = ScatterDp(place, mover, grad_query, out_qkv.at[:, pl.ds(0, query_width)], *take(3))
    grad_moved, to_c, from_c, from_x = take(4)
    grad_att, grad_keys, grad_values, grad_lin, bias = take(5)
    blocks_out, blocks_in, rows_in, row_c, row_x = take(5)

    greet(dp_peers(place) + [place.x_peer, place.c_peer])
    for part in mlp:
        part.start()
    gain_sums[...] = jnp.zeros_like(gain_sums)
    gain_sums[:, width : 2 * width] = gain_mlp[...]
    grad_keys[...] = jnp.zeros_like(grad_keys)
    grad_values[...] = jnp.zeros_like(grad_values)

    def attended_grad(part, carry):
        spots = pl.ds(pl.multiple_of(part * tokens, tokens), tokens)
        for start in range(0, query_width, 256):
            result = jnp.dot(full_proj[part], wo[:, start : start + 256], preferred_element_type=F32)
            grad_att[spots, start : start + 256] = result.astype(BF16)
        return carry

    lax.fori_loop(0, parts, attended_grad, 0)

    def out_weight_grad(index, carry):
        lanes = pl.ds(pl.multiple_of(index * 256, 256), 256)
        source = full_proj[:, :, lanes].reshape(parts * tokens, 256)
        grad_wo[lanes, :] = product(source, attended[...], CONTRACT_ROWS).astype(BF16)
        return carry

    lax.fori_loop(0, width // 256, out_weight_grad, 0)
    wo_sum.start()

    scale = head ** (-0.5)
    gain_query = gains[:, 2 * width : 2 * width + head]
    gain_key = gains[:, 2 * width + head : 2 * width + 2 * head]

    def unrotate(spots, lanes, grad, gain, gain_lanes):
        turned = grad * cosine[spots, :] - lane_swap(grad) * sine[spots, :]
        values, terms = norm_back(lin[spots, lanes].astype(F32), gain, turned)
        grad_lin[spots, lanes] = values.astype(BF16)
        gain_sums[:, gain_lanes] += jnp.sum(terms, axis=0, keepdims=True)

    for part in range(parts):
        keys = (part + 1) * tokens
        spots = pl.ds(part * tokens, tokens)
        allowed = (seg_col[:keys, :] == seg_row[:, spots]) & (pos_col[:keys, :] <= pos_row[:, spots])
        some = jnp.where(allowed, 0.0, MASKED)
        for copy in range(repeat):
            bias[:keys, copy * tokens : (copy + 1) * tokens] = some

        def attend(pair, carry):
            key_lanes = pl.ds(pl.multiple_of(query_width + pair * head, head), head)
            value_lanes = pl.ds(pl.multiple_of(rotated + pair * head, head), head)
            own_lanes = pl.ds(pl.multiple_of(pair * head, head), head)
            query_lanes = [
                pl.ds(pl.multiple_of((pair * repeat + copy) * head, head), head)
                for copy in range(repeat)
            ]
            queries = jnp.concatenate([rot[spots, lanes] for lanes in query_lanes], axis=0)
            grads = jnp.concatenate([grad_att[spots, lanes] for lanes in query_lanes], axis=0)
            key_rows, value_rows = rot[:keys, key_lanes], rot[:keys, value_lanes]
            scores = product(key_rows, queries, CONTRACT_COLS) * scale + bias[:keys, :]
            probs = jnp.exp(scores - log_row[pair, part])
            grad_values[:keys, own_lanes] += jnp.dot(
                probs.astype(BF16), grads, preferred_element_type=F32
            )
            grad_probs = product(value_rows, grads, CONTRACT_COLS)
            spread = jnp.sum(probs * grad_probs, axis=0, keepdims=True)
            grad_scores = (probs * (grad_probs - spread)).astype(BF16)
            grad_keys[:keys, own_lanes] += jnp.dot(
                grad_scores, queries, preferred_element_type=F32
            )
            grad_queries = product(grad_scores, key_rows, CONTRACT_ROWS) * scale
            for copy in range(repeat):
                unrotate(
                    spots,
                    query_lanes[copy],
                    grad_queries[copy * tokens : (copy + 1) * tokens],
                    gain_query,
                    pl.ds(2 * width, head),
                )
            return carry

        lax.fori_loop(0, key_width // head, attend, 0)
        if part == parts - 2:
            mlp[0].forward_x(column_stage)
            wo_sum.forward_y()
    for pair in range(key_width // head):

        def back_keys(part, carry):
            spots = pl.ds(pl.multiple_of(part * tokens, tokens), tokens)
            lanes = pl.ds(pair * head, head)
            unrotate(
                spots,
                pl.ds(query_width + pair * head, head),
                grad_keys[spots, lanes] * scale,
                gain_key,
                pl.ds(2 * width + head, head),
            )
            grad_lin[spots, pl.ds(rotated + pair * head, head)] = grad_values[spots, lanes].astype(
                BF16
            )
            return carry

        lax.fori_loop(0, parts, back_keys, 0)

    def weight_grad(target, start, size):
        def step(index, carry):
            lanes = pl.ds(pl.multiple_of(index * 256, 256), 256)
            source = normed[:, :, lanes].reshape(parts * tokens, 256)
            target[lanes, :] = product(
                source, grad_lin[:, start : start + size], CONTRACT_ROWS
            ).astype(BF16)
            return carry

        lax.fori_loop(0, width // 256, step, 0)

    weight_grad(grad_key, query_width, 2 * key_width)
    key_sum.start()
    weight_grad(grad_query, 0, query_width)
    query_sum.start()

    def normed_grad(part, target):
        source = grad_lin[pl.ds(pl.multiple_of(part * tokens, tokens), tokens), :]

        def step(index, carry):
            block = pl.ds(pl.multiple_of(index * 256, 256), 256)
            target[:, block] = product(source, full_qkv[block, :], CONTRACT_COLS).astype(BF16)
            return carry

        lax.fori_loop(0, width // 256, step, 0)

    cores = place.cores
    places = ((1 - place.x) * cores, place.x * cores)
    normed_grad(places[0] + 1 - place.c, to_c.at[0])
    over_c = [mover.send(to_c.at[0], from_c.at[0], place.c_peer)]
    normed_grad(places[0] + place.c, to_c.at[1])
    over_c[0].wait_recv()
    add_rows(to_c.at[1], [to_c.at[1], from_c.at[0]], tokens, 32)
    over_x = mover.send(to_c.at[1], from_x, place.x_peer)
    normed_grad(places[1] + 1 - place.c, to_c.at[2])
    over_c.append(mover.send(to_c.at[2], from_c.at[1], place.c_peer))
    normed_grad(places[1] + place.c, to_c.at[3])
    mlp[1].forward_x(column_stage)
    mlp[0].forward_high()
    wo_sum.forward_l()
    key_sum.forward_y()
    over_c[1].wait_recv()
    over_x.wait_recv()

    def back_normed(index, carry):
        rows = pl.ds(pl.multiple_of(index * 32, 32), 32)
        total = to_c[3, rows, :].astype(F32) + from_c[1, rows, :].astype(F32)
        total = total + from_x[rows, :].astype(F32)
        grad, terms = norm_back(moved[rows, :].astype(F32), gains[:, :width], total)
        grad_moved[rows, :] = (grad_resid[rows, :] + grad).astype(BF16)
        gain_sums[:, :width] += jnp.sum(terms, axis=0, keepdims=True)
        return carry

    lax.fori_loop(0, tokens // 32, back_normed, 0)
    for q in range(GROUP):
        lanes = pl.ds(q * columns, columns)
        piece = jnp.dot(recv_maps_t[q], grad_moved[:, lanes], preferred_element_type=F32)
        total = piece if q == 0 else total + piece
    blocks_out[...] = total.astype(BF16).reshape(blocks_out.shape)
    copies = []
    for step in range(1, place.dp_size):
        other = lax.rem(place.d + step, place.dp_size)
        copies.append(mover.send(blocks_out.at[other], blocks_in.at[place.d], (other, place.s)))
        copies.append(mover.send(gain_sums, rows_in.at[place.d], (other, place.s)))
    blocks_in[place.d] = blocks_out[place.d]
    rows_in[place.d] = gain_sums[...]
    query_sum.forward_y()
    key_sum.forward_l()
    mlp[2].forward_x(column_stage)
    for copy in copies:
        copy.wait_recv()
    row_total = rows_in[0]
    for index in range(1, place.dp_size):
        row_total = row_total + rows_in[index]
    row_c[0] = row_total
    pass_c = mover.send(row_c.at[0], row_c.at[1], place.c_peer)
    returned = blocks_in[...].reshape(place.dp_size * 16, columns)
    for q in range(GROUP):
        lanes = pl.ds(q * columns, columns)
        here = jnp.dot(send_maps_t[q], returned, preferred_element_type=F32)
        here = here + jnp.where(keep[...] > 0.0, grad_moved[:, lanes].astype(F32), 0.0)
        grad_hidden[:, lanes] = here.astype(BF16)
    query_sum.forward_l()
    pass_c.wait_recv()
    row_x[0] = row_c[0] + row_c[1]
    pass_x = mover.send(row_x.at[0], row_x.at[1], place.x_peer)
    mlp[1].forward_high()
    mlp[2].forward_high()
    mlp[0].finish(out_stage, out_gd)
    wo_sum.finish()
    mlp[1].finish(out_stage, out_gg)
    key_sum.finish()
    query_sum.finish()
    pass_x.wait_recv()
    mlp[2].finish(out_stage, out_gu)
    mover.finish()
    gain_sums[...] = row_x[0] + row_x[1]


def backward(sizes, collective_id, args):
    dp_size, seq_size = sizes
    part_gd, wo, moved, gains = args[0], args[3], args[6], args[9]
    rot, attended = args[20], args[21]
    tokens, width = moved.shape
    high = dp_size // GROUP
    rows = width // dp_size
    quarter = part_gd.shape[1] // 2
    row_len = seq_size * tokens
    query_width = attended.shape[1]
    key_width = (rot.shape[1] - query_width) // 2
    repeat = query_width // key_width
    outs = [
        ((tokens, width), BF16, VMEM),
        (gains.shape, F32, VMEM),
        ((rows, GROUP * quarter), F32, HBM),
        ((rows, GROUP * quarter), F32, HBM),
        ((rows, GROUP * quarter), F32, HBM),
        ((rows, rot.shape[1]), F32, VMEM),
        ((rows, query_width), F32, VMEM),
    ]
    piece = high * GROUP * rows // ScatterColumns.pieces
    scratch = [
        pltpu.VMEM((2, piece, quarter), BF16),
        pltpu.VMEM((rows, GROUP * quarter), F32),
    ]
    scratch += [
        pltpu.VMEM(wo.shape, BF16),
        pltpu.VMEM((width, 2 * key_width), BF16),
        pltpu.VMEM((width, query_width), BF16),
    ]
    for _ in range(3):
        scratch += ScatterColumns.scratch(high, rows, quarter)
    scratch += ScatterDp.scratch(high, rows, query_width)
    scratch += ScatterDp.scratch(high, rows, 2 * key_width)
    scratch += ScatterDp.scratch(high, rows, query_width)
    scratch += [
        pltpu.VMEM((tokens, width), BF16),
        pltpu.VMEM((seq_size, tokens, width), BF16),
        pltpu.VMEM((2, tokens, width), BF16),
        pltpu.VMEM((tokens, width), BF16),
        pltpu.VMEM((row_len, query_width), BF16),
        pltpu.VMEM((row_len, key_width), F32),
        pltpu.VMEM((row_len, key_width), F32),
        pltpu.VMEM((row_len, rot.shape[1]), BF16),
        pltpu.VMEM((row_len, repeat * tokens), F32),
        pltpu.VMEM((dp_size, 16, width // GROUP), BF16),
        pltpu.VMEM((dp_size, 16, width // GROUP), BF16),
        pltpu.VMEM((dp_size,) + gains.shape, F32),
        pltpu.VMEM((2,) + gains.shape, F32),
        pltpu.VMEM((2,) + gains.shape, F32),
    ]
    sends = 3 * (high + 3) + 3 * ScatterDp.sends(high)
    sends += 3 + 2 * (dp_size - 1) + 2
    local = 3 * (ScatterColumns.pieces + 1) + 1
    return pl.pallas_call(
        functools.partial(backward_kernel, sizes),
        out_shape=[jax.ShapeDtypeStruct(shape, dtype) for shape, dtype, _ in outs],
        in_specs=[HBM] * 3 + [VMEM] * 21,
        out_specs=[spec for _, _, spec in outs],
        scratch_shapes=scratch + sems(sends, local),
        compiler_params=comm_params(collective_id, 63 * 1024 * 1024),
        name="backward_attention",
    )(*args)


def per_device(
    sizes,
    hidden_in,
    valid_len,
    doc_lengths,
    doc_perm,
    attn_norm,
    w_query,
    key_weight,
    value_weight,
    w_out,
    query_norm,
    key_norm_gain,
    mlp_norm,
    w_gate,
    w_up,
    w_down,
    out_grad,
):
    shard_len = hidden_in.shape[0]
    model_width = hidden_in.shape[1]
    seq_count = doc_lengths.shape[0]
    row_count = doc_lengths.shape[1]
    shorts = doc_lengths.shape[2]
    row_len = shard_len * seq_count
    cap_len = MAXSHORT
    body_len = shard_len - shorts * cap_len
    my_row = lax.axis_index("dp")
    my_part = lax.axis_index("seq")
    valid_here = valid_len[my_row]
    all_starts, all_kept, all_new, all_dest = jax.vmap(
        lambda lengths_part, perm_part: layout(lengths_part, perm_part, body_len)
    )(doc_lengths, doc_perm)
    part_ids = jnp.arange(seq_count, dtype=jnp.int32)
    seg_parts, pos_parts, long_parts, short_parts = jax.vmap(
        lambda kept_p, new_p, dest_p, part: slot_labels(
            kept_p, new_p, dest_p, part, my_row, valid_here, body_len, shard_len, row_len, row_count
        )
    )(all_kept, all_new, all_dest, part_ids)
    segment = seg_parts.reshape(row_len)
    position = pos_parts.reshape(row_len)
    seg_local = lax.dynamic_index_in_dim(seg_parts, my_part, 0, keepdims=False)
    pos_local = lax.dynamic_index_in_dim(pos_parts, my_part, 0, keepdims=False)
    keep_long = lax.dynamic_index_in_dim(long_parts, my_part, 0, keepdims=False)
    live_local = keep_long | lax.dynamic_index_in_dim(short_parts, my_part, 0, keepdims=False)
    starts = lax.dynamic_index_in_dim(all_starts, my_part, 0, keepdims=False)
    kept_flat = lax.dynamic_index_in_dim(all_kept, my_part, 0, keepdims=False)
    new_start = lax.dynamic_index_in_dim(all_new, my_part, 0, keepdims=False)
    dest_row = lax.dynamic_index_in_dim(all_dest, my_part, 0, keepdims=False)
    row_ids = jnp.arange(row_count, dtype=jnp.int32)
    local_slots = jnp.arange(shard_len, dtype=jnp.int32)
    cap_ids = jnp.arange(cap_len, dtype=jnp.int32)
    my_dest = lax.dynamic_slice_in_dim(dest_row, my_row * shorts, shorts)
    my_starts = lax.dynamic_slice_in_dim(starts, my_row * shorts, shorts)
    my_kept = lax.dynamic_slice_in_dim(kept_flat, my_row * shorts, shorts)
    going = my_dest[None, :] == row_ids[:, None]
    send_start = jnp.sum(jnp.where(going, my_starts[None, :], 0), axis=1)
    send_len = jnp.sum(jnp.where(going, my_kept[None, :], 0), axis=1)
    send_map = (
        (
            (cap_ids[None, :, None] < send_len[:, None, None])
            & (local_slots[None, None, :] == send_start[:, None, None] + cap_ids[None, :, None])
        )
        .reshape(row_count * cap_len, shard_len)
        .astype(jnp.bfloat16)
    )
    coming = (dest_row == my_row).reshape(row_count, shorts)
    recv_start = jnp.sum(jnp.where(coming, new_start.reshape(row_count, shorts), 0), axis=1)
    recv_len = jnp.sum(jnp.where(coming, kept_flat.reshape(row_count, shorts), 0), axis=1)
    recv_map = (
        (
            (cap_ids[None, None, :] < recv_len[None, :, None])
            & (local_slots[:, None, None] == recv_start[None, :, None] + cap_ids[None, None, :])
        )
        .reshape(shard_len, row_count * cap_len)
        .astype(jnp.bfloat16)
    )
    same_piece = jnp.eye(GROUP, dtype=BF16)

    def spread(piece, total):
        return lax.dynamic_update_slice(
            jnp.zeros((total,), F32), piece.astype(F32), (my_row * piece.shape[0],)
        )

    head_size = query_norm.shape[0] * row_count
    gain_row = jnp.concatenate(
        [
            spread(attn_norm, model_width),
            spread(mlp_norm, model_width),
            spread(query_norm, head_size),
            spread(key_norm_gain, head_size),
        ]
    )[None, :]
    send_maps = (same_piece[:, None, :, None] * send_map[None, :, None, :]).reshape(
        GROUP, -1, shard_len
    )
    recv_maps = (recv_map[None, :, :, None] * same_piece[:, None, None, :]).reshape(
        GROUP, shard_len, -1
    )
    half_width = head_size // 2
    freq_index = jnp.arange(half_width, dtype=F32)
    inverse = jnp.exp(freq_index * (-2.0 * math.log(ROPE_BASE) / head_size))
    angles = position.astype(F32)[:, None] * inverse[None, :]
    cosine = jnp.concatenate([jnp.cos(angles)] * 2, axis=1)
    sine = jnp.concatenate([-jnp.sin(angles), jnp.sin(angles)], axis=1)
    live_scale = live_local.astype(F32)[:, None]
    keep_scale = keep_long.astype(F32)[:, None]
    (
        moved_low,
        gains,
        normed,
        qkv_mat,
        out_mat,
        gate_mat,
        up_mat,
        down_mat,
        grad_y_own,
        rotated_lin,
        rotated_all,
        attended,
        log_total,
        resid_rows,
        normed_mlp,
    ) = forward(
        sizes,
        1,
        head_size,
        (
            hidden_in,
            keep_scale,
            send_maps,
            recv_maps,
            gain_row,
            cosine,
            sine,
            segment[:, None],
            position[:, None],
            segment[None, :],
            position[None, :],
            out_grad,
            live_scale,
            w_query,
            key_weight,
            value_weight,
            w_out.T,
            w_gate,
            w_up,
            w_down.T,
        ),
    )
    cuts = (model_width, 2 * model_width, 2 * model_width + head_size)
    gate_mat = gate_mat.reshape(model_width, -1)
    up_mat = up_mat.reshape(model_width, -1)
    down_mat = down_mat.reshape(model_width, -1)
    query_width = w_query.shape[1]
    key_width = key_weight.shape[1]
    qkv_cuts = (query_width, query_width + key_width)
    mixed, grad_resid, grad_proj, gain_mlp_sum, grad_down, grad_gate, grad_up = feed_forward(
        sizes,
        2,
        (normed_mlp, gate_mat, up_mat, down_mat, grad_y_own, resid_rows, live_scale, gains),
    )
    grad_hidden, gain_sums, out_down, out_gate, out_up, out_qkv, out_wo = backward(
        sizes,
        3,
        (
            grad_down,
            grad_gate,
            grad_up,
            out_mat,
            grad_resid,
            grad_proj,
            moved_low,
            keep_scale,
            gain_mlp_sum,
            gains,
            cosine,
            sine,
            segment[:, None],
            position[:, None],
            segment[None, :],
            position[None, :],
            jnp.swapaxes(log_total, 2, 3),
            normed,
            qkv_mat,
            rotated_lin,
            rotated_all,
            attended,
            jnp.swapaxes(recv_maps, 1, 2),
            jnp.swapaxes(send_maps, 1, 2),
        ),
    )
    out_query, out_key, out_value = jnp.split(out_qkv, qkv_cuts, axis=1)
    device = my_row * seq_count + my_part

    def own_piece(vector):
        size = vector.shape[0] // (row_count * seq_count)
        return lax.dynamic_slice_in_dim(vector, device * size, size)

    sum_attn, sum_mlp, sum_query, sum_key = [own_piece(v) for v in jnp.split(gain_sums[0], cuts)]
    return (
        mixed,
        grad_hidden,
        sum_attn,
        out_query,
        out_key,
        out_value,
        out_wo.T,
        sum_query,
        sum_key,
        sum_mlp,
        out_gate,
        out_up,
        out_down.T,
    )


def solution(mesh):
    in_specs = (
        P(("dp", "seq"), None),
        P(),
        P(),
        P(),
        P("dp"),
        P("dp", "seq"),
        P("dp", "seq"),
        P("dp", "seq"),
        P("seq", "dp"),
        P("dp"),
        P("dp"),
        P("dp"),
        P("dp", "seq"),
        P("dp", "seq"),
        P("seq", "dp"),
        P(("dp", "seq"), None),
    )
    out_specs = (
        P(("dp", "seq"), None),
        P(("dp", "seq"), None),
        P(("dp", "seq")),
        P("dp", "seq"),
        P("dp", "seq"),
        P("dp", "seq"),
        P("seq", "dp"),
        P(("dp", "seq")),
        P(("dp", "seq")),
        P(("dp", "seq")),
        P("dp", "seq"),
        P("dp", "seq"),
        P("seq", "dp"),
    )
    return jax.shard_map(
        functools.partial(per_device, (mesh.shape["dp"], mesh.shape["seq"])), mesh=mesh, in_specs=in_specs, out_specs=out_specs, check_vma=False
    )
```

time: 850 us -> 589 us (0.69)
  matrix products: 129 us -> 0 us
  other arithmetic: 71.4 us -> 20.3 us
  blocking collectives: 41.6 us -> 0 us
  local copies, waits for them, and re-layouts: 58.9 us -> 26.6 us
    dot_general x25 -> x0, matrix products: 129 us -> none  [the longest x12 67.4 us: product(): lax.dot_general(left, right, dims, preferred_element_type=jnp.float32)]
    psum x1 -> x0, blocking collectives: 41.6 us -> none  [per_device(): lax.psum(jnp.concatenate([grad_gain_attn, grad_gain_mlp, grad_gain_query,...]
    convert_element_type x9 -> x4, other arithmetic: 25.7 us -> 0.82 us  [the longest x1 0.66 us: per_device(): angles = position.astype(F32)[:, None] * inverse[None, :]]
    reduce_sum x9 -> x0, other arithmetic: 17.2 us -> none  [the longest x4 8.72 us: root_mean_norm(): values * lax.rsqrt(jnp.mean(values * values, axis=-1, keepdims=True) + NO...]
    unnamed x197 -> x20, local copies, waits for them, and re-layouts: 21.1 us -> 10.8 us
    reshape x7 -> x0, local copies, waits for them, and re-layouts: 9.1 us -> none  [the longest x2 4.75 us: head_prep(): flat.reshape(flat.shape[0], -1, gain.shape[0])]
    pallas_call x9 -> x3, Pallas kernels: 536 us -> 532 us  [the longest x1 227 us: forward(): pl.pallas_call(functools.partial(forward_kernel, sizes), out_shape=[jax.S...]
where the time goes in v2:
time: 589 us; the launch traced here: 580 us
  Pallas kernels  532 us (90%)
  local copies, waits for them, and re-layouts  26.6 us (5%)
  other arithmetic  20.3 us (3%)
    pallas_call x1, Pallas kernels, forward(): pl.pallas_call(functools.partial(forward_kernel, sizes), out_shape=[jax.S...  227 us
    pallas_call x1, Pallas kernels, backward(): pl.pallas_call(functools.partial(backward_kernel, sizes), out_shape=[jax....  197 us
    pallas_call x1, Pallas kernels, feed_forward(): pl.pallas_call(functools.partial(feed_forward_kernel, sizes), out_shape=[...  108 us

profile of v2, /device:TPU:0, one launch (start us, length us, event | category | flops | bytes accessed | tf_op | source)
XLA Modules:
  0.0 579.8 jit_solution(16371818191069244764)
XLA Ops:
  0.7 1.2 dynamic_slice.50
  3.6 0.8 reshape.605
  4.4 0.8 select_reduce_fusion.3
  9.4 0.9 select_reduce_fusion.2
  11.6 1.3 fusion.20
  14.3 1.9 reduce_window_sum.17
  20.1 1.8 copy.57
  23.5 1.6 fusion.2
  25.2 0.9 broadcast_multiply_fusion
  26.1 1.2 copy.58
  27.2 1.4 fusion.4
  28.7 1.2 pad_maximum_fusion
  29.8 226.5 %forward_attention.1 = (bf16[192,2048]{1,0:T(8,128)(2,1)}, f32[1,4352]{1,0:T(1,128)}, bf16[4,192,2048]{2,1,0:T(8,128)(2,1)}, bf16[2048,1024]{1,0:T(8,128)(2,1)},...) custom-call(bf16[192,2048]{1,0:T(8,128)(2,1)} %refs_0_.1, ...), custom_call_target="tpu_custom_call" | custom-call | tf_op jit(solution)/shard_map/forward_attention/pallas_call | solution.py:578
  256.3 108.2 %feed_forward.1 = (bf16[192,2048]{1,0:T(8,128)(2,1)}, f32[192,2048]{1,0:T(8,128)}, bf16[4,192,2048]{2,1,0:T(8,128)(2,1)}, f32[1,2048]{1,0:T(1,128)}, bf16[2048,7...) custom-call(bf16[4,2,192,2048]{3,2,1,0:T(8,128)(2,1)} %get-tuple-element.42.refs_0_, ...), custom_call_target="tpu_custom_call" | custom-call | tf_op jit(solution)/shard_map/feed_forward/pallas_call | solution.py:985
  364.6 1.9 reduce.2
  367.1 196.9 %backward_attention.1 = (bf16[192,2048]{1,0:T(8,128)(2,1)}, f32[1,4352]{1,0:T(1,128)}, f32[256,1536]{1,0:T(8,128)}, f32[256,1536]{1,0:T(8,128)}, f32[256,1536]{1...) custom-call(bf16[2048,768]{1,0:T(8,128)(2,1)} %get-tuple-element.50.refs_0_, ...), custom_call_target="tpu_custom_call" | custom-call | tf_op jit(solution)/shard_map/backward_attention/pallas_call | solution.py:1285
  564.0 2.2 copy.65
  569.9 1.9 split.22
  571.8 1.9 fusion.21
  573.7 1.6 copy.66
  575.3 0.9 copy.75
  576.2 0.9 copy.76
  577.1 1.1 copy.77
  578.2 1.1 copy.78
  (96 shorter events, 18.4 us)
Async XLA Ops:
  21.9 4.2 copy-start.3
  564.0 9.7 %copy-start.2 = (f32[256,1536]{1,0:T(8,128)S(1)}, f32[256,1536]{1,0:T(8,128)}, u32[]{:S(2)}) copy-start(f32[256,1536]{1,0:T(8,128)} %get-tuple-element.70) | copy-start | bytes 4718596
  571.8 3.6 copy-start.4
  573.7 2.5 copy-start.5
  575.3 1.8 copy-start.1
  576.2 2.0 copy-start

commit v3 on v2

--- a/solution.py
+++ b/solution.py
@@ -26,52 +26,6 @@
 
 def product(left, right, dims):
     return lax.dot_general(left, right, dims, preferred_element_type=jnp.float32)
-
-
-def layout(lengths_part, perm_part, body_len):
-    row_count, shorts = lengths_part.shape
-    doc_total = row_count * shorts
-    starts = body_len + jnp.cumsum(lengths_part, axis=1) - lengths_part
-    kept_flat = lengths_part.reshape(doc_total)
-    matched = perm_part[:, None] == jnp.arange(doc_total, dtype=jnp.int32)[None, :]
-    placed = jnp.sum(jnp.where(matched, kept_flat[:, None], 0), axis=0).reshape(row_count, shorts)
-    new_at = body_len + jnp.cumsum(placed, axis=1) - placed
-    new_start = jnp.sum(jnp.where(matched, new_at.reshape(doc_total)[None, :], 0), axis=1)
-    return (starts.reshape(doc_total), kept_flat, new_start, perm_part // shorts)
-
-
-def slot_labels(
-    kept_flat,
-    new_start,
-    dest_row,
-    part,
-    my_row,
-    valid_here,
-    body_len,
-    shard_len,
-    row_len,
-    row_count,
-):
-    doc_total = kept_flat.shape[0]
-    local = jnp.arange(shard_len, dtype=jnp.int32)
-    doc_ids = jnp.arange(doc_total, dtype=jnp.int32)
-    inside = (
-        (dest_row == my_row)[None, :]
-        & (local[:, None] >= new_start[None, :])
-        & (local[:, None] < (new_start + kept_flat)[None, :])
-    )
-    offset = local[:, None] - new_start[None, :]
-    in_short = jnp.any(inside, axis=1)
-    short_seg = jnp.sum(
-        jnp.where(inside, row_count + part * doc_total + doc_ids[None, :], 0), axis=1
-    )
-    short_pos = jnp.sum(jnp.where(inside, offset, 0), axis=1)
-    long_pos = part * body_len + local
-    in_long = (local < body_len) & (long_pos < valid_here)
-    flat_slot = my_row * row_len + part * shard_len + local
-    segment = jnp.where(in_long, my_row, jnp.where(in_short, short_seg, -1 - flat_slot))
-    position = jnp.where(in_long, long_pos, short_pos)
-    return (segment, position, in_long, in_short)
 
 
 class Place:
@@ -253,44 +207,64 @@
 
 class GatherDp:
     def __init__(self, place, mover, pieces, full):
-        self.place, self.mover, self.full = place, mover, full
+        self.place, self.mover, self.full, self.pieces = place, mover, full, pieces
         first, last = pieces[0], pieces[-1]
         self.window = pl.ds(first[1], last[1] + last[2] - first[1])
         self.rows = full.shape[0] // place.dp_size
-        self.local, self.over_h, self.over_l, self.over_y = [], [], [], []
         own_rows = self.block(place.d)
-        high_sends = [[] for _ in range(1, place.high)]
-        l_own, y_own = [], []
-        for own, start, size in pieces:
-            spot = full.at[own_rows, pl.ds(start, size)]
-            for step in range(1, place.high):
-                high_sends[step - 1].append(mover.send(own, spot, place.h_peer(step)))
-            l_own.append(mover.send(own, spot, place.l_peer))
-            y_own.append(mover.send(own, spot, place.y_peer))
-            self.local.append(mover.local(own, spot))
-        self.over_h = high_sends
-        self.over_l = [l_own]
-        self.over_y = y_own
+        self.spots = [full.at[own_rows, pl.ds(start, size)] for _, start, size in pieces]
+        self.local = [
+            mover.local(piece[0], spot) for piece, spot in zip(pieces, self.spots)
+        ]
+        self.over_y, self.passed_l = [], []
 
     def block(self, index):
         return pl.ds(pl.multiple_of(index * self.rows, self.rows), self.rows)
 
-    def forward_high(self):
+    def own_to(self, peer):
+        return [
+            self.mover.send(piece[0], spot, peer) for piece, spot in zip(self.pieces, self.spots)
+        ]
+
+    def send_h(self):
+        place = self.place
+        self.over_h = [self.own_to(place.h_peer(step)) for step in range(1, place.high)]
+
+    def send_l(self):
+        self.own_l = self.own_to(self.place.l_peer)
+
+    def send_y(self):
+        self.over_y += self.own_to(self.place.y_peer)
+
+    def part(self, high, index):
+        return self.full.at[self.block(high * GROUP + index), self.window]
+
+    def pass_h_to_l(self):
         place = self.place
         for step, copies in enumerate(self.over_h, 1):
             for copy in copies:
                 copy.wait_recv()
-            part = self.full.at[self.block(place.h_from(step) * GROUP + place.g), self.window]
-            self.over_l.append([self.mover.send(part, part, place.l_peer)])
+            part = self.part(place.h_from(step), place.g)
+            self.passed_l.append(self.mover.send(part, part, place.l_peer))
+
+    def pass_h_to_y(self):
+        place = self.place
+        for step in range(1, place.high):
+            part = self.part(place.h_from(step), place.g)
             self.over_y.append(self.mover.send(part, part, place.y_peer))
 
-    def forward_l(self):
+    def pass_own_l_to_y(self):
         place = self.place
-        for step, copies in enumerate(self.over_l):
-            for copy in copies:
-                copy.wait_recv()
-            high = place.h if step == 0 else place.h_from(step)
-            part = self.full.at[self.block(high * GROUP + place.gl), self.window]
+        for copy in self.own_l:
+            copy.wait_recv()
+        part = self.part(place.h, place.gl)
+        self.over_y.append(self.mover.send(part, part, place.y_peer))
+
+    def pass_l_to_y(self):
+        place = self.place
+        for step, copy in enumerate(self.passed_l, 1):
+            copy.wait_recv()
+            part = self.part(place.h_from(step), place.gl)
             self.over_y.append(self.mover.send(part, part, place.y_peer))
 
     def finish(self):
@@ -302,12 +276,23 @@
 
 class GatherColumns:
     def __init__(self, place, mover, own, full):
-        self.place, self.mover, self.full = place, mover, full
+        self.place, self.mover, self.full, self.own = place, mover, full, own
         self.quarter = own.shape[1] // GROUP
+        self.rows = own.shape[0]
         self.near = pl.ds(0, self.quarter)
         self.far = pl.ds(self.quarter, self.quarter)
+
+    def block(self, high):
+        rows = GROUP * self.rows
+        return pl.ds(pl.multiple_of(high * rows, rows), rows)
+
+    def send_g(self, spot=None):
+        place, mover, own = self.place, self.mover, self.own
+        if spot is None:
+            spot = self.full.at[
+                pl.ds(pl.multiple_of(place.d * self.rows, self.rows), self.rows), self.near
+            ]
         self.over_g = []
-        spot = full.at[place.h, place.g, :, self.near]
         for step in (3, 1, 2):
             to = lax.rem(place.g + step, GROUP)
             columns = pl.ds(pl.multiple_of(to * self.quarter, self.quarter), self.quarter)
@@ -315,28 +300,33 @@
         columns = pl.ds(pl.multiple_of(place.g * self.quarter, self.quarter), self.quarter)
         self.local = mover.local(own.at[:, columns], spot)
 
-    def forward_g(self):
-        place = self.place
+    def wait_g(self):
         self.local.wait()
         for copy in self.over_g:
             copy.wait_recv()
-        near = self.full.at[place.h, :, :, self.near]
-        far = self.full.at[place.h, :, :, self.far]
+
+    def send_h(self, source=None):
+        place = self.place
+        near = self.full.at[self.block(place.h), self.near]
+        source = near if source is None else source
         self.over_h = [
-            self.mover.send(near, near, place.h_peer(step)) for step in range(1, place.high)
+            self.mover.send(source, near, place.h_peer(step)) for step in range(1, place.high)
         ]
-        self.over_x = [self.mover.send(near, far, place.x_peer)]
-
-    def forward_high(self):
+
+    def send_x(self, source=None):
+        place = self.place
+        rows = self.block(place.h)
+        source = self.full.at[rows, self.near] if source is None else source
+        self.over_x = [self.mover.send(source, self.full.at[rows, self.far], place.x_peer)]
+
+    def pass_h_to_x(self):
         place = self.place
         for step, copy in enumerate(self.over_h, 1):
             copy.wait_recv()
-            high = place.h_from(step)
+            rows = self.block(place.h_from(step))
             self.over_x.append(
                 self.mover.send(
-                    self.full.at[high, :, :, self.near],
-                    self.full.at[high, :, :, self.far],
-                    place.x_peer,
+                    self.full.at[rows, self.near], self.full.at[rows, self.far], place.x_peer
                 )
             )
 
@@ -355,13 +345,96 @@
     return values * scale * gain
 
 
+def index_of(shape, dim):
+    return lax.broadcasted_iota(jnp.int32, shape, dim)
+
+
+def total_of(condition, values, axis):
+    picked = jnp.where(condition, values.astype(F32), 0.0)
+    return jnp.sum(picked, axis=axis, keepdims=True)
+
+
+class Layout:
+    def __init__(self, refs, part, row_count, body):
+        len_row, perm_row, len_col, perm_col = refs
+        docs = len_row.shape[-1]
+        self.docs, self.body, self.row_count = docs, body, row_count
+        self.bits = (docs // row_count).bit_length() - 1
+        down, along = index_of((docs, docs), 0), index_of((docs, docs), 1)
+        same_row = (down >> self.bits) == (along >> self.bits)
+        before = jnp.where(same_row & (down < along), 1.0, 0.0).astype(BF16)
+        self.lens = len_row[part].astype(F32)
+        self.lens_col = len_col[part].astype(F32)
+        perm, perm_of_col = perm_row[part], perm_col[part]
+        matched = perm_of_col == along
+        self.dest, self.dest_col = perm >> self.bits, perm_of_col >> self.bits
+        self.starts = body + jnp.dot(self.lens.astype(BF16), before, preferred_element_type=F32)
+        placed = total_of(matched, jnp.broadcast_to(self.lens_col, matched.shape), 0)
+        new_at = body + jnp.dot(placed.astype(BF16), before, preferred_element_type=F32)
+        self.new_col = total_of(matched, jnp.broadcast_to(new_at, matched.shape), 1)
+        self.new = product(
+            new_at.astype(BF16), jnp.where(matched, 1.0, 0.0).astype(BF16), CONTRACT_COLS
+        )
+
+    def labels(self, part, row, valid, tokens, row_len, column):
+        shape = (tokens, self.docs) if column else (self.docs, tokens)
+        axis = 1 if column else 0
+        slot, doc = index_of(shape, 1 - axis).astype(F32), index_of(shape, axis)
+        start, size, dest = (
+            (self.new, self.lens, self.dest)
+            if column
+            else (self.new_col, self.lens_col, self.dest_col)
+        )
+        inside = (dest == row) & (slot >= start) & (slot < start + size)
+        first = self.row_count + part * self.docs
+        segment = total_of(inside, doc + first, axis).astype(jnp.int32)
+        position = total_of(inside, slot - start, axis).astype(jnp.int32)
+        here = total_of(inside, jnp.ones(shape, F32), axis) > 0.0
+        local = index_of((tokens, 1) if column else (1, tokens), 1 - axis)
+        long_position = part * self.body + local
+        in_long = (local < self.body) & (long_position.astype(F32) < valid)
+        empty = -1 - (row * row_len + part * tokens + local)
+        segment = jnp.where(in_long, row, jnp.where(here, segment, empty))
+        return segment, jnp.where(in_long, long_position, position), in_long, in_long | here
+
+    def send_map(self, row, tokens):
+        shape = (self.row_count * 16, self.docs)
+        target, doc = index_of(shape, 0) >> 4, index_of(shape, 1)
+        mine = ((doc >> self.bits) == row) & (self.dest == target)
+        start = total_of(mine, jnp.broadcast_to(self.starts, shape), 1)
+        size = total_of(mine, jnp.broadcast_to(self.lens, shape), 1)
+        shape = (shape[0], tokens)
+        token = ((index_of(shape, 0) >> 2) & 3).astype(F32)
+        slot = index_of(shape, 1).astype(F32)
+        return jnp.where((token < size) & (slot == start + token), 1.0, 0.0).astype(BF16)
+
+    def recv_map(self, row, tokens):
+        shape = (self.docs, self.row_count * 16)
+        source, doc = index_of(shape, 1) >> 4, index_of(shape, 0)
+        mine = ((doc >> self.bits) == source) & (self.dest_col == row)
+        start = total_of(mine, jnp.broadcast_to(self.new_col, shape), 0)
+        size = total_of(mine, jnp.broadcast_to(self.lens_col, shape), 0)
+        shape = (tokens, shape[1])
+        token = ((index_of(shape, 1) >> 2) & 3).astype(F32)
+        slot = index_of(shape, 0).astype(F32)
+        return jnp.where((token < size) & (slot == start + token), 1.0, 0.0).astype(BF16)
+
+
+def spread_piece(piece, place, total):
+    size = piece.shape[1]
+    shape = (size, total)
+    spot = index_of(shape, 1) == index_of(shape, 0) + place.d * size
+    return jnp.dot(piece, jnp.where(spot, 1.0, 0.0).astype(BF16), preferred_element_type=F32)
+
+
 def forward_kernel(sizes, *refs):
-    (hidden, keep, send_maps, recv_maps, gain_row, cosine, sine, seg_col, pos_col, seg_row,
-     pos_row, out_grad, live, wq, wk, wv, wo, wg, wu, wd) = refs[:20]
+    (hidden, valid_row, len_row, perm_row, len_col, perm_col, attn_gain, mlp_gain, query_gain,
+     key_gain, out_grad, wq, wk, wv, wo, wg, wu, wd) = refs[:18]
     (moved, gains, normed, full_qkv, full_wo, full_g, full_u, full_d, grad_y, lin, rot, attended,
-     log_total, resid, full_nm) = refs[20:35]
-    (blocks_out, blocks_in, rows_in, normed_own, bias, part_own, from_c, from_x, to_c,
-     nm_own, send_sems, recv_sems, local_sems) = refs[35:]
+     log_total, resid, full_nm, cosine, sine, seg_col, pos_col, seg_row, pos_row, keep, live,
+     send_map, recv_map) = refs[18:43]
+    (blocks_out, blocks_in, rows_in, gain_row, part_seg, part_pos, normed_own, bias, part_own,
+     from_c, from_x, to_c, nm_own, send_sems, recv_sems, local_sems) = refs[43:]
     place = Place(*sizes)
     mover = Mover(send_sems, recv_sems, local_sems)
     tokens, width = hidden.shape
@@ -371,29 +444,44 @@
     parts = sizes[1]
     repeat = query_width // key_width
 
+    greet(dp_peers(place) + [place.x_peer, place.c_peer])
+    key_parts = [(wk, query_width, key_width), (wv, query_width + key_width, key_width)]
+    query = GatherDp(place, mover, [(wq, 0, query_width)], full_qkv)
+    key = GatherDp(place, mover, key_parts, full_qkv)
+    out = GatherDp(place, mover, [(wo, 0, wo.shape[1])], full_wo)
+    gate = GatherColumns(place, mover, wg, full_g)
+    upper = GatherColumns(place, mover, wu, full_u)
+    lower = GatherColumns(place, mover, wd, full_d)
+    gate.send_g()
+    key.send_h()
+    lower.send_g()
+    row_len = parts * tokens
+    body = tokens - (len_row.shape[2] // place.dp_size) * MAXSHORT
+    layout_refs = (len_row, perm_row, len_col, perm_col)
+    here = index_of(valid_row.shape, 1) == place.d
+    valid = total_of(here, valid_row[...], 1)
+    own = Layout(layout_refs, place.s, place.dp_size, body)
+    send_map[...] = own.send_map(place.d, tokens)
+    recv_map[...] = own.recv_map(place.d, tokens)
+    _, _, own_long, own_live = own.labels(place.s, place.d, valid, tokens, row_len, True)
+    keep[...] = jnp.where(own_long, 1.0, 0.0)
+    live[...] = jnp.where(own_live, 1.0, 0.0)
+    gain_row[:, :width] = spread_piece(attn_gain[...], place, width)
+    gain_row[:, width : 2 * width] = spread_piece(mlp_gain[...], place, width)
+    gain_row[:, 2 * width : 2 * width + head] = spread_piece(query_gain[...], place, head)
+    gain_row[:, 2 * width + head :] = spread_piece(key_gain[...], place, head)
+    piece_row = index_of((place.dp_size * 16, 1), 0) & 3
     for q in range(GROUP):
         lanes = pl.ds(q * columns, columns)
-        piece = jnp.dot(send_maps[q], hidden[:, lanes], preferred_element_type=F32)
-        if q == 0:
-            total = piece
-        else:
-            total = total + piece
+        piece = jnp.dot(send_map[...], hidden[:, lanes], preferred_element_type=F32)
+        piece = jnp.where(piece_row == q, piece, 0.0)
+        total = piece if q == 0 else total + piece
     blocks_out[...] = total.astype(BF16).reshape(blocks_out.shape)
-    greet(dp_peers(place) + [place.x_peer, place.c_peer])
     copies = []
     for step in range(1, place.dp_size):
         other = lax.rem(place.d + step, place.dp_size)
         copies.append(mover.send(blocks_out.at[other], blocks_in.at[place.d], (other, place.s)))
         copies.append(mover.send(gain_row, rows_in.at[place.d], (other, place.s)))
-    key_parts = [(wk, query_width, key_width), (wv, query_width + key_width, key_width)]
-    attn = [
-        GatherDp(place, mover, [(wq, 0, query_width)], full_qkv),
-        GatherDp(place, mover, key_parts, full_qkv),
-    ]
-    mlp = [GatherColumns(place, mover, wg, full_g)]
-    attn.append(GatherDp(place, mover, [(wo, 0, wo.shape[1])], full_wo))
-    mlp.append(GatherColumns(place, mover, wu, full_u))
-    mlp.append(GatherColumns(place, mover, wd, full_d))
     blocks_in[place.d] = blocks_out[place.d]
     rows_in[place.d] = gain_row[...]
     for copy in copies:
@@ -405,7 +493,8 @@
     incoming = blocks_in[...].reshape(place.dp_size * 16, columns)
     for q in range(GROUP):
         lanes = pl.ds(q * columns, columns)
-        here = jnp.dot(recv_maps[q], incoming, preferred_element_type=F32)
+        chosen = jnp.where(piece_row == q, incoming, jnp.zeros_like(incoming))
+        here = jnp.dot(recv_map[...], chosen, preferred_element_type=F32)
         here = here + jnp.where(keep[...] > 0.0, hidden[:, lanes].astype(F32), 0.0)
         moved[:, lanes] = here.astype(BF16)
 
@@ -417,19 +506,59 @@
 
     lax.fori_loop(0, tokens // 32, norm_moved, 0)
     row = GatherSeq(place, mover, normed_own, normed)
-    attn[0].forward_high()
-    mlp[0].forward_g()
-    attn[1].forward_high()
-    attn[0].forward_l()
+
+    def label_part(part, carry):
+        layout = Layout(layout_refs, part, place.dp_size, body)
+        spots = pl.ds(pl.multiple_of(part * tokens, tokens), tokens)
+        segment, position, _, _ = layout.labels(part, place.d, valid, tokens, row_len, True)
+        seg_col[spots, :], pos_col[spots, :] = segment, position
+        segment, position, _, _ = layout.labels(part, place.d, valid, tokens, row_len, False)
+        part_seg[part], part_pos[part] = segment, position
+        half = head // 2
+        lane = index_of((1, head), 1)
+        power = jnp.where(lane < half, lane, lane - half).astype(F32)
+        angles = pos_col[spots, :].astype(F32) * jnp.exp(
+            power * (-2.0 * math.log(ROPE_BASE) / head)
+        )
+        cosine[spots, :] = jnp.cos(angles)
+        sine[spots, :] = jnp.where(lane < half, -1.0, 1.0) * jnp.sin(angles)
+        return carry
+
+    query.send_y()
+    out.send_h()
+    key.send_l()
+    lower.wait_g()
+    key.pass_h_to_l()
+    key.pass_h_to_y()
+    query.send_h()
+    query.send_l()
+    key.pass_own_l_to_y()
+    gate.wait_g()
+    gate.send_h()
+    gate.send_x()
+    key.send_y()
+    query.pass_h_to_l()
+    upper.send_g()
+    out.send_l()
+    key.pass_l_to_y()
+    lower.send_x()
+    query.pass_h_to_y()
+    query.pass_own_l_to_y()
     row.forward()
-    attn[1].forward_l()
-    mlp[1].forward_g()
-    attn[2].forward_high()
-    mlp[2].forward_g()
-    attn[2].forward_l()
+    lower.send_h()
+    out.pass_h_to_l()
+    query.pass_l_to_y()
+    out.pass_h_to_y()
+    upper.wait_g()
+    upper.send_x()
+    out.send_y()
+    upper.send_h()
+    lax.fori_loop(0, parts, label_part, 0)
+    seg_row[...] = jnp.concatenate([part_seg[part] for part in range(parts)], axis=1)
+    pos_row[...] = jnp.concatenate([part_pos[part] for part in range(parts)], axis=1)
     row.finish()
-    attn[0].finish()
-    attn[1].finish()
+    query.finish()
+    key.finish()
 
     gain_query = gains[:, 2 * width : 2 * width + head]
     gain_key = gains[:, 2 * width + head : 2 * width + 2 * head]
@@ -454,7 +583,8 @@
         return carry
 
     lax.fori_loop(0, parts, project, 0)
-    mlp[0].forward_high()
+    out.pass_own_l_to_y()
+    gate.pass_h_to_x()
     scale = head ** (-0.5)
     for part in range(parts):
         keys = (part + 1) * tokens
@@ -487,8 +617,9 @@
             return carry
 
         lax.fori_loop(0, key_width // head, attend, 0)
-    mlp[1].forward_high()
-    attn[2].finish()
+        if part == 2:
+            out.pass_l_to_y()
+    out.finish()
 
     def project_out(part, target):
         source = attended[pl.ds(pl.multiple_of(part * tokens, tokens), tokens), :]
@@ -511,7 +642,7 @@
     project_out(places[1] + 1 - place.c, to_c.at[1])
     over_c.append(mover.send(to_c.at[1], from_c.at[1], place.c_peer))
     project_out(places[1] + place.c, part_own.at[1])
-    mlp[2].forward_high()
+    lower.pass_h_to_x()
     over_c[1].wait_recv()
     over_x.wait_recv()
 
@@ -525,34 +656,37 @@
 
     lax.fori_loop(0, tokens // 32, norm_resid, 0)
     group = GatherGroup(place, mover, nm_own, full_nm)
+    upper.pass_h_to_x()
     group.forward()
     group.finish_ici()
-    for part in [group] + mlp:
+    for part in (group, gate, upper, lower):
         part.finish()
     mover.finish()
 
 
 def forward(sizes, collective_id, head_size, args):
     dp_size, seq_size = sizes
-    hidden, wq, wk, wo, wg = args[0], args[13], args[14], args[16], args[17]
+    hidden, wq, wk, wo, wg = args[0], args[11], args[12], args[14], args[15]
     tokens, width = hidden.shape
     high = dp_size // GROUP
     rows = wq.shape[0]
     row_len = seq_size * tokens
     rotated = wq.shape[1] + wk.shape[1]
-    wide = (high, GROUP, rows, wg.shape[1] // 2)
+    inner = wg.shape[1] // 2
     group = (GROUP, seq_size // 2, tokens, width)
     heads = wq.shape[1] // head_size
-    gain_width = args[4].shape[1]
+    gain_width = 2 * (width + head_size)
+    routes = dp_size * 16
+    column, line = (row_len, 1), (1, row_len)
     outs = [
         ((tokens, width), BF16, VMEM),
         ((1, gain_width), F32, VMEM),
         ((seq_size, tokens, width), BF16, VMEM),
         ((width, rotated + wk.shape[1]), BF16, VMEM),
         ((width, wo.shape[1]), BF16, VMEM),
-        (wide, BF16, HBM),
-        (wide, BF16, HBM),
-        (wide, BF16, HBM),
+        ((width, inner), BF16, HBM),
+        ((width, inner), BF16, HBM),
+        ((width, inner), BF16, HBM),
         ((tokens, width), BF16, VMEM),
         ((row_len, rotated), BF16, VMEM),
         ((row_len, rotated + wk.shape[1]), BF16, VMEM),
@@ -560,11 +694,24 @@
         ((wk.shape[1] // head_size, seq_size, heads * head_size // wk.shape[1] * tokens, 1), F32, VMEM),
         ((tokens, width), F32, VMEM),
         (group, BF16, HBM),
+        ((row_len, head_size), F32, VMEM),
+        ((row_len, head_size), F32, VMEM),
+        (column, jnp.int32, VMEM),
+        (column, jnp.int32, VMEM),
+        (line, jnp.int32, VMEM),
+        (line, jnp.int32, VMEM),
+        ((tokens, 1), F32, VMEM),
+        ((tokens, 1), F32, VMEM),
+        ((routes, tokens), BF16, VMEM),
+        ((tokens, routes), BF16, VMEM),
     ]
     scratch = [
         pltpu.VMEM((dp_size, 16, width // GROUP), BF16),
         pltpu.VMEM((dp_size, 16, width // GROUP), BF16),
         pltpu.VMEM((dp_size, 1, gain_width), F32),
+        pltpu.VMEM((1, gain_width), F32),
+        pltpu.VMEM((seq_size, 1, tokens), jnp.int32),
+        pltpu.VMEM((seq_size, 1, tokens), jnp.int32),
         pltpu.VMEM((tokens, width), BF16),
         pltpu.VMEM((wq.shape[1] // wk.shape[1] * tokens, row_len), F32),
         pltpu.VMEM((2, tokens, width), BF16),
@@ -578,7 +725,7 @@
     return pl.pallas_call(
         functools.partial(forward_kernel, sizes),
         out_shape=[jax.ShapeDtypeStruct(shape, dtype) for shape, dtype, _ in outs],
-        in_specs=[VMEM] * 13 + [HBM] * 7,
+        in_specs=[VMEM] * 11 + [HBM] * 7,
         out_specs=[spec for _, _, spec in outs],
         scratch_shapes=scratch + sems(sends, 16),
         compiler_params=comm_params(collective_id),
@@ -587,8 +734,7 @@
 
 
 class ScatterColumns:
-    sends = GROUP
-    pieces = 4
+    stage_rows = 512
 
     @staticmethod
     def scratch(high, rows, quarter):
@@ -605,35 +751,63 @@
         self.group_rows = from_h.shape[1]
         self.quarter = from_x.shape[1]
 
-    def start(self):
+    def rows_of(self, step):
+        high = lax.rem(self.place.h + step, self.place.high)
+        return high * self.group_rows
+
+    def start(self, steps):
         quarter = self.quarter
-        far = self.parts.at[:, pl.ds(quarter, quarter)]
-        self.over_x = self.mover.send(far, self.from_x, self.place.x_peer)
-
-    def forward_x(self, stage):
-        place, mover, total = self.place, self.mover, self.from_x
-        rows = total.shape[0] // self.pieces
+        for step in steps:
+            rows = pl.ds(pl.multiple_of(self.rows_of(step), self.group_rows), self.group_rows)
+            self.over_x[step] = self.mover.send(
+                self.parts.at[rows, pl.ds(quarter, quarter)],
+                self.from_x.at[rows],
+                self.place.x_peer,
+            )
+
+    def start_far(self):
+        self.over_x = {}
+        self.start(range(1, self.place.high))
+
+    def start_near(self):
+        self.start((0,))
+
+    def add_x(self, step, stage):
+        mover, total = self.mover, self.from_x
+        rows = stage.shape[1]
+        base = self.rows_of(step)
         near = pl.ds(0, self.quarter)
+        pieces = self.group_rows // rows
+
+        def block(index):
+            return pl.ds(pl.multiple_of(base + index * rows, rows), rows)
 
         def load(index):
-            block = pl.ds(index * rows, rows)
-            return mover.local(self.parts.at[block, near], stage.at[index % 2])
+            return mover.local(self.parts.at[block(index), near], stage.at[index % 2])
 
         copies = [load(0)]
-        self.over_x.wait_recv()
-        for index in range(self.pieces):
-            if index + 1 < self.pieces:
+        self.over_x[step].wait_recv()
+        for index in range(pieces):
+            if index + 1 < pieces:
                 copies.append(load(index + 1))
             copies[index].wait()
-            part = total.at[pl.ds(index * rows, rows)]
+            part = total.at[block(index)]
             add_rows(part, [part, stage.at[index % 2]], rows, 64)
+
+    def forward_far(self, stage):
+        place = self.place
         self.over_h = []
         for step in range(1, place.high):
-            high = lax.rem(place.h + step, place.high)
-            block = pl.ds(pl.multiple_of(high * self.group_rows, self.group_rows), self.group_rows)
+            self.add_x(step, stage)
+            block = pl.ds(pl.multiple_of(self.rows_of(step), self.group_rows), self.group_rows)
             self.over_h.append(
-                mover.send(total.at[block], self.from_h.at[step - 1], place.h_peer(step))
+                self.mover.send(
+                    self.from_x.at[block], self.from_h.at[step - 1], place.h_peer(step)
+                )
             )
+
+    def add_near(self, stage):
+        self.add_x(0, stage)
 
     def block(self, index):
         rows = self.group_rows // GROUP
@@ -859,6 +1033,21 @@
             gate_grad[rows, lanes] = (upper * (gain + silu * (1.0 - gain))).astype(BF16)
         return carry
 
+    def weight_grads(source, grads, targets):
+        copies = []
+        count = len(grads)
+        for index in range(width // tile):
+            lanes = pl.ds(index * tile, tile)
+            left = source[:, :, :, lanes].reshape(GROUP * block, tile)
+            for which in range(count):
+                slot = (index * count + which) % 2
+                if len(copies) >= 2:
+                    copies[-2].wait()
+                stage[slot] = product(left, grads[which][...], CONTRACT_ROWS).astype(BF16)
+                copies.append(mover.local(stage.at[slot], targets[which].at[lanes]))
+        copies[-2].wait()
+        copies[-1].wait()
+
     nm_loads[0].wait()
     nm_loads[1].wait()
     lax.fori_loop(0, 2, gate_up, 0)
@@ -922,19 +1111,6 @@
     for index in range(GROUP):
         down.start(index)
 
-    def weight_grad(grad, source, target):
-        copies = []
-        tiles = width // tile
-        for index in range(tiles):
-            lanes = pl.ds(index * tile, tile)
-            left = source[:, :, :, lanes].reshape(GROUP * block, tile)
-            if index >= 2:
-                copies[index - 2].wait()
-            stage[index % 2] = product(left, grad[...], CONTRACT_ROWS).astype(BF16)
-            copies.append(mover.local(stage.at[index % 2], target.at[lanes]))
-        copies[-2].wait()
-        copies[-1].wait()
-
     def back_mlp(rows, total):
         grad, terms = norm_back(resid[rows, :], gains[:, width : 2 * width], total)
         grad = grad + grad_y[rows, :].astype(F32)
@@ -945,15 +1121,14 @@
     def mix(rows, total):
         mixed[rows, :] = ((resid[rows, :] + total) * live[rows, :]).astype(BF16)
 
-    weight_grad(hidden, gy, out_gd)
+    weight_grads(gy, [hidden], [out_gd])
     nmlp.finish(back_mlp)
     row = GatherSeq(place, mover, grad_proj, full_proj)
     for index in range(GROUP):
         down.forward(index)
-    weight_grad(gate_grad, nm, out_gg)
+    weight_grads(nm, [gate_grad, up_grad], [out_gg, out_gu])
     down.forward_diag()
     row.forward()
-    weight_grad(up_grad, nm, out_gu)
     down.finish(mix)
     row.finish()
     mover.finish()
@@ -996,7 +1171,7 @@
 def backward_kernel(sizes, *refs):
     (part_gd, part_gg, part_gu, wo, grad_resid, full_proj, moved, keep, gain_mlp, gains, cosine,
      sine, seg_col, pos_col, seg_row, pos_row, log_row, normed, full_qkv, lin, rot, attended,
-     recv_maps_t, send_maps_t) = refs[:24]
+     recv_map, send_map) = refs[:24]
     grad_hidden, gain_sums, out_gd, out_gg, out_gu, out_qkv, out_wo = refs[24:31]
     send_sems, recv_sems, local_sems = refs[-3:]
     scratch = list(refs[31:-3])
@@ -1029,8 +1204,10 @@
     blocks_out, blocks_in, rows_in, row_c, row_x = take(5)
 
     greet(dp_peers(place) + [place.x_peer, place.c_peer])
-    for part in mlp:
-        part.start()
+    lower, gate, upper = mlp
+    gate.start_far()
+    lower.start_far()
+    upper.start_far()
     gain_sums[...] = jnp.zeros_like(gain_sums)
     gain_sums[:, width : 2 * width] = gain_mlp[...]
     grad_keys[...] = jnp.zeros_like(grad_keys)
@@ -1050,9 +1227,6 @@
         source = full_proj[:, :, lanes].reshape(parts * tokens, 256)
         grad_wo[lanes, :] = product(source, attended[...], CONTRACT_ROWS).astype(BF16)
         return carry
-
-    lax.fori_loop(0, width // 256, out_weight_grad, 0)
-    wo_sum.start()
 
     scale = head ** (-0.5)
     gain_query = gains[:, 2 * width : 2 * width + head]
@@ -1106,9 +1280,14 @@
             return carry
 
         lax.fori_loop(0, key_width // head, attend, 0)
+        if part == 0:
+            gate.forward_far(column_stage)
         if part == parts - 2:
-            mlp[0].forward_x(column_stage)
-            wo_sum.forward_y()
+            lax.fori_loop(0, width // 256, out_weight_grad, 0)
+            lower.forward_far(column_stage)
+            wo_sum.start()
+            for columns_sum in (gate, upper, lower):
+                columns_sum.start_near()
     for pair in range(key_width // head):
 
         def back_keys(part, carry):
@@ -1139,10 +1318,13 @@
 
         lax.fori_loop(0, width // 256, step, 0)
 
+    wo_sum.forward_y()
+    weight_grad(grad_query, 0, query_width)
     weight_grad(grad_key, query_width, 2 * key_width)
-    key_sum.start()
-    weight_grad(grad_query, 0, query_width)
     query_sum.start()
+    gate.add_near(column_stage)
+    upper.forward_far(column_stage)
+    gate.forward_high()
 
     def normed_grad(part, target):
         source = grad_lin[pl.ds(pl.multiple_of(part * tokens, tokens), tokens), :]
@@ -1162,13 +1344,20 @@
     over_c[0].wait_recv()
     add_rows(to_c.at[1], [to_c.at[1], from_c.at[0]], tokens, 32)
     over_x = mover.send(to_c.at[1], from_x, place.x_peer)
+    query_sum.forward_y()
+    key_sum.start()
+    lower.add_near(column_stage)
+    lower.forward_high()
     normed_grad(places[1] + 1 - place.c, to_c.at[2])
     over_c.append(mover.send(to_c.at[2], from_c.at[1], place.c_peer))
     normed_grad(places[1] + place.c, to_c.at[3])
-    mlp[1].forward_x(column_stage)
-    mlp[0].forward_high()
+    upper.add_near(column_stage)
+    gate.finish(out_stage, out_gg)
+    query_sum.forward_l()
     wo_sum.forward_l()
     key_sum.forward_y()
+    key_sum.forward_l()
+    upper.forward_high()
     over_c[1].wait_recv()
     over_x.wait_recv()
 
@@ -1182,9 +1371,11 @@
         return carry
 
     lax.fori_loop(0, tokens // 32, back_normed, 0)
+    piece_row = index_of((place.dp_size * 16, 1), 0) & 3
     for q in range(GROUP):
         lanes = pl.ds(q * columns, columns)
-        piece = jnp.dot(recv_maps_t[q], grad_moved[:, lanes], preferred_element_type=F32)
+        piece = product(recv_map[...], grad_moved[:, lanes], CONTRACT_ROWS)
+        piece = jnp.where(piece_row == q, piece, 0.0)
         total = piece if q == 0 else total + piece
     blocks_out[...] = total.astype(BF16).reshape(blocks_out.shape)
     copies = []
@@ -1194,9 +1385,7 @@
         copies.append(mover.send(gain_sums, rows_in.at[place.d], (other, place.s)))
     blocks_in[place.d] = blocks_out[place.d]
     rows_in[place.d] = gain_sums[...]
-    query_sum.forward_y()
-    key_sum.forward_l()
-    mlp[2].forward_x(column_stage)
+    query_sum.finish()
     for copy in copies:
         copy.wait_recv()
     row_total = rows_in[0]
@@ -1207,22 +1396,18 @@
     returned = blocks_in[...].reshape(place.dp_size * 16, columns)
     for q in range(GROUP):
         lanes = pl.ds(q * columns, columns)
-        here = jnp.dot(send_maps_t[q], returned, preferred_element_type=F32)
+        chosen = jnp.where(piece_row == q, returned, jnp.zeros_like(returned))
+        here = product(send_map[...], chosen, CONTRACT_ROWS)
         here = here + jnp.where(keep[...] > 0.0, grad_moved[:, lanes].astype(F32), 0.0)
         grad_hidden[:, lanes] = here.astype(BF16)
-    query_sum.forward_l()
     pass_c.wait_recv()
     row_x[0] = row_c[0] + row_c[1]
     pass_x = mover.send(row_x.at[0], row_x.at[1], place.x_peer)
-    mlp[1].forward_high()
-    mlp[2].forward_high()
-    mlp[0].finish(out_stage, out_gd)
+    lower.finish(out_stage, out_gd)
+    upper.finish(out_stage, out_gu)
     wo_sum.finish()
-    mlp[1].finish(out_stage, out_gg)
     key_sum.finish()
-    query_sum.finish()
     pass_x.wait_recv()
-    mlp[2].finish(out_stage, out_gu)
     mover.finish()
     gain_sums[...] = row_x[0] + row_x[1]
 
@@ -1248,7 +1433,7 @@
         ((rows, rot.shape[1]), F32, VMEM),
         ((rows, query_width), F32, VMEM),
     ]
-    piece = high * GROUP * rows // ScatterColumns.pieces
+    piece = min(GROUP * rows, ScatterColumns.stage_rows)
     scratch = [
         pltpu.VMEM((2, piece, quarter), BF16),
         pltpu.VMEM((rows, GROUP * quarter), F32),
@@ -1279,9 +1464,9 @@
         pltpu.VMEM((2,) + gains.shape, F32),
         pltpu.VMEM((2,) + gains.shape, F32),
     ]
-    sends = 3 * (high + 3) + 3 * ScatterDp.sends(high)
+    sends = 3 * (2 * high + 2) + 3 * ScatterDp.sends(high)
     sends += 3 + 2 * (dp_size - 1) + 2
-    local = 3 * (ScatterColumns.pieces + 1) + 1
+    local = 3 * (high * GROUP * rows // piece + 1)
     return pl.pallas_call(
         functools.partial(backward_kernel, sizes),
         out_shape=[jax.ShapeDtypeStruct(shape, dtype) for shape, dtype, _ in outs],
@@ -1312,94 +1497,12 @@
     w_down,
     out_grad,
 ):
-    shard_len = hidden_in.shape[0]
     model_width = hidden_in.shape[1]
-    seq_count = doc_lengths.shape[0]
-    row_count = doc_lengths.shape[1]
-    shorts = doc_lengths.shape[2]
-    row_len = shard_len * seq_count
-    cap_len = MAXSHORT
-    body_len = shard_len - shorts * cap_len
+    seq_count, row_count, _ = doc_lengths.shape
     my_row = lax.axis_index("dp")
     my_part = lax.axis_index("seq")
-    valid_here = valid_len[my_row]
-    all_starts, all_kept, all_new, all_dest = jax.vmap(
-        lambda lengths_part, perm_part: layout(lengths_part, perm_part, body_len)
-    )(doc_lengths, doc_perm)
-    part_ids = jnp.arange(seq_count, dtype=jnp.int32)
-    seg_parts, pos_parts, long_parts, short_parts = jax.vmap(
-        lambda kept_p, new_p, dest_p, part: slot_labels(
-            kept_p, new_p, dest_p, part, my_row, valid_here, body_len, shard_len, row_len, row_count
-        )
-    )(all_kept, all_new, all_dest, part_ids)
-    segment = seg_parts.reshape(row_len)
-    position = pos_parts.reshape(row_len)
-    seg_local = lax.dynamic_index_in_dim(seg_parts, my_part, 0, keepdims=False)
-    pos_local = lax.dynamic_index_in_dim(pos_parts, my_part, 0, keepdims=False)
-    keep_long = lax.dynamic_index_in_dim(long_parts, my_part, 0, keepdims=False)
-    live_local = keep_long | lax.dynamic_index_in_dim(short_parts, my_part, 0, keepdims=False)
-    starts = lax.dynamic_index_in_dim(all_starts, my_part, 0, keepdims=False)
-    kept_flat = lax.dynamic_index_in_dim(all_kept, my_part, 0, keepdims=False)
-    new_start = lax.dynamic_index_in_dim(all_new, my_part, 0, keepdims=False)
-    dest_row = lax.dynamic_index_in_dim(all_dest, my_part, 0, keepdims=False)
-    row_ids = jnp.arange(row_count, dtype=jnp.int32)
-    local_slots = jnp.arange(shard_len, dtype=jnp.int32)
-    cap_ids = jnp.arange(cap_len, dtype=jnp.int32)
-    my_dest = lax.dynamic_slice_in_dim(dest_row, my_row * shorts, shorts)
-    my_starts = lax.dynamic_slice_in_dim(starts, my_row * shorts, shorts)
-    my_kept = lax.dynamic_slice_in_dim(kept_flat, my_row * shorts, shorts)
-    going = my_dest[None, :] == row_ids[:, None]
-    send_start = jnp.sum(jnp.where(going, my_starts[None, :], 0), axis=1)
-    send_len = jnp.sum(jnp.where(going, my_kept[None, :], 0), axis=1)
-    send_map = (
-        (
-            (cap_ids[None, :, None] < send_len[:, None, None])
-            & (local_slots[None, None, :] == send_start[:, None, None] + cap_ids[None, :, None])
-        )
-        .reshape(row_count * cap_len, shard_len)
-        .astype(jnp.bfloat16)
-    )
-    coming = (dest_row == my_row).reshape(row_count, shorts)
-    recv_start = jnp.sum(jnp.where(coming, new_start.reshape(row_count, shorts), 0), axis=1)
-    recv_len = jnp.sum(jnp.where(coming, kept_flat.reshape(row_count, shorts), 0), axis=1)
-    recv_map = (
-        (
-            (cap_ids[None, None, :] < recv_len[None, :, None])
-            & (local_slots[:, None, None] == recv_start[None, :, None] + cap_ids[None, None, :])
-        )
-        .reshape(shard_len, row_count * cap_len)
-        .astype(jnp.bfloat16)
-    )
-    same_piece = jnp.eye(GROUP, dtype=BF16)
-
-    def spread(piece, total):
-        return lax.dynamic_update_slice(
-            jnp.zeros((total,), F32), piece.astype(F32), (my_row * piece.shape[0],)
-        )
-
     head_size = query_norm.shape[0] * row_count
-    gain_row = jnp.concatenate(
-        [
-            spread(attn_norm, model_width),
-            spread(mlp_norm, model_width),
-            spread(query_norm, head_size),
-            spread(key_norm_gain, head_size),
-        ]
-    )[None, :]
-    send_maps = (same_piece[:, None, :, None] * send_map[None, :, None, :]).reshape(
-        GROUP, -1, shard_len
-    )
-    recv_maps = (recv_map[None, :, :, None] * same_piece[:, None, None, :]).reshape(
-        GROUP, shard_len, -1
-    )
-    half_width = head_size // 2
-    freq_index = jnp.arange(half_width, dtype=F32)
-    inverse = jnp.exp(freq_index * (-2.0 * math.log(ROPE_BASE) / head_size))
-    angles = position.astype(F32)[:, None] * inverse[None, :]
-    cosine = jnp.concatenate([jnp.cos(angles)] * 2, axis=1)
-    sine = jnp.concatenate([-jnp.sin(angles), jnp.sin(angles)], axis=1)
-    live_scale = live_local.astype(F32)[:, None]
-    keep_scale = keep_long.astype(F32)[:, None]
+    lengths = doc_lengths.reshape(seq_count, -1)
     (
         moved_low,
         gains,
@@ -1416,24 +1519,32 @@
         log_total,
         resid_rows,
         normed_mlp,
+        cosine,
+        sine,
+        seg_col,
+        pos_col,
+        seg_row,
+        pos_row,
+        keep,
+        live,
+        send_map,
+        recv_map,
     ) = forward(
         sizes,
         1,
         head_size,
         (
             hidden_in,
-            keep_scale,
-            send_maps,
-            recv_maps,
-            gain_row,
-            cosine,
-            sine,
-            segment[:, None],
-            position[:, None],
-            segment[None, :],
-            position[None, :],
+            valid_len[None, :],
+            lengths[:, None, :],
+            doc_perm[:, None, :],
+            lengths[:, :, None],
+            doc_perm[:, :, None],
+            attn_norm[None, :],
+            mlp_norm[None, :],
+            query_norm[None, :],
+            key_norm_gain[None, :],
             out_grad,
-            live_scale,
             w_query,
             key_weight,
             value_weight,
@@ -1444,16 +1555,13 @@
         ),
     )
     cuts = (model_width, 2 * model_width, 2 * model_width + head_size)
-    gate_mat = gate_mat.reshape(model_width, -1)
-    up_mat = up_mat.reshape(model_width, -1)
-    down_mat = down_mat.reshape(model_width, -1)
     query_width = w_query.shape[1]
     key_width = key_weight.shape[1]
     qkv_cuts = (query_width, query_width + key_width)
     mixed, grad_resid, grad_proj, gain_mlp_sum, grad_down, grad_gate, grad_up = feed_forward(
         sizes,
         2,
-        (normed_mlp, gate_mat, up_mat, down_mat, grad_y_own, resid_rows, live_scale, gains),
+        (normed_mlp, gate_mat, up_mat, down_mat, grad_y_own, resid_rows, live, gains),
     )
     grad_hidden, gain_sums, out_down, out_gate, out_up, out_qkv, out_wo = backward(
         sizes,
@@ -1466,23 +1574,23 @@
             grad_resid,
             grad_proj,
             moved_low,
-            keep_scale,
+            keep,
             gain_mlp_sum,
             gains,
             cosine,
             sine,
-            segment[:, None],
-            position[:, None],
-            segment[None, :],
-            position[None, :],
+            seg_col,
+            pos_col,
+            seg_row,
+            pos_row,
             jnp.swapaxes(log_total, 2, 3),
             normed,
             qkv_mat,
             rotated_lin,
             rotated_all,
             attended,
-            jnp.swapaxes(recv_maps, 1, 2),
-            jnp.swapaxes(send_maps, 1, 2),
+            recv_map,
+            send_map,
         ),
     )
     out_query, out_key, out_value = jnp.split(out_qkv, qkv_cuts, axis=1)

time: 589 us -> 536 us (0.910)
  Pallas kernels: 532 us -> 504 us
  other arithmetic: 20.3 us -> 1.89 us
  local copies, waits for them, and re-layouts: 26.6 us -> 19.8 us
    pallas_call x1, Pallas kernels: 227 us -> 197 us  [forward(): pl.pallas_call(functools.partial(forward_kernel, sizes), out_shape=[jax.S...]
    unnamed x20 -> x30, local copies, waits for them, and re-layouts: 10.8 us -> 12.3 us
where the time goes in v3:
time: 536 us; the launch traced here: 527 us
  Pallas kernels  504 us (94%)
  local copies, waits for them, and re-layouts  19.8 us (4%)
    pallas_call x1, Pallas kernels, forward(): pl.pallas_call(functools.partial(forward_kernel, sizes), out_shape=[jax.S...  197 us
    pallas_call x1, Pallas kernels, backward(): pl.pallas_call(functools.partial(backward_kernel, sizes), out_shape=[jax....  196 us
    pallas_call x1, Pallas kernels, feed_forward(): pl.pallas_call(functools.partial(feed_forward_kernel, sizes), out_shape=[...  110 us
    unnamed x30, local copies, waits for them, and re-layouts  12.3 us

profile of v3, /device:TPU:0, one launch (start us, length us, event | category | flops | bytes accessed | tf_op | source)
XLA Modules:
  0.0 526.5 jit_solution(5458174079677377176)
XLA Ops:
  0.7 0.0 copy-start.8
  0.7 2.3 copy.34
  3.0 1.8 copy.33
  4.8 0.8 broadcast_in_dim_reshape.8.refs_4_
  5.5 0.8 copy.36.refs_5_
  6.3 0.7 broadcast_in_dim_reshape.6.refs_2_
  7.0 0.6 broadcast_in_dim.24.refs_6_
  7.6 0.6 broadcast_in_dim.25.refs_7_
  8.1 197.3 %forward_attention.1 = (bf16[192,2048]{1,0:T(8,128)(2,1)}, f32[1,4352]{1,0:T(1,128)}, bf16[4,192,2048]{2,1,0:T(8,128)(2,1)}, bf16[2048,1024]{1,0:T(8,128)(2,1)},...) custom-call(bf16[192,2048]{1,0:T(8,128)(2,1)} %refs_0_.1, ...), custom_call_target="tpu_custom_call" | custom-call | tf_op jit(solution)/shard_map/forward_attention/pallas_call | solution.py:725
  205.4 110.4 %feed_forward.1 = (bf16[192,2048]{1,0:T(8,128)(2,1)}, f32[192,2048]{1,0:T(8,128)}, bf16[4,192,2048]{2,1,0:T(8,128)(2,1)}, f32[1,2048]{1,0:T(1,128)}, bf16[2048,7...) custom-call(bf16[4,2,192,2048]{3,2,1,0:T(8,128)(2,1)} %get-tuple-element.52.refs_0_, ...), custom_call_target="tpu_custom_call" | custom-call | tf_op jit(solution)/shard_map/feed_forward/pallas_call | solution.py:1160
  315.8 1.9 reduce
  317.7 0.6 transpose.20.refs_16_
  318.3 196.2 %backward_attention.1 = (bf16[192,2048]{1,0:T(8,128)(2,1)}, f32[1,4352]{1,0:T(1,128)}, f32[256,1536]{1,0:T(8,128)}, f32[256,1536]{1,0:T(8,128)}, f32[256,1536]{1...) custom-call(bf16[2048,768]{1,0:T(8,128)(2,1)} %get-tuple-element.61.refs_0_, ...), custom_call_target="tpu_custom_call" | custom-call | tf_op jit(solution)/shard_map/backward_attention/pallas_call | solution.py:1470
  514.5 0.8 fusion.6
  515.3 0.6 fusion.1
  515.9 3.1 copy.39
  519.0 0.6 fusion
  519.6 0.8 fusion.4
  520.4 1.0 copy.38
  521.4 0.8 split.22
  522.3 0.9 copy.44
  523.1 0.9 copy.45
  524.0 1.1 copy.46
  525.2 1.1 copy.47
  (22 shorter events, 0.0 us)
Async XLA Ops:
  0.6 4.1 copy-start.6
  0.7 4.9 copy-start.8
  0.7 6.3 %copy-start.9 = (bf16[256]{0:T(256)(128)(2,1)S(1)}, bf16[256]{0:T(256)(128)(2,1)}, u32[]{:S(2)}) copy-start(bf16[256]{0:T(256)(128)(2,1)} %param.20) | copy-start | bytes 1540
  0.7 6.9 %copy-start.10 = (bf16[256]{0:T(256)(128)(2,1)S(1)}, bf16[256]{0:T(256)(128)(2,1)}, u32[]{:S(2)}) copy-start(bf16[256]{0:T(256)(128)(2,1)} %param.27) | copy-start | bytes 1540
  514.5 4.5 copy-start.7
  514.5 5.0 copy-start.2
  515.9 4.5 copy-start.5
  519.0 3.3 copy-start.3
  520.4 2.7 copy-start.4
  521.4 2.6 copy-start.1
  523.1 2.0 copy-start

commit v4 on v3

--- a/solution.py
+++ b/solution.py
@@ -430,11 +430,12 @@
 def forward_kernel(sizes, *refs):
     (hidden, valid_row, len_row, perm_row, len_col, perm_col, attn_gain, mlp_gain, query_gain,
      key_gain, out_grad, wq, wk, wv, wo, wg, wu, wd) = refs[:18]
-    (moved, gains, normed, full_qkv, full_wo, full_g, full_u, full_d, grad_y, lin, rot, attended,
-     log_total, resid, full_nm, cosine, sine, seg_col, pos_col, seg_row, pos_row, keep, live,
+    (moved, gains, normed_out, qkv_out, wo_out, full_g, full_u, full_d, grad_y, lin_out, rot_out,
+     attended_out, log_total, resid, full_nm, cosine, sine, seg_col, pos_col, seg_row, pos_row, keep, live,
      send_map, recv_map) = refs[18:43]
     (blocks_out, blocks_in, rows_in, gain_row, part_seg, part_pos, normed_own, bias, part_own,
-     from_c, from_x, to_c, nm_own, send_sems, recv_sems, local_sems) = refs[43:]
+     from_c, from_x, to_c, nm_own, normed, full_qkv, full_wo, lin, rot, attended, send_sems,
+     recv_sems, local_sems) = refs[43:]
     place = Place(*sizes)
     mover = Mover(send_sems, recv_sems, local_sems)
     tokens, width = hidden.shape
@@ -559,6 +560,7 @@
     row.finish()
     query.finish()
     key.finish()
+    stores = [mover.local(normed, normed_out), mover.local(full_qkv, qkv_out)]
 
     gain_query = gains[:, 2 * width : 2 * width + head]
     gain_key = gains[:, 2 * width + head : 2 * width + 2 * head]
@@ -583,6 +585,7 @@
         return carry
 
     lax.fori_loop(0, parts, project, 0)
+    stores += [mover.local(lin, lin_out), mover.local(rot, rot_out)]
     out.pass_own_l_to_y()
     gate.pass_h_to_x()
     scale = head ** (-0.5)
@@ -620,6 +623,7 @@
         if part == 2:
             out.pass_l_to_y()
     out.finish()
+    stores += [mover.local(full_wo, wo_out), mover.local(attended, attended_out)]
 
     def project_out(part, target):
         source = attended[pl.ds(pl.multiple_of(part * tokens, tokens), tokens), :]
@@ -661,6 +665,8 @@
     group.finish_ici()
     for part in (group, gate, upper, lower):
         part.finish()
+    for copy in stores:
+        copy.wait()
     mover.finish()
 
 
@@ -681,16 +687,16 @@
     outs = [
         ((tokens, width), BF16, VMEM),
         ((1, gain_width), F32, VMEM),
-        ((seq_size, tokens, width), BF16, VMEM),
-        ((width, rotated + wk.shape[1]), BF16, VMEM),
-        ((width, wo.shape[1]), BF16, VMEM),
+        ((seq_size, tokens, width), BF16, HBM),
+        ((width, rotated + wk.shape[1]), BF16, HBM),
+        ((width, wo.shape[1]), BF16, HBM),
         ((width, inner), BF16, HBM),
         ((width, inner), BF16, HBM),
         ((width, inner), BF16, HBM),
         ((tokens, width), BF16, VMEM),
-        ((row_len, rotated), BF16, VMEM),
-        ((row_len, rotated + wk.shape[1]), BF16, VMEM),
-        ((row_len, wq.shape[1]), BF16, VMEM),
+        ((row_len, rotated), BF16, HBM),
+        ((row_len, rotated + wk.shape[1]), BF16, HBM),
+        ((row_len, wq.shape[1]), BF16, HBM),
         ((wk.shape[1] // head_size, seq_size, heads * head_size // wk.shape[1] * tokens, 1), F32, VMEM),
         ((tokens, width), F32, VMEM),
         (group, BF16, HBM),
@@ -720,6 +726,14 @@
         pltpu.VMEM((2, tokens, width), BF16),
         pltpu.VMEM((tokens, width), BF16),
     ]
+    scratch += [
+        pltpu.VMEM((seq_size, tokens, width), BF16),
+        pltpu.VMEM((width, rotated + wk.shape[1]), BF16),
+        pltpu.VMEM((width, wo.shape[1]), BF16),
+        pltpu.VMEM((row_len, rotated), BF16),
+        pltpu.VMEM((row_len, rotated + wk.shape[1]), BF16),
+        pltpu.VMEM((row_len, wq.shape[1]), BF16),
+    ]
     sends = 2 * (dp_size - 1) + 4 * (high + 1) + 9 * high
     sends += 3 * (3 + 2 * high) + 2 * GatherGroup.sends + GatherSeq.sends + 3
     return pl.pallas_call(
@@ -727,7 +741,7 @@
         out_shape=[jax.ShapeDtypeStruct(shape, dtype) for shape, dtype, _ in outs],
         in_specs=[VMEM] * 11 + [HBM] * 7,
         out_specs=[spec for _, _, spec in outs],
-        scratch_shapes=scratch + sems(sends, 16),
+        scratch_shapes=scratch + sems(sends, 24),
         compiler_params=comm_params(collective_id),
         name="forward_attention",
     )(*args)
@@ -745,11 +759,10 @@
             pltpu.VMEM((GROUP - 1, rows, quarter), BF16),
         ]
 
-    def __init__(self, place, mover, parts, from_x, from_h, from_g):
-        self.place, self.mover, self.parts = place, mover, parts
+    def __init__(self, place, mover, parts, from_x, from_h, from_g, mine=None):
+        self.place, self.mover, self.parts, self.mine = place, mover, parts, mine
         self.from_x, self.from_h, self.from_g = from_x, from_h, from_g
-        self.group_rows = from_h.shape[1]
-        self.quarter = from_x.shape[1]
+        self.group_rows, self.quarter = (from_h.shape[1:] if mine is None else mine.shape)
 
     def rows_of(self, step):
         high = lax.rem(self.place.h + step, self.place.high)
@@ -806,47 +819,49 @@
                 )
             )
 
+    def send_far(self, added):
+        self.over_x, self.over_h = {}, []
+        for step in range(1, self.place.high):
+            rows = pl.ds(pl.multiple_of(self.rows_of(step), self.group_rows), self.group_rows)
+            peer = self.place.h_peer(step)
+            self.over_h.append(
+                self.mover.send(added.at[rows], self.from_h.at[step - 1], peer)
+            )
+
     def add_near(self, stage):
         self.add_x(0, stage)
 
+    def merge(self):
+        rows = pl.ds(pl.multiple_of(self.rows_of(0), self.group_rows), self.group_rows)
+        self.mine = self.from_x.at[rows]
+        for copy in self.over_h:
+            copy.wait_recv()
+        terms = [self.mine] + [self.from_h.at[step] for step in range(self.place.high - 1)]
+        add_rows(self.mine, terms, self.group_rows, 64)
+
     def block(self, index):
         rows = self.group_rows // GROUP
-        return pl.ds(
-            pl.multiple_of(self.place.h * self.group_rows + index * rows, rows), rows
-        )
-
-    def forward_high(self):
+        return self.mine.at[pl.ds(pl.multiple_of(index * rows, rows), rows)]
+
+    def send_g(self):
         place = self.place
-        own_rows = pl.ds(
-            pl.multiple_of(place.h * self.group_rows, self.group_rows), self.group_rows
-        )
-        for copy in self.over_h:
-            copy.wait_recv()
-        mine = self.from_x.at[own_rows]
-        terms = [mine] + [self.from_h.at[step] for step in range(place.high - 1)]
-        add_rows(mine, terms, self.group_rows, 64)
         self.over_g = []
         for step in (3, 1, 2):
             block = self.block(lax.rem(place.g + step, GROUP))
-            self.over_g.append(
-                (
-                    step,
-                    self.mover.send(
-                        self.from_x.at[block], self.from_g.at[step - 1], place.g_peer(step)
-                    ),
-                )
-            )
+            copy = self.mover.send(block, self.from_g.at[step - 1], place.g_peer(step))
+            self.over_g.append((step, copy))
 
     def finish(self, stage, out):
         place, quarter = self.place, self.quarter
         columns = pl.ds(pl.multiple_of(place.g * quarter, quarter), quarter)
-        stage[:, columns] = self.from_x[self.block(place.g), :].astype(F32)
+        stage[:, columns] = self.block(place.g)[...].astype(F32)
         for step, copy in self.over_g:
             copy.wait_recv()
             source = lax.rem(place.g + GROUP - step, GROUP)
             columns = pl.ds(pl.multiple_of(source * quarter, quarter), quarter)
             stage[:, columns] = self.from_g[step - 1].astype(F32)
-        self.mover.local(stage, out).wait()
+        if out is not None:
+            self.mover.local(stage, out).wait()
 
 
 class ScatterDp:
@@ -999,10 +1014,10 @@
 
 def feed_forward_kernel(sizes, *refs):
     nm_hbm, wg_hbm, wu_hbm, wd_hbm, grad_y, resid, live, gains = refs[:8]
-    mixed, grad_resid, full_proj, gain_sum, out_gd, out_gg, out_gu = refs[8:15]
+    mixed, grad_resid, full_proj, gain_sum, part_gd, out_gd, out_gg, out_gu = refs[8:16]
     (nm, gy, wg, wu, wd, hidden, gate_grad, up_grad, part_nmlp, part_down, nmlp_c, nmlp_landed,
-     down_c, down_landed, grad_proj, stage) = refs[15:31]
-    send_sems, recv_sems, local_sems = refs[31:]
+     down_c, down_landed, grad_proj, stage, column_stage, gd_from_x, gd_from_h) = refs[16:35]
+    send_sems, recv_sems, local_sems = refs[35:]
     place = Place(*sizes)
     mover = Mover(send_sems, recv_sems, local_sems)
     tokens, width = resid.shape
@@ -1013,7 +1028,10 @@
     loads = [mover.local(wg_hbm, wg), mover.local(wu_hbm, wu)]
     nm_loads = [mover.local(nm_hbm.at[index], nm.at[index]) for index in range(GROUP)]
     wd_load = mover.local(wd_hbm, wd)
-    greet([place.y_peer, place.l_peer, place.c_peer, place.x_peer])
+    greet(
+        [place.y_peer, place.l_peer, place.c_peer, place.x_peer]
+        + [place.h_peer(step) for step in range(1, place.high)]
+    )
     gather = GatherGroup(place, mover, grad_y, gy)
     gain_sum[...] = jnp.zeros_like(gain_sum)
     for copy in loads:
@@ -1055,7 +1073,6 @@
     nm_loads[2].wait()
     nm_loads[3].wait()
     lax.fori_loop(2, GROUP, gate_up, 0)
-    gather.finish_ici()
     wd_load.wait()
 
     def down_block(owner):
@@ -1070,9 +1087,12 @@
         lax.fori_loop(0, width // tile, step, 0)
 
     down = ScatterGroup(place, mover, part_down, down_c, down_landed)
-    down_block(down.owners[0])
-    down_block(down.owners[1])
+    for index in range(GROUP):
+        down_block(down.owners[index])
+        down.start(index)
+    gather.finish_ici()
     gather.finish()
+    lower = ScatterColumns(place, mover, part_gd, gd_from_x, gd_from_h, None)
 
     def back_block(owner):
         rows = pl.ds(pl.multiple_of(owner * block, block), block)
@@ -1101,15 +1121,13 @@
     back_block(nmlp.owners[2])
     nmlp.start(2)
     nmlp.forward(1)
+    nmlp.forward(2)
+    weight_grads(gy, [hidden], [part_gd])
+    lower.start_far()
+    nmlp.forward_diag()
     back_block(nmlp.owners[3])
     nmlp.start(3)
-    nmlp.forward(2)
-    down_block(down.owners[2])
     nmlp.forward(3)
-    nmlp.forward_diag()
-    down_block(down.owners[3])
-    for index in range(GROUP):
-        down.start(index)
 
     def back_mlp(rows, total):
         grad, terms = norm_back(resid[rows, :], gains[:, width : 2 * width], total)
@@ -1121,16 +1139,22 @@
     def mix(rows, total):
         mixed[rows, :] = ((resid[rows, :] + total) * live[rows, :]).astype(BF16)
 
-    weight_grads(gy, [hidden], [out_gd])
     nmlp.finish(back_mlp)
     row = GatherSeq(place, mover, grad_proj, full_proj)
     for index in range(GROUP):
         down.forward(index)
     weight_grads(nm, [gate_grad, up_grad], [out_gg, out_gu])
+    row.forward()
     down.forward_diag()
-    row.forward()
+    added = []
+    for step in range(1, place.high):
+        lower.add_x(step, column_stage)
+        rows = pl.ds(pl.multiple_of(lower.rows_of(step), lower.group_rows), lower.group_rows)
+        added.append(mover.local(gd_from_x.at[rows], out_gd.at[rows]))
     down.finish(mix)
     row.finish()
+    for copy in added:
+        copy.wait()
     mover.finish()
 
 
@@ -1139,6 +1163,8 @@
     nm, wg, resid, gains = args[0], args[1], args[5], args[7]
     tokens, width = resid.shape
     inner = wg.shape[1]
+    high = dp_size // GROUP
+    piece = min(width // high, ScatterColumns.stage_rows)
     rows = GROUP * (seq_size // 2) * tokens
     outs = [
         ((tokens, width), BF16, VMEM),
@@ -1146,6 +1172,7 @@
         ((seq_size, tokens, width), BF16, HBM),
         ((1, width), F32, VMEM),
         ((width, inner), BF16, HBM),
+        ((width, inner // 2), BF16, HBM),
         ((width, inner), BF16, HBM),
         ((width, inner), BF16, HBM),
     ]
@@ -1155,8 +1182,10 @@
     scratch += [pltpu.VMEM(nm.shape, BF16)] * 2
     scratch += ScatterGroup.scratch(tokens, width) * 2
     scratch += [pltpu.VMEM((tokens, width), BF16), pltpu.VMEM((2, 256, inner), BF16)]
-    sends = 3 * 10 + GatherSeq.sends
-    local = 9 + 3 * (width // 256)
+    scratch += [pltpu.VMEM((2, piece, inner // 2), BF16)]
+    scratch += ScatterColumns.scratch(high, width // dp_size, inner // 2)[:2]
+    sends = 3 * 10 + GatherSeq.sends + 2 * high
+    local = 10 + 3 * (width // 256) + high * (width // high // piece)
     return pl.pallas_call(
         functools.partial(feed_forward_kernel, sizes),
         out_shape=[jax.ShapeDtypeStruct(shape, dtype) for shape, dtype, _ in outs],
@@ -1169,12 +1198,12 @@
 
 
 def backward_kernel(sizes, *refs):
-    (part_gd, part_gg, part_gu, wo, grad_resid, full_proj, moved, keep, gain_mlp, gains, cosine,
-     sine, seg_col, pos_col, seg_row, pos_row, log_row, normed, full_qkv, lin, rot, attended,
-     recv_map, send_map) = refs[:24]
-    grad_hidden, gain_sums, out_gd, out_gg, out_gu, out_qkv, out_wo = refs[24:31]
+    part_gg, part_gu, part_gd, gd_far = refs[:4]
+    moved, keep, gain_mlp, gains, cosine, sine = refs[12:18]
+    seg_col, pos_col, seg_row, pos_row, log_row, recv_map, send_map = refs[18:25]
+    grad_hidden, gain_sums, out_gd, out_gg, out_gu, out_q, out_k, out_v, out_wo = refs[25:34]
     send_sems, recv_sems, local_sems = refs[-3:]
-    scratch = list(refs[31:-3])
+    scratch = list(refs[34:-3])
 
     def take(count):
         taken = scratch[:count]
@@ -1186,28 +1215,28 @@
     tokens, width = moved.shape
     parts = sizes[1]
     head = cosine.shape[1]
-    query_width = attended.shape[1]
-    key_width = (rot.shape[1] - query_width) // 2
+    query_width = refs[6].shape[1]
+    key_width = (refs[7].shape[1] - query_width) // 2
     rotated = query_width + key_width
     columns = width // GROUP
     repeat = query_width // key_width
     column_stage, out_stage = take(2)
     grad_wo, grad_key, grad_query = take(3)
-    mlp = [
-        ScatterColumns(place, mover, part, *take(3)) for part in (part_gd, part_gg, part_gu)
-    ]
-    wo_sum = ScatterDp(place, mover, grad_wo, out_wo, *take(3))
-    key_sum = ScatterDp(place, mover, grad_key, out_qkv.at[:, pl.ds(query_width, 2 * key_width)], *take(3))
-    query_sum = ScatterDp(place, mover, grad_query, out_qkv.at[:, pl.ds(0, query_width)], *take(3))
+    loaded = take(8)
+    wo, full_proj, attended, rot, lin, normed, full_qkv, grad_resid = loaded
+    lower = ScatterColumns(place, mover, part_gd, *take(3))
+    gate = ScatterColumns(place, mover, part_gg, *take(3))
+    upper = ScatterColumns(place, mover, part_gu, *take(3))
+    wo_total, key_total = take(2)
+    wo_sum = ScatterDp(place, mover, grad_wo, wo_total, *take(3))
+    key_sum = ScatterDp(place, mover, grad_key, key_total, *take(3))
+    query_sum = ScatterDp(place, mover, grad_query, out_q, *take(3))
     grad_moved, to_c, from_c, from_x = take(4)
     grad_att, grad_keys, grad_values, grad_lin, bias = take(5)
     blocks_out, blocks_in, rows_in, row_c, row_x = take(5)
 
+    loads = [mover.local(source, target) for source, target in zip(refs[4:12], loaded)]
     greet(dp_peers(place) + [place.x_peer, place.c_peer])
-    lower, gate, upper = mlp
-    gate.start_far()
-    lower.start_far()
-    upper.start_far()
     gain_sums[...] = jnp.zeros_like(gain_sums)
     gain_sums[:, width : 2 * width] = gain_mlp[...]
     grad_keys[...] = jnp.zeros_like(grad_keys)
@@ -1220,7 +1249,6 @@
             grad_att[spots, start : start + 256] = result.astype(BF16)
         return carry
 
-    lax.fori_loop(0, parts, attended_grad, 0)
 
     def out_weight_grad(index, carry):
         lanes = pl.ds(pl.multiple_of(index * 256, 256), 256)
@@ -1238,7 +1266,7 @@
         grad_lin[spots, lanes] = values.astype(BF16)
         gain_sums[:, gain_lanes] += jnp.sum(terms, axis=0, keepdims=True)
 
-    for part in range(parts):
+    def attention_part(part):
         keys = (part + 1) * tokens
         spots = pl.ds(part * tokens, tokens)
         allowed = (seg_col[:keys, :] == seg_row[:, spots]) & (pos_col[:keys, :] <= pos_row[:, spots])
@@ -1280,32 +1308,26 @@
             return carry
 
         lax.fori_loop(0, key_width // head, attend, 0)
-        if part == 0:
-            gate.forward_far(column_stage)
-        if part == parts - 2:
-            lax.fori_loop(0, width // 256, out_weight_grad, 0)
-            lower.forward_far(column_stage)
-            wo_sum.start()
-            for columns_sum in (gate, upper, lower):
-                columns_sum.start_near()
-    for pair in range(key_width // head):
-
-        def back_keys(part, carry):
-            spots = pl.ds(pl.multiple_of(part * tokens, tokens), tokens)
-            lanes = pl.ds(pair * head, head)
-            unrotate(
-                spots,
-                pl.ds(query_width + pair * head, head),
-                grad_keys[spots, lanes] * scale,
-                gain_key,
-                pl.ds(2 * width + head, head),
-            )
-            grad_lin[spots, pl.ds(rotated + pair * head, head)] = grad_values[spots, lanes].astype(
-                BF16
-            )
-            return carry
-
-        lax.fori_loop(0, parts, back_keys, 0)
+
+    def back_all_keys():
+        for pair in range(key_width // head):
+
+            def back_keys(part, carry):
+                spots = pl.ds(pl.multiple_of(part * tokens, tokens), tokens)
+                lanes = pl.ds(pair * head, head)
+                unrotate(
+                    spots,
+                    pl.ds(query_width + pair * head, head),
+                    grad_keys[spots, lanes] * scale,
+                    gain_key,
+                    pl.ds(2 * width + head, head),
+                )
+                grad_lin[spots, pl.ds(rotated + pair * head, head)] = grad_values[spots, lanes].astype(
+                    BF16
+                )
+                return carry
+
+            lax.fori_loop(0, parts, back_keys, 0)
 
     def weight_grad(target, start, size):
         def step(index, carry):
@@ -1318,14 +1340,6 @@
 
         lax.fori_loop(0, width // 256, step, 0)
 
-    wo_sum.forward_y()
-    weight_grad(grad_query, 0, query_width)
-    weight_grad(grad_key, query_width, 2 * key_width)
-    query_sum.start()
-    gate.add_near(column_stage)
-    upper.forward_far(column_stage)
-    gate.forward_high()
-
     def normed_grad(part, target):
         source = grad_lin[pl.ds(pl.multiple_of(part * tokens, tokens), tokens), :]
 
@@ -1338,28 +1352,20 @@
 
     cores = place.cores
     places = ((1 - place.x) * cores, place.x * cores)
-    normed_grad(places[0] + 1 - place.c, to_c.at[0])
-    over_c = [mover.send(to_c.at[0], from_c.at[0], place.c_peer)]
-    normed_grad(places[0] + place.c, to_c.at[1])
-    over_c[0].wait_recv()
-    add_rows(to_c.at[1], [to_c.at[1], from_c.at[0]], tokens, 32)
-    over_x = mover.send(to_c.at[1], from_x, place.x_peer)
-    query_sum.forward_y()
-    key_sum.start()
-    lower.add_near(column_stage)
-    lower.forward_high()
-    normed_grad(places[1] + 1 - place.c, to_c.at[2])
-    over_c.append(mover.send(to_c.at[2], from_c.at[1], place.c_peer))
-    normed_grad(places[1] + place.c, to_c.at[3])
-    upper.add_near(column_stage)
-    gate.finish(out_stage, out_gg)
-    query_sum.forward_l()
-    wo_sum.forward_l()
-    key_sum.forward_y()
-    key_sum.forward_l()
-    upper.forward_high()
-    over_c[1].wait_recv()
-    over_x.wait_recv()
+    over = {}
+
+    def send_other_row():
+        normed_grad(places[0] + 1 - place.c, to_c.at[0])
+        first = mover.send(to_c.at[0], from_c.at[0], place.c_peer)
+        normed_grad(places[0] + place.c, to_c.at[1])
+        first.wait_recv()
+        add_rows(to_c.at[1], [to_c.at[1], from_c.at[0]], tokens, 32)
+        over["x"] = mover.send(to_c.at[1], from_x, place.x_peer)
+
+    def send_own_row():
+        normed_grad(places[1] + 1 - place.c, to_c.at[2])
+        over["c"] = mover.send(to_c.at[2], from_c.at[1], place.c_peer)
+        normed_grad(places[1] + place.c, to_c.at[3])
 
     def back_normed(index, carry):
         rows = pl.ds(pl.multiple_of(index * 32, 32), 32)
@@ -1370,56 +1376,116 @@
         gain_sums[:, :width] += jnp.sum(terms, axis=0, keepdims=True)
         return carry
 
-    lax.fori_loop(0, tokens // 32, back_normed, 0)
     piece_row = index_of((place.dp_size * 16, 1), 0) & 3
-    for q in range(GROUP):
-        lanes = pl.ds(q * columns, columns)
-        piece = product(recv_map[...], grad_moved[:, lanes], CONTRACT_ROWS)
-        piece = jnp.where(piece_row == q, piece, 0.0)
-        total = piece if q == 0 else total + piece
-    blocks_out[...] = total.astype(BF16).reshape(blocks_out.shape)
     copies = []
-    for step in range(1, place.dp_size):
-        other = lax.rem(place.d + step, place.dp_size)
-        copies.append(mover.send(blocks_out.at[other], blocks_in.at[place.d], (other, place.s)))
-        copies.append(mover.send(gain_sums, rows_in.at[place.d], (other, place.s)))
-    blocks_in[place.d] = blocks_out[place.d]
-    rows_in[place.d] = gain_sums[...]
+
+    def finish_row():
+        over["c"].wait_recv()
+        over["x"].wait_recv()
+        lax.fori_loop(0, tokens // 32, back_normed, 0)
+        for q in range(GROUP):
+            lanes = pl.ds(q * columns, columns)
+            piece = product(recv_map[...], grad_moved[:, lanes], CONTRACT_ROWS)
+            piece = jnp.where(piece_row == q, piece, 0.0)
+            total = piece if q == 0 else total + piece
+        blocks_out[...] = total.astype(BF16).reshape(blocks_out.shape)
+        for step in range(1, place.dp_size):
+            other = lax.rem(place.d + step, place.dp_size)
+            copies.append(mover.send(blocks_out.at[other], blocks_in.at[place.d], (other, place.s)))
+            copies.append(mover.send(gain_sums, rows_in.at[place.d], (other, place.s)))
+        blocks_in[place.d] = blocks_out[place.d]
+        rows_in[place.d] = gain_sums[...]
+
+    def finish_hidden():
+        for copy in copies:
+            copy.wait_recv()
+        row_total = rows_in[0]
+        for index in range(1, place.dp_size):
+            row_total = row_total + rows_in[index]
+        row_c[0] = row_total
+        over["gc"] = mover.send(row_c.at[0], row_c.at[1], place.c_peer)
+        returned = blocks_in[...].reshape(place.dp_size * 16, columns)
+        for q in range(GROUP):
+            lanes = pl.ds(q * columns, columns)
+            chosen = jnp.where(piece_row == q, returned, jnp.zeros_like(returned))
+            here = product(send_map[...], chosen, CONTRACT_ROWS)
+            here = here + jnp.where(keep[...] > 0.0, grad_moved[:, lanes].astype(F32), 0.0)
+            grad_hidden[:, lanes] = here.astype(BF16)
+
+    def pass_gains():
+        over["gc"].wait_recv()
+        row_x[0] = row_c[0] + row_c[1]
+        over["gx"] = mover.send(row_x.at[0], row_x.at[1], place.x_peer)
+
+    lower.send_far(gd_far)
+    for copy in loads[:2]:
+        copy.wait()
+    lax.fori_loop(0, parts, attended_grad, 0)
+    for copy in loads[2:5]:
+        copy.wait()
+    gate.start_far()
+    upper.start_far()
+    lax.fori_loop(0, width // 256, out_weight_grad, 0)
+    wo_sum.start()
+    attention_part(0)
+    attention_part(1)
+    attention_part(2)
+    lower.start_near()
+    for part in range(3, parts):
+        attention_part(part)
+    gate.start_near()
+    gate.forward_far(column_stage)
+    back_all_keys()
+    wo_sum.forward_y()
+    for copy in loads[5:]:
+        copy.wait()
+    weight_grad(grad_query, 0, query_width)
+    query_sum.start()
+    query_sum.forward_y()
+    send_other_row()
+    wo_sum.forward_l()
+    lower.add_near(column_stage)
+    upper.forward_far(column_stage)
+    weight_grad(grad_key, query_width, 2 * key_width)
+    upper.start_near()
+    key_sum.start()
+    lower.merge()
+    lower.send_g()
+    key_sum.forward_y()
+    key_sum.forward_l()
+    gate.add_near(column_stage)
+    gate.merge()
+    gate.send_g()
+    lower.finish(out_stage, None)
+    out_gd[...] = out_stage[...].T
+    upper.add_near(column_stage)
+    wo_sum.finish()
+    out_wo[...] = wo_total[...].T
+    send_own_row()
+    finish_row()
+    upper.merge()
+    upper.send_g()
+    query_sum.forward_l()
+    key_sum.finish()
+    out_k[...] = key_total[:, :key_width]
+    out_v[...] = key_total[:, key_width:]
+    finish_hidden()
+    pass_gains()
+    gate.finish(out_stage, out_gg)
+    upper.finish(out_stage, out_gu)
     query_sum.finish()
-    for copy in copies:
-        copy.wait_recv()
-    row_total = rows_in[0]
-    for index in range(1, place.dp_size):
-        row_total = row_total + rows_in[index]
-    row_c[0] = row_total
-    pass_c = mover.send(row_c.at[0], row_c.at[1], place.c_peer)
-    returned = blocks_in[...].reshape(place.dp_size * 16, columns)
-    for q in range(GROUP):
-        lanes = pl.ds(q * columns, columns)
-        chosen = jnp.where(piece_row == q, returned, jnp.zeros_like(returned))
-        here = product(send_map[...], chosen, CONTRACT_ROWS)
-        here = here + jnp.where(keep[...] > 0.0, grad_moved[:, lanes].astype(F32), 0.0)
-        grad_hidden[:, lanes] = here.astype(BF16)
-    pass_c.wait_recv()
-    row_x[0] = row_c[0] + row_c[1]
-    pass_x = mover.send(row_x.at[0], row_x.at[1], place.x_peer)
-    lower.finish(out_stage, out_gd)
-    upper.finish(out_stage, out_gu)
-    wo_sum.finish()
-    key_sum.finish()
-    pass_x.wait_recv()
+    over["gx"].wait_recv()
     mover.finish()
     gain_sums[...] = row_x[0] + row_x[1]
 
 
 def backward(sizes, collective_id, args):
     dp_size, seq_size = sizes
-    part_gd, wo, moved, gains = args[0], args[3], args[6], args[9]
-    rot, attended = args[20], args[21]
+    part_gg, attended, rot, moved, gains = args[0], args[6], args[7], args[12], args[15]
     tokens, width = moved.shape
     high = dp_size // GROUP
     rows = width // dp_size
-    quarter = part_gd.shape[1] // 2
+    quarter = part_gg.shape[1] // 2
     row_len = seq_size * tokens
     query_width = attended.shape[1]
     key_width = (rot.shape[1] - query_width) // 2
@@ -1427,11 +1493,13 @@
     outs = [
         ((tokens, width), BF16, VMEM),
         (gains.shape, F32, VMEM),
+        ((GROUP * quarter, rows), F32, VMEM),
         ((rows, GROUP * quarter), F32, HBM),
         ((rows, GROUP * quarter), F32, HBM),
-        ((rows, GROUP * quarter), F32, HBM),
-        ((rows, rot.shape[1]), F32, VMEM),
         ((rows, query_width), F32, VMEM),
+        ((rows, key_width), F32, VMEM),
+        ((rows, key_width), F32, VMEM),
+        ((query_width, rows), F32, VMEM),
     ]
     piece = min(GROUP * rows, ScatterColumns.stage_rows)
     scratch = [
@@ -1439,12 +1507,17 @@
         pltpu.VMEM((rows, GROUP * quarter), F32),
     ]
     scratch += [
-        pltpu.VMEM(wo.shape, BF16),
+        pltpu.VMEM((width, query_width), BF16),
         pltpu.VMEM((width, 2 * key_width), BF16),
         pltpu.VMEM((width, query_width), BF16),
     ]
+    scratch += [pltpu.VMEM(array.shape, array.dtype) for array in args[4:12]]
     for _ in range(3):
         scratch += ScatterColumns.scratch(high, rows, quarter)
+    scratch += [
+        pltpu.VMEM((rows, query_width), F32),
+        pltpu.VMEM((rows, 2 * key_width), F32),
+    ]
     scratch += ScatterDp.scratch(high, rows, query_width)
     scratch += ScatterDp.scratch(high, rows, 2 * key_width)
     scratch += ScatterDp.scratch(high, rows, query_width)
@@ -1466,16 +1539,50 @@
     ]
     sends = 3 * (2 * high + 2) + 3 * ScatterDp.sends(high)
     sends += 3 + 2 * (dp_size - 1) + 2
-    local = 3 * (high * GROUP * rows // piece + 1)
+    local = 3 * (high * GROUP * rows // piece + 1) + 9
     return pl.pallas_call(
         functools.partial(backward_kernel, sizes),
         out_shape=[jax.ShapeDtypeStruct(shape, dtype) for shape, dtype, _ in outs],
-        in_specs=[HBM] * 3 + [VMEM] * 21,
+        in_specs=[HBM] * 12 + [VMEM] * 13,
         out_specs=[spec for _, _, spec in outs],
         scratch_shapes=scratch + sems(sends, local),
         compiler_params=comm_params(collective_id, 63 * 1024 * 1024),
         name="backward_attention",
     )(*args)
+
+
+def hand_over_kernel(count, *refs):
+    held = refs[2 * count : 3 * count]
+    sems_in, sems_out = refs[3 * count :]
+    loads = [
+        pltpu.make_async_copy(refs[index], held[index], sems_in.at[index])
+        for index in range(count)
+    ]
+    stores = [
+        pltpu.make_async_copy(held[index], refs[count + index], sems_out.at[index])
+        for index in range(count)
+    ]
+    for copy in loads:
+        copy.start()
+    for load, store in zip(loads, stores):
+        load.wait()
+        store.start()
+    for copy in stores:
+        copy.wait()
+
+
+def hand_over(arrays):
+    count = len(arrays)
+    return pl.pallas_call(
+        functools.partial(hand_over_kernel, count),
+        out_shape=[jax.ShapeDtypeStruct(array.shape, array.dtype) for array in arrays],
+        in_specs=[HBM] * count,
+        out_specs=[HBM] * count,
+        scratch_shapes=[pltpu.VMEM(array.shape, array.dtype) for array in arrays]
+        + [pltpu.SemaphoreType.DMA((count,)), pltpu.SemaphoreType.DMA((count,))],
+        compiler_params=pltpu.CompilerParams(vmem_limit_bytes=62 * 1024 * 1024),
+        name="hand_over",
+    )(*arrays)
 
 
 def per_device(
@@ -1555,24 +1662,37 @@
         ),
     )
     cuts = (model_width, 2 * model_width, 2 * model_width + head_size)
-    query_width = w_query.shape[1]
-    key_width = key_weight.shape[1]
-    qkv_cuts = (query_width, query_width + key_width)
-    mixed, grad_resid, grad_proj, gain_mlp_sum, grad_down, grad_gate, grad_up = feed_forward(
+    mixed, grad_resid, grad_proj, gain_mlp_sum, part_down, grad_down, grad_gate, grad_up = feed_forward(
         sizes,
         2,
         (normed_mlp, gate_mat, up_mat, down_mat, grad_y_own, resid_rows, live, gains),
     )
-    grad_hidden, gain_sums, out_down, out_gate, out_up, out_qkv, out_wo = backward(
+    (
+        grad_hidden,
+        gain_sums,
+        out_down,
+        out_gate,
+        out_up,
+        out_query,
+        out_key,
+        out_value,
+        out_wo,
+    ) = backward(
         sizes,
         3,
         (
-            grad_down,
             grad_gate,
             grad_up,
+            part_down,
+            grad_down,
             out_mat,
+            grad_proj,
+            attended,
+            rotated_all,
+            rotated_lin,
+            normed,
+            qkv_mat,
             grad_resid,
-            grad_proj,
             moved_low,
             keep,
             gain_mlp_sum,
@@ -1584,16 +1704,10 @@
             seg_row,
             pos_row,
             jnp.swapaxes(log_total, 2, 3),
-            normed,
-            qkv_mat,
-            rotated_lin,
-            rotated_all,
-            attended,
             recv_map,
             send_map,
         ),
     )
-    out_query, out_key, out_value = jnp.split(out_qkv, qkv_cuts, axis=1)
     device = my_row * seq_count + my_part
 
     def own_piece(vector):
@@ -1601,6 +1715,29 @@
         return lax.dynamic_slice_in_dim(vector, device * size, size)
 
     sum_attn, sum_mlp, sum_query, sum_key = [own_piece(v) for v in jnp.split(gain_sums[0], cuts)]
+    (
+        mixed,
+        grad_hidden,
+        out_query,
+        out_key,
+        out_value,
+        out_wo,
+        out_gate,
+        out_up,
+        out_down,
+    ) = hand_over(
+        (
+            mixed,
+            grad_hidden,
+            out_query,
+            out_key,
+            out_value,
+            out_wo,
+            out_gate,
+            out_up,
+            out_down,
+        )
+    )
     return (
         mixed,
         grad_hidden,
@@ -1608,13 +1745,13 @@
         out_query,
         out_key,
         out_value,
-        out_wo.T,
+        out_wo,
         sum_query,
         sum_key,
         sum_mlp,
         out_gate,
         out_up,
-        out_down.T,
+        out_down,
     )
 
 

time: 536 us -> 516 us (0.963)
  Pallas kernels: 504 us -> 493 us
  local copies, waits for them, and re-layouts: 19.8 us -> 9.63 us
    pallas_call x1, Pallas kernels: 196 us -> 171 us  [backward(): pl.pallas_call(functools.partial(backward_kernel, sizes), out_shape=[jax....]
    pallas_call x1, Pallas kernels: 110 us -> 122 us  [feed_forward(): pl.pallas_call(functools.partial(feed_forward_kernel, sizes), out_shape=[...]
    unnamed x30 -> x12, local copies, waits for them, and re-layouts: 12.3 us -> 3.19 us
    pallas_call x0 -> x1, Pallas kernels: none -> 6.37 us  [hand_over(): pl.pallas_call(functools.partial(hand_over_kernel, count), out_shape=[jax...]
where the time goes in v4:
time: 516 us; the launch traced here: 505 us
  Pallas kernels  493 us (96%)
  local copies, waits for them, and re-layouts  9.63 us (2%)
    pallas_call x1, Pallas kernels, forward(): pl.pallas_call(functools.partial(forward_kernel, sizes), out_shape=[jax.S...  193 us
    pallas_call x1, Pallas kernels, backward(): pl.pallas_call(functools.partial(backward_kernel, sizes), out_shape=[jax....  171 us
    pallas_call x1, Pallas kernels, feed_forward(): pl.pallas_call(functools.partial(feed_forward_kernel, sizes), out_shape=[...  122 us

profile of v4, /device:TPU:0, one launch (start us, length us, event | category | flops | bytes accessed | tf_op | source)
XLA Modules:
  0.0 505.4 jit_solution(8546424421158879804)
XLA Ops:
  0.6 0.0 copy-start
  0.7 0.0 copy-start.1
  0.7 0.0 copy-start.2
  0.7 0.0 copy-start.3
  0.7 0.0 copy-start.4
  0.7 2.3 copy.32
  3.0 0.0 copy-done
  3.0 0.8 copy.31
  3.9 0.0 copy-done.1
  3.9 0.8 broadcast_in_dim_reshape.8.refs_4_
  4.6 0.8 copy.34.refs_5_
  5.4 0.7 broadcast_in_dim_reshape.6.refs_2_
  6.1 0.6 broadcast_in_dim.24.refs_6_
  6.6 0.6 broadcast_in_dim.25.refs_7_
  7.2 193.5 %forward_attention.1 = (bf16[192,2048]{1,0:T(8,128)(2,1)}, f32[1,4352]{1,0:T(1,128)}, bf16[4,192,2048]{2,1,0:T(8,128)(2,1)}, bf16[2048,1024]{1,0:T(8,128)(2,1)},...) custom-call(bf16[192,2048]{1,0:T(8,128)(2,1)} %refs_0_.1, ...), custom_call_target="tpu_custom_call" | custom-call | tf_op jit(solution)/shard_map/forward_attention/pallas_call | solution.py:739
  200.7 122.3 %feed_forward.1 = (bf16[192,2048]{1,0:T(8,128)(2,1)}, f32[192,2048]{1,0:T(8,128)}, bf16[4,192,2048]{2,1,0:T(8,128)(2,1)}, f32[1,2048]{1,0:T(1,128)}, bf16[2048,7...) custom-call(bf16[4,2,192,2048]{3,2,1,0:T(8,128)(2,1)} %get-tuple-element.64.r, ...), custom_call_target="tpu_custom_call" | custom-call | tf_op jit(solution)/shard_map/feed_forward/pallas_call | solution.py:1189
  323.0 1.9 reduce
  324.9 0.6 transpose.12.refs_22_
  325.5 170.7 %backward_attention.1 = (bf16[192,2048]{1,0:T(8,128)(2,1)}, f32[1,4352]{1,0:T(1,128)}, f32[1536,256]{1,0:T(8,128)}, f32[256,1536]{1,0:T(8,128)}, f32[256,1536]{1...) custom-call(bf16[2048,768]{1,0:T(8,128)(2,1)} %get-tuple-element.73.refs_0_, ...), custom_call_target="tpu_custom_call" | custom-call | tf_op jit(solution)/shard_map/backward_attention/pallas_call | solution.py:1543
  496.2 0.6 fusion.5
  496.8 0.6 fusion.1
  497.4 0.7 fusion.4
  498.1 0.6 fusion
  498.7 6.4 %hand_over.1 = (bf16[192,2048]{1,0:T(8,128)(2,1)}, bf16[192,2048]{1,0:T(8,128)(2,1)}, f32[256,512]{1,0:T(8,128)}, f32[256,256]{1,0:T(8,128)}, f32[256,256]{1,0:T...) custom-call(bf16[192,2048]{1,0:T(8,128)(2,1)} %get-tuple-element.72.refs_0_, ...), custom_call_target="tpu_custom_call" | custom-call | tf_op jit(solution)/shard_map/hand_over/pallas_call | solution.py:1576
  (3 shorter events, 0.0 us)
Async XLA Ops:
  0.6 2.4 copy-start
  0.7 3.2 copy-start.1
  0.7 4.0 copy-start.2
  0.7 5.4 %copy-start.3 = (bf16[256]{0:T(256)(128)(2,1)S(1)}, bf16[256]{0:T(256)(128)(2,1)}, u32[]{:S(2)}) copy-start(bf16[256]{0:T(256)(128)(2,1)} %param.20) | copy-start | bytes 1540
  0.7 5.9 %copy-start.4 = (bf16[256]{0:T(256)(128)(2,1)S(1)}, bf16[256]{0:T(256)(128)(2,1)}, u32[]{:S(2)}) copy-start(bf16[256]{0:T(256)(128)(2,1)} %param.27) | copy-start | bytes 1540
